TPU v7x, 32 devices: a whole 2x2x4 slice. The times are simulated.
32 devices in a mesh: vert: 16 (over z, x, core), row: 2 (over y).
Axes of the slice: x: 2, y: 2, z: 4, core: 2. Of those that a mesh axis runs over, the one named last changes fastest.
Arguments:
- features: float32 [131072, 256], P(('vert', 'row')), may hold values from -6 to 6
- w_self: float32 [256, 256], replicated, may hold values from -0.375 to 0.375
- w_neigh: float32 [256, 256], replicated, may hold values from -0.75 to 0.75
- bias: float32 [256], replicated, may hold values from -3 to 3
- w_head: float32 [256], replicated, may hold values from -0.75 to 0.75
- tile_weights: float32 [4096, 128, 128], P(('vert', 'row')), may hold values from 0.01 to 1
- tile_dst: int32 [4096], P(('vert', 'row')), may hold values from 0 to 31
- tile_src: int32 [4096], P(('vert', 'row')), may hold values from 0 to 65
- tile_count: int32 [32], P(('vert', 'row')), may hold values from 16 to 128, as said below
- hub_block: int32 [32], P(('vert', 'row')), may hold values from 0 to 31
- send_rows: int32 [32, 32, 8], P(('vert', 'row')), may hold values from 0 to 4095
- send_count: int32 [32, 32], P(('vert', 'row')), may hold values from 1 to 8, as said below
- labels: int32 [131072], P(('vert', 'row')), may hold values from 0 to 1
Outputs:
- grad_self: float32 [256, 256], replicated
- grad_neigh: float32 [256, 256], replicated
- grad_bias: float32 [256], replicated
- grad_head: float32 [256], replicated
Inputs may be any that keep to these rules, and one draw needn't show every extreme that they name: Tile t of a device is used when t < its tile_count; some device uses all 128 tiles and some 128 // 8. `send_count`: each sending device fills all 8 slots for at least one receiving device.
All inputs are finite; a program needn't handle non-finite values.
Results may differ from a plain program's by a relative error of at most 0.0003.
Values sent between devices are 32-bit elements; how exact they have to be, the bound alone decides.
No kernel may reach another device: no remote copies, remote signals or barrier semaphores. Data moves between devices by JAX's collectives and lax.ppermute only.
A program may use at most 128 MiB of HBM per device.

v0:
```python
import math

import jax
import jax.numpy as jnp
from jax import lax
from jax.sharding import PartitionSpec as P

FULL_PRECISION = lax.Precision.HIGHEST


def on_device(
    features,
    w_self,
    w_neigh,
    bias,
    w_head,
    tile_weights,
    tile_dst,
    tile_src,
    tile_count,
    hub_block,
    send_rows,
    send_count,
    labels,
):
    tile_size = tile_weights.shape[1]
    tile_total = tile_weights.shape[0]
    feature_width = features.shape[1]
    block_count = features.shape[0] // tile_size
    slot_count = send_rows.shape[2]
    own_blocks = features.reshape(block_count, tile_size, feature_width)
    hub_local = lax.dynamic_slice_in_dim(own_blocks, hub_block[0], 1, 0)
    hub_blocks = lax.all_gather(hub_local, ("vert", "row"), axis=0, tiled=True)
    outgoing = features[send_rows[0]]
    slot_index = jnp.arange(slot_count, dtype=jnp.int32)
    alive = slot_index[None, :] < send_count[0][:, None]
    outgoing = jnp.where(alive[:, :, None], outgoing, jnp.zeros_like(outgoing))
    incoming = lax.all_to_all(outgoing, ("vert", "row"), split_axis=0, concat_axis=0, tiled=True)
    source_table = jnp.concatenate(
        [own_blocks, incoming.reshape(-1, tile_size, feature_width), hub_blocks], 0
    )
    active = jnp.arange(tile_total, dtype=jnp.int32) < tile_count[0]
    picked = source_table[tile_src]
    contrib = jnp.einsum("tij,tjf->tif", tile_weights, picked, precision=FULL_PRECISION)
    block_ids = jnp.arange(block_count, dtype=jnp.int32)
    selector = ((tile_dst[None, :] == block_ids[:, None]) & active[None, :]).astype(features.dtype)
    summed = jnp.einsum("bt,tif->bif", selector, contrib, precision=FULL_PRECISION)
    weight_sum = jnp.einsum(
        "bt,ti->bi", selector, jnp.sum(tile_weights, axis=2), precision=FULL_PRECISION
    )
    neigh_mean = ((own_blocks + summed) / (1.0 + weight_sum)[:, :, None]).reshape(-1, feature_width)
    pre_act = (
        jnp.dot(features, w_self, precision=FULL_PRECISION)
        + jnp.dot(neigh_mean, w_neigh, precision=FULL_PRECISION)
        + bias[None, :]
    )
    sigmoid_pre = jax.nn.sigmoid(pre_act)
    hidden = pre_act * sigmoid_pre
    head_score = jnp.dot(hidden, w_head, precision=FULL_PRECISION)
    target = 2.0 * labels.astype(features.dtype) - 1.0
    vertex_total = features.shape[0] * lax.axis_size(("vert", "row"))
    loss_scale = 1.0 / math.sqrt(vertex_total)
    dscore = (head_score - target) * loss_scale
    dpre = dscore[:, None] * w_head[None, :] * (sigmoid_pre * (1.0 + pre_act * (1.0 - sigmoid_pre)))
    local_self = jnp.dot(features.T, dpre, precision=FULL_PRECISION)
    local_neigh = jnp.dot(neigh_mean.T, dpre, precision=FULL_PRECISION)
    local_bias = jnp.sum(dpre, axis=0)
    local_head = jnp.dot(hidden.T, dscore, precision=FULL_PRECISION)
    grad_self, grad_neigh, grad_bias, grad_head = lax.psum(
        (local_self, local_neigh, local_bias, local_head), ("vert", "row")
    )
    return (grad_self, grad_neigh, grad_bias, grad_head)


def solution(mesh):
    in_specs = (
        P(("vert", "row"), None),
        P(),
        P(),
        P(),
        P(),
        P(("vert", "row"), None, None),
        P(("vert", "row")),
        P(("vert", "row")),
        P(("vert", "row")),
        P(("vert", "row")),
        P(("vert", "row"), None, None),
        P(("vert", "row"), None),
        P(("vert", "row")),
    )
    out_specs = (P(), P(), P(), P())
    return jax.shard_map(
        on_device, mesh=mesh, in_specs=in_specs, out_specs=out_specs, check_vma=False
    )
```

profile of v0, /device:TPU:0, one launch (start us, length us, event | category | flops | bytes accessed | tf_op | source)
XLA Modules:
  0.0 328.3 jit_solution(9357706984771237963)
XLA Ops:
  7.2 0.0 all-gather.2.cloned.1.call-start
  7.9 1.6 constant_dynamic-slice_fusion
  9.5 0.0 all-gather.2.cloned.1.call-update
  9.5 0.7 compare_select_fusion
  10.2 0.1 copy.24
  10.3 0.1 reshape.83
  10.4 3.2 gather_fusion
  13.5 0.7 iota_compare_fusion
  14.3 0.8 bitcast_select_fusion
  15.1 7.3 %all-to-all-start = ((f32[32,8,256]{2,1,0:T(8,128)}), f32[32,8,256]{2,1,0:T(8,128)S(1)}, u32[]{:S(2)}, u32[]{:S(2)}) async-start(f32[32,8,256]{2,1,0:T(8,128)} %bitcast_select_fusion), calls=%async_computation | async-start | bytes 524288 | tf_op jit(solution)/shard_map/all_to_all | solution.py:38
  22.4 0.0 all-reduce.4.cloned.1.call-start
  23.1 5.6 %reduce_sum.18 = f32[128,128]{1,0:T(8,128)S(1)} reduce(f32[128,128,128]{2,1,0:T(8,128)} %param.18, f32[]{:T(128)} %constant.11.clone.1), dimensions={2}, to_apply=%region_0.1 | reduce | flops 2080768 | bytes 8454148 | tf_op jit(solution)/shard_map/reduce_sum | solution.py:49
  28.8 0.1 convolution_add_fusion.1
  28.9 0.1 copy.28
  29.1 7.7 %fusion.21 = f32[4096,256]{1,0:T(8,128)} fusion(f32[4096,256]{1,0:T(8,128)} %param.13, f32[256,256]{1,0:T(8,128)S(1)} %copy-done), kind=kOutput, calls=%fused_computation.41 | convolution fusion | flops 3221225472 | bytes 8650752 | tf_op jit(solution)/shard_map/dot_general | solution.py:53
  36.8 40.7 %all-gather.2.cloned.1.call-done = f32[32,128,256]{2,1,0:T(8,128)} async-done(((f32[1,128,256]{2,1,0:T(8,128)}), f32[32,128,256]{2,1,0:T(8,128)}) %all-gather.2.cloned.1.call-update) | async-done | bytes 4194320 | tf_op jit(solution)/shard_map/all_gather | solution.py:33
  77.5 6.2 %pad_maximum_fusion = f32[66,128,256]{2,1,0:T(8,128)} fusion(f32[32,128,256]{2,1,0:T(8,128)} %all-gather.2.cloned.1.call-done, f32[2,128,256]{2,1,0:T(8,128)S(1)} %bitcast.58, f32[32,128,256]{2,1,0:T(8,128)} %bitcast.54), kind=kLoop, calls=%fused_computation.2 | loop fusion | flops 4325376 | bytes 17301504 | tf_op jit(solution)/shard_map/concatenate | solution.py:39
  83.7 13.3 %gather_fusion.1 = f32[128,128,256]{2,1,0:T(8,128)} fusion(f32[66,128,256]{2,1,0:T(8,128)} %pad_maximum_fusion, s32[1024]{0:T(1024)S(1)} %pad_clamp_fusion), kind=kCustom, calls=%fused_computation.1 | custom fusion | bytes 33554944 | tf_op jit(solution)/shard_map/gather | solution.py:43
  97.0 34.3 %convolution_bitcast_fusion = f32[128,128,256]{1,2,0:T(8,128)} fusion(f32[128,128,256]{2,1,0:T(8,128)} %gather_fusion.1, f32[128,128,128]{2,1,0:T(8,128)} %param.18), kind=kOutput, calls=%fused_computation.3 | convolution fusion | flops 6442450944 | bytes 41943040 | tf_op jit(solution)/shard_map/tij,tjf->tif/dot_general | solution.py:44
  131.4 17.7 %copy.26 = f32[128,128,256]{2,0,1:T(8,128)} copy(f32[128,128,256]{1,2,0:T(8,128)} %convolution_bitcast_fusion) | data formatting | bytes 33554432 | tf_op jit(solution)/shard_map/tij,tjf->tif/dot_general | solution.py:44
  149.0 13.7 %fusion.4 = f32[32,128,256]{2,0,1:T(8,128)S(1)} fusion(f32[32,128,256]{2,1,0:T(8,128)} %bitcast.55, f32[128,128,256]{2,0,1:T(8,128)} %copy.26, f32[32,128]{0,1:T(8,128)S(1)} %copy.28, s32[128]{0:T(128)S(1)} %copy-done.7, pred[128]{0:T(512)(128)(4,1)S(1)} %iota_compare_fusion.2), kind=kOutput, calls=%fused_computation.12 | convolution fusion | flops 1612718080 | bytes 25182848 | tf_op jit(solution)/shard_map/bt,tif->bif/dot_general | solution.py:47
  162.8 2.4 copy.29
  165.2 3.4 %fusion = f32[4096,256]{1,0:T(8,128)S(1)} fusion(f32[4096,256]{1,0:T(8,128)S(1)} %copy-done.4, f32[4096,256]{1,0:T(8,128)S(1)} %bitcast.56, f32[256,256]{1,0:T(8,128)S(1)} %copy-done.5, f32[256]{0:T(256)S(1)} %copy-done.8), kind=kOutput, calls=%fused_computation.5 | convolution fusion | flops 3223322624 | bytes 12846080 | tf_op jit(solution)/shard_map/dot_general | solution.py:54
  168.7 4.4 %fusion.5 = f32[1,4096]{1,0:T(1,128)S(1)} fusion(f32[256,1]{0,1:T(1,128)S(1)} %bitcast.61, f32[4096,256]{1,0:T(8,128)S(1)} %fusion), kind=kOutput, calls=%fused_computation.14 | convolution fusion | flops 16777216 | bytes 4211712 | tf_op jit(solution)/shard_map/dot_general | solution.py:59
  173.2 2.4 fusion.20
  175.7 7.5 %fusion.22 = f32[256,256]{1,0:T(8,128)} fusion(f32[4096,256]{1,0:T(8,128)S(1)} %bitcast.57, f32[4096,256]{1,0:T(8,128)S(1)} %get-tuple-element.21), kind=kOutput, calls=%fused_computation.42 | convolution fusion | flops 3221225472 | bytes 8650752 | tf_op jit(solution)/shard_map/dot_general | solution.py:66
  183.1 7.7 %convolution_bitcast_fusion.1 = f32[256,256]{0,1:T(8,128)} fusion(f32[4096,256]{1,0:T(8,128)S(1)} %get-tuple-element.21, f32[4096,256]{1,0:T(8,128)S(1)} %copy-done.2), kind=kOutput, calls=%fused_computation.20 | convolution fusion | flops 3221225472 | bytes 8650752 | tf_op jit(solution)/shard_map/dot_general | solution.py:65
  190.8 5.2 %fusion.7 = f32[1,256]{1,0:T(1,128)S(1)} fusion(f32[4096,1]{0,1:T(1,128)S(1)} %bitcast.59, f32[4096,256]{1,0:T(8,128)} %copy-done.3), kind=kOutput, calls=%fused_computation.17 | convolution fusion | flops 16777216 | bytes 4211712 | tf_op jit(solution)/shard_map/dot_general | solution.py:68
  196.0 39.2 %all-reduce = (f32[256]{0:T(256)}, f32[256]{0:T(256)}) all-reduce(f32[256]{0:T(256)S(1)} %get-tuple-element.20, f32[256]{0:T(256)S(1)} %bitcast.62), channel_id=1, replica_groups=mesh['vert'=16,'row'=2] {'vert','row'}, use_global_device_ids=true, to_apply=%region_4.5 | all-reduce | flops 512 | bytes 4096 | tf_op jit(solution)/shard_map/psum | solution.py:69
  235.1 82.6 %all-reduce.4.cloned.1.call-done = (f32[256,256]{0,1:T(8,128)}, f32[256,256]{1,0:T(8,128)}) async-done(((f32[256,256]{0,1:T(8,128)}, f32[256,256]{1,0:T(8,128)}), (f32[256,256]{0,1:T(8,128)}, f32[256,256]{1,0:T(8,128)})) %all-reduce.4.cloned.1.call-update) | async-done | bytes 524304 | tf_op jit(solution)/shard_map/psum | solution.py:69
  317.8 1.8 copy.30
  319.6 1.7 copy.39
  (29 shorter events, 0.1 us)
Async XLA Ops:
  7.2 21.9 %copy-start = (f32[256,256]{1,0:T(8,128)S(1)}, f32[256,256]{1,0:T(8,128)}, u32[]{:S(2)}) copy-start(f32[256,256]{1,0:T(8,128)} %param.14) | copy-start | bytes 786436
  7.2 70.3 %all-gather.2.cloned.1.call-start = ((), (), s32[]{:S(2)}) async-start(), calls=%async_computation.1 | async-start | bytes 4325376 | tf_op jit(solution)/shard_map/all_gather | solution.py:33
  15.1 21.7 %all-to-all-start = ((f32[32,8,256]{2,1,0:T(8,128)}), f32[32,8,256]{2,1,0:T(8,128)S(1)}, u32[]{:S(2)}, u32[]{:S(2)}) async-start(f32[32,8,256]{2,1,0:T(8,128)} %bitcast_select_fusion), calls=%async_computation | async-start | bytes 524288 | tf_op jit(solution)/shard_map/all_to_all | solution.py:38
  22.4 295.4 %all-reduce.4.cloned.1.call-start = ((), (), s32[]{:S(2)}) async-start(), calls=%async_computation.2 | async-start | bytes 1048576 | tf_op jit(solution)/shard_map/psum | solution.py:69
  23.1 5.7 %copy-start.7 = (s32[128]{0:T(128)S(1)}, s32[128]{0:T(128)}, u32[]{:S(2)}) copy-start(s32[128]{0:T(128)} %param.19) | copy-start | bytes 1540
  23.1 5.9 %copy-start.10 = (s32[128]{0:T(128)S(1)}, s32[128]{0:T(128)}, u32[]{:S(2)}) copy-start(s32[128]{0:T(128)} %param.20) | copy-start | bytes 1540
  162.7 2.5 copy-start.4
  162.7 2.5 copy-start.5
  162.7 2.5 copy-start.8
  165.2 3.5 %copy-start.9 = (f32[256]{0:T(256)S(1)}, f32[256]{0:T(256)}, u32[]{:S(2)}) copy-start(f32[256]{0:T(256)} %param.17) | copy-start | bytes 3076
  168.7 4.5 %copy-start.3 = (f32[4096,256]{1,0:T(8,128)}, f32[4096,256]{1,0:T(8,128)S(1)}, u32[]{:S(2)}) copy-start(f32[4096,256]{1,0:T(8,128)S(1)} %fusion) | copy-start | bytes 12582916
  168.7 4.5 %copy-start.6 = (s32[4096]{0:T(1024)S(1)}, s32[4096]{0:T(1024)}, u32[]{:S(2)}) copy-start(s32[4096]{0:T(1024)} %param.25) | copy-start | bytes 49156
  175.6 7.5 %copy-start.2 = (f32[4096,256]{1,0:T(8,128)S(1)}, f32[4096,256]{1,0:T(8,128)}, u32[]{:S(2)}) copy-start(f32[4096,256]{1,0:T(8,128)} %param.13) | copy-start | bytes 12582916
  190.8 130.4 %copy-start.1 = (f32[256,256]{1,0:T(8,128)S(1)}, f32[256,256]{1,0:T(8,128)}, u32[]{:S(2)}) copy-start(f32[256,256]{1,0:T(8,128)} %param.14) | copy-start | bytes 786436
Sparse Core Ops, SparseCore 0:
  11.5 65.9 all-gather.1
  190.9 126.7 all-reduce.3
where the time goes:
time: 334 us; the launch traced here: 328 us
  waiting for transfers between devices  123 us (37%)
  matrix products  84 us (25%)
  local copies, waits for them, and re-layouts  42 us (13%)
  blocking collectives  39.2 us (12%)
  other arithmetic  16.6 us (5%)
  between operations  15.8 us (5%)
  starting transfers between devices  7.38 us (2%)
    psum x1, waiting for transfers between devices, on_device(): lax.psum((local_self, local_neigh, local_bias, local_head), ('vert', 'row'))  82.6 us
    all_gather x1, waiting for transfers between devices, on_device(): hub_blocks = lax.all_gather(hub_local, ('vert', 'row'), axis=0, tiled=True)  40.7 us
    psum x1, blocking collectives, on_device(): lax.psum((local_self, local_neigh, local_bias, local_head), ('vert', 'row'))  39.2 us
    dot_general x1, matrix products, on_device(): jnp.einsum('tij,tjf->tif', tile_weights, picked, precision=FULL_PRECISION)  34.3 us
    dot_general x1, local copies, waits for them, and re-layouts, on_device(): jnp.einsum('tij,tjf->tif', tile_weights, picked, precision=FULL_PRECISION)  17.7 us
    dot_general x1, matrix products, on_device(): jnp.einsum('bt,tif->bif', selector, contrib, precision=FULL_PRECISION)  13.7 us
    gather x1, local copies, waits for them, and re-layouts, on_device(): picked = source_table[tile_src]  13.3 us
    dot_general x1, matrix products, on_device(): jnp.dot(features, w_self, precision=FULL_PRECISION)  7.68 us
  transfers between devices with their start and end apart: 3, of which 2 were waited for; matrix products, arithmetic and copies ran while one was open for 7% of the time, Pallas kernels for 0%

commit v1 on v0

v1 whole, which is shorter than its diff:
```python
import functools
import math

import jax
import jax.numpy as jnp
from jax import lax
from jax.experimental import pallas as pl
from jax.experimental.pallas import tpu as pltpu
from jax.sharding import PartitionSpec as P

AXES = ("vert", "row")
F32 = jnp.float32
BF16 = jnp.bfloat16
BUFFERS = 16
GROUP = 4
CHUNK = 512
VMEM_BYTES = 40 * 1024 * 1024


def split(x):
    hi = x.astype(BF16)
    return hi, (x - hi.astype(F32)).astype(BF16)


def dot(a, b, contract=((1,), (0,))):
    return lax.dot_general(a, b, (contract, ((), ())), preferred_element_type=F32)


def dot3(a, b, contract=((1,), (0,))):
    (a_hi, a_lo), (b_hi, b_lo) = a, b
    return dot(a_hi, b_hi, contract) + dot(a_hi, b_lo, contract) + dot(a_lo, b_hi, contract)


def tile_product(weights, source):
    w_hi, w_lo = split(weights)
    s_hi, s_lo = split(source)
    wide = jnp.concatenate([w_hi, w_hi], 1)
    tall = jnp.concatenate([s_hi, s_lo], 0)
    return dot(wide, tall) + dot(w_lo, s_hi)


def stream_tiles(total, tile_of, weights_ref, buffer_ref, sems, use):
    depth = buffer_ref.shape[0] // GROUP

    def copies(group):
        base = lax.rem(group, depth) * GROUP
        for k in range(GROUP):
            i = jnp.minimum(group * GROUP + k, total - 1)
            yield pltpu.make_async_copy(weights_ref.at[tile_of(i)], buffer_ref.at[base + k], sems.at[base + k])

    groups = (total + GROUP - 1) // GROUP

    for ahead in range(depth):
        @pl.when(ahead < groups)
        def _():
            for copy in copies(jnp.int32(ahead)):
                copy.start()

    def step(group, carry):
        for copy in copies(group):
            copy.wait()
        base = lax.rem(group, depth) * GROUP
        at = [jnp.minimum(group * GROUP + k, total - 1) for k in range(GROUP)]
        use(at, [buffer_ref[base + k] for k in range(GROUP)], [group * GROUP + k < total for k in range(GROUP)])

        @pl.when(group + depth < groups)
        def _():
            for copy in copies(group + depth):
                copy.start()

        return carry

    lax.fori_loop(0, groups, step, 0)


def add_tiles(list_ref, weights_ref, buffer_ref, sems, source_of, acc_ref):
    size = buffer_ref.shape[1]
    total = list_ref[list_ref.shape[0] - 7]

    def use(at, weights, live):
        entries = [list_ref[i] for i in at]
        products = [tile_product(w, source_of(entry // 16384)) for w, entry in zip(weights, entries)]
        for entry, product, alive in zip(entries, products, live):
            block = lax.rem(entry // 256, 64)
            where = pl.ds(pl.multiple_of(block * size, size), size)

            @pl.when(alive)
            def _():
                acc_ref[where, :] += product

    stream_tiles(total, lambda i: lax.rem(list_ref[i], 256), weights_ref, buffer_ref, sems, use)


def own_kernel(
    dst_ref, code_ref, count_ref, rows_ref, used_ref, features_ref, weights_ref,
    acc_ref, outgoing_ref, early_ref, late_ref,
    own_ref, buffer_ref, sems,
):
    tiles = dst_ref.shape[0]
    size = buffer_ref.shape[1]
    peers = used_ref.shape[0]
    slots = rows_ref.shape[0] // peers
    lists = (own_ref, early_ref, late_ref)

    def sort(t, counts):
        code = code_ref[t]
        stage = code // 65536
        entry = (lax.rem(code, 65536) * 64 + dst_ref[t]) * 256 + t
        for ref, count in zip(lists, counts):
            ref[count] = entry
        return tuple(count + jnp.where(stage == i, 1, 0) for i, count in enumerate(counts))

    counts = lax.fori_loop(0, count_ref[0], sort, (jnp.int32(0),) * 3)
    for ref, count in zip(lists, counts):
        ref[tiles + 1] = count

    acc_ref[...] = features_ref[...]

    def gather(peer, carry):
        for k in range(slots):
            row = features_ref[pl.ds(rows_ref[peer * slots + k], 1), :]
            outgoing_ref[peer, k : k + 1, :] = jnp.where(k < used_ref[peer], row, 0.0)
        return carry

    lax.fori_loop(0, peers, gather, 0)

    def source_of(block):
        return features_ref[pl.ds(pl.multiple_of(block * size, size), size), :]

    add_tiles(own_ref, weights_ref, buffer_ref, sems, source_of, acc_ref)


def own_dense_kernel(
    dst_ref, count_ref, features_ref, weights_ref, w_self_ref, bias_ref, labels_ref,
    pre_ref, aux_ref,
    buffer_ref, weight_acc_ref, sems,
):
    blocks, size, _ = weight_acc_ref.shape
    weight_acc_ref[...] = jnp.zeros_like(weight_acc_ref)

    def use(at, weights, live):
        for i, w, alive in zip(at, weights, live):
            @pl.when(alive)
            def _():
                weight_acc_ref[dst_ref[i]] += w

    stream_tiles(count_ref[0], lambda i: i, weights_ref, buffer_ref, sems, use)

    eye = lax.broadcasted_iota(jnp.int32, (size, size), 0) == lax.broadcasted_iota(jnp.int32, (size, size), 1)
    left = lax.broadcasted_iota(jnp.int32, (size, size), 1) < size // 2

    def columns(block, carry):
        inverse = 1.0 / (1.0 + jnp.sum(weight_acc_ref[block], axis=1, keepdims=True))
        target = 2.0 * labels_ref[pl.ds(block, 1), :].astype(F32) - 1.0
        target = jnp.sum(jnp.where(eye, jnp.broadcast_to(target, eye.shape), 0.0), axis=1, keepdims=True)
        aux_ref[pl.ds(pl.multiple_of(block * size, size), size), :] = jnp.where(left, inverse, target)
        return carry

    lax.fori_loop(0, blocks, columns, 0)

    w_self = split(w_self_ref[...])

    def dense(i, carry):
        where = pl.ds(pl.multiple_of(i * CHUNK, CHUNK), CHUNK)
        pre_ref[where, :] = dot3(split(features_ref[where, :]), w_self) + bias_ref[...]
        return carry

    lax.fori_loop(0, features_ref.shape[0] // CHUNK, dense, 0)


def early_kernel(
    list_ref, border_ref, mine_ref, far_ref, other_ref, far_other_ref, acc_in_ref, weights_ref, acc_ref,
    buffer_ref, sources_ref, sems, load_sems,
):
    del acc_in_ref
    at, copies = 0, []
    for i, part in enumerate((border_ref, mine_ref, far_ref, other_ref, far_other_ref)):
        blocks = part.shape[0]
        copies.append(pltpu.make_async_copy(part, sources_ref.at[pl.ds(at, blocks)], load_sems.at[i]))
        at += blocks
    for copy in copies:
        copy.start()
    for copy in copies:
        copy.wait()
    add_tiles(list_ref, weights_ref, buffer_ref, sems, lambda i: sources_ref[i], acc_ref)


def late_kernel(
    list_ref, place_ref, mine_ref, other_ref, acc_in_ref, weights_ref,
    features_ref, pre_ref, aux_ref, w_neigh_ref, w_head_ref,
    keep_ref, send_ref,
    buffer_ref, sources_ref, acc_ref, feat_ref, base_ref, col_ref, total_ref, bias_ref, head_ref,
    sems, load_sems, *, scale,
):
    blocks = mine_ref.shape[0]
    loads = [
        (mine_ref, sources_ref.at[pl.ds(0, blocks)]),
        (other_ref, sources_ref.at[pl.ds(blocks, blocks)]),
        (acc_in_ref, acc_ref),
        (features_ref, feat_ref),
        (pre_ref, base_ref),
        (aux_ref, col_ref),
    ]
    copies = [pltpu.make_async_copy(a, b, load_sems.at[i]) for i, (a, b) in enumerate(loads)]
    for copy in copies:
        copy.start()
    total_ref[...] = jnp.zeros_like(total_ref)
    bias_ref[...] = jnp.zeros_like(bias_ref)
    head_ref[...] = jnp.zeros_like(head_ref)
    w_neigh = split(w_neigh_ref[...])
    w_head = w_head_ref[...]
    for copy in copies[:3]:
        copy.wait()
    add_tiles(list_ref, weights_ref, buffer_ref, sems, lambda i: sources_ref[i], acc_ref)
    for copy in copies[3:]:
        copy.wait()
    width = feat_ref.shape[1]
    half = col_ref.shape[1] // 2

    def dense(i, carry):
        where = pl.ds(pl.multiple_of(i * CHUNK, CHUNK), CHUNK)
        columns = col_ref[where, :]
        mean = split(acc_ref[where, :] * columns[:, 0:1])
        pre = base_ref[where, :] + dot3(mean, w_neigh)
        sig = jax.nn.sigmoid(pre)
        hidden = pre * sig
        score = jnp.sum(hidden * w_head, axis=1, keepdims=True)
        dscore = (score - columns[:, half : half + 1]) * scale
        dpre = dscore * w_head * (sig * (1.0 + pre * (1.0 - sig)))
        bias_ref[...] += jnp.sum(dpre.reshape(CHUNK // 8, 8, width), axis=0)
        head_ref[...] += jnp.sum((hidden * dscore).reshape(CHUNK // 8, 8, width), axis=0)
        dpre = split(dpre)
        total_ref[0:width, :] += dot3(split(feat_ref[where, :]), dpre, ((0,), (0,)))
        total_ref[width : 2 * width, :] += dot3(mean, dpre, ((0,), (0,)))
        return carry

    lax.fori_loop(0, feat_ref.shape[0] // CHUNK, dense, 0)

    me = place_ref[0]
    rows = 2 * width // 8
    extra = keep_ref.shape[1] - rows
    row_ids = lax.broadcasted_iota(jnp.int32, (extra, width), 0)
    vectors = jnp.where(row_ids == 0, jnp.sum(bias_ref[...], axis=0, keepdims=True), 0.0)
    vectors = jnp.where(row_ids == 1, jnp.sum(head_ref[...], axis=0, keepdims=True), vectors)
    for ref, away in ((keep_ref, 0), (send_ref, 4)):
        for j in range(4):
            piece = me ^ (away + j)
            ref[j, 0:rows, :] = total_ref[pl.ds(pl.multiple_of(piece * rows, rows), rows), :]
            ref[j, rows:, :] = jnp.where(piece == 0, vectors, 0.0)


def finish_kernel(place_ref, mine_ref, other_ref, self_ref, neigh_ref, bias_ref, head_ref):
    me = place_ref[0]
    width = self_ref.shape[1]
    rows = 2 * width // 8
    for ref, away in ((mine_ref, 0), (other_ref, 4)):
        for j in range(4):
            piece = me ^ (away + j)
            part = ref[j, 0:rows, :]
            at = pl.ds(pl.multiple_of(lax.rem(piece, 4) * rows, rows), rows)

            @pl.when(piece < 4)
            def _():
                self_ref[at, :] = part

            @pl.when(piece >= 4)
            def _():
                neigh_ref[at, :] = part

            @pl.when(piece == 0)
            def _():
                bias_ref[...] = ref[j, rows : rows + 1, :]
                head_ref[...] = ref[j, rows + 1 : rows + 2, :]


def shape(*dims, dtype=F32):
    return jax.ShapeDtypeStruct(dims, dtype)


SMEM = pl.BlockSpec(memory_space=pltpu.SMEM)
VMEM = pl.BlockSpec(memory_space=pltpu.VMEM)
ANY = pl.BlockSpec(memory_space=pl.ANY)


def on_device(
    peers,
    features,
    w_self,
    w_neigh,
    bias,
    w_head,
    tile_weights,
    tile_dst,
    tile_src,
    tile_count,
    hub_block,
    send_rows,
    send_count,
    labels,
):
    tiles, size, _ = tile_weights.shape
    verts, width = features.shape
    blocks = verts // size
    slots = send_rows.shape[2]
    border_blocks = peers * slots // size
    me = (lax.axis_index("vert") * lax.axis_size("row") + lax.axis_index("row")).astype(jnp.int32)

    bits = peers.bit_length() - 1
    core = 2
    line = [k << (bits - 2) for k in (1, 2, 3)]
    plane = [1 << b for b in range(bits - 2) if 1 << b != core]
    order = (plane[::-1], plane)

    def across(x, mask_of):
        return lax.ppermute(x, AXES, [(i, i ^ mask_of(i)) for i in range(peers)])

    source = tile_src.astype(jnp.int32)
    hub = jnp.clip(source - blocks - border_blocks, 0, peers - 1)
    apart = hub ^ me
    place_in_line = apart >> (bits - 2)
    sender_core = (hub >> 1) & 1
    steps = len(plane)

    def differs(s):
        return jnp.where(sender_core == 0, apart & order[0][s], apart & order[1][s]) != 0

    held_blocks, far_blocks = peers // 4, peers // 8
    index = place_in_line
    for s in range(steps - 1):
        index = index + jnp.where(differs(s), 4 << s, 0)
    through = differs(steps - 1)
    late = through & (index >= far_blocks)
    early_code = 65536 + border_blocks + index + jnp.where(through, held_blocks, 0)
    early_code = early_code + jnp.where((apart & core) != 0, held_blocks + far_blocks, 0)
    late_code = 2 * 65536 + index - far_blocks + jnp.where((apart & core) != 0, far_blocks, 0)
    code = jnp.where(late, late_code, early_code)
    code = jnp.where(source < blocks + border_blocks, 65536 + source - blocks, code)
    code = jnp.where(source < blocks, source, code)

    mine = lax.dynamic_slice_in_dim(features, hub_block[0] * size, size, 0)[None]
    held = jnp.concatenate([mine] + [across(mine, lambda i, m=m: m) for m in line], 0)

    acc, outgoing, early_list, late_list = pl.pallas_call(
        own_kernel,
        out_shape=(
            shape(verts, width),
            shape(peers, slots, width),
            shape(tiles + 8, dtype=jnp.int32),
            shape(tiles + 8, dtype=jnp.int32),
        ),
        in_specs=[SMEM] * 5 + [VMEM, ANY],
        out_specs=(VMEM, VMEM, SMEM, SMEM),
        scratch_shapes=[
            pltpu.SMEM((tiles + 8,), jnp.int32),
            pltpu.VMEM((BUFFERS, size, size), F32),
            pltpu.SemaphoreType.DMA((BUFFERS,)),
        ],
        compiler_params=pltpu.CompilerParams(vmem_limit_bytes=VMEM_BYTES),
        cost_estimate=pl.CostEstimate(flops=8_000_000_000, bytes_accessed=24_000_000, transcendentals=0),
        name="own_tiles",
    )(
        tile_dst, code, tile_count, send_rows.reshape(-1), send_count.reshape(-1),
        features, tile_weights,
    )
    held, acc, outgoing = lax.optimization_barrier((held, acc, outgoing))

    pre, aux = pl.pallas_call(
        own_dense_kernel,
        out_shape=(shape(verts, width), shape(verts, size)),
        in_specs=[SMEM] * 2 + [VMEM, ANY, VMEM, VMEM, VMEM],
        out_specs=(VMEM, VMEM),
        scratch_shapes=[
            pltpu.VMEM((BUFFERS, size, size), F32),
            pltpu.VMEM((blocks, size, size), F32),
            pltpu.SemaphoreType.DMA((BUFFERS,)),
        ],
        compiler_params=pltpu.CompilerParams(vmem_limit_bytes=VMEM_BYTES),
        cost_estimate=pl.CostEstimate(flops=6_000_000_000, bytes_accessed=18_000_000, transcendentals=0),
        name="own_dense",
    )(
        tile_dst, tile_count, features, tile_weights, w_self, bias.reshape(1, width),
        labels.reshape(blocks, size),
    )

    incoming = lax.all_to_all(outgoing, AXES, split_axis=0, concat_axis=0, tiled=True)
    border = incoming.reshape(border_blocks, size, width)

    for s in range(steps - 1):
        near = held
        held = jnp.concatenate([held, across(held, lambda i, s=s: order[(i >> 1) & 1][s])], 0)
    far_near = across(near, lambda i: order[(i >> 1) & 1][steps - 1])
    held, far_near, border, pre, aux = lax.optimization_barrier((held, far_near, border, pre, aux))
    far = across(held[far_blocks:], lambda i: order[(i >> 1) & 1][steps - 1])
    held_other = across(held, lambda i: core)
    far_near_other = across(far_near, lambda i: core)

    acc = pl.pallas_call(
        early_kernel,
        out_shape=shape(verts, width),
        in_specs=[SMEM] + [ANY] * 5 + [VMEM, ANY],
        out_specs=VMEM,
        scratch_shapes=[
            pltpu.VMEM((BUFFERS, size, size), F32),
            pltpu.VMEM((border_blocks + 2 * (held_blocks + far_blocks), size, width), F32),
            pltpu.SemaphoreType.DMA((BUFFERS,)),
            pltpu.SemaphoreType.DMA((5,)),
        ],
        input_output_aliases={6: 0},
        compiler_params=pltpu.CompilerParams(vmem_limit_bytes=VMEM_BYTES),
        cost_estimate=pl.CostEstimate(flops=6_000_000_000, bytes_accessed=12_000_000, transcendentals=0),
        name="early_tiles",
    )(early_list, border, held, far_near, held_other, far_near_other, acc, tile_weights)
    far, acc = lax.optimization_barrier((far, acc))
    far_other = across(far, lambda i: core)

    place = ((me >> 1) & 1) * 4 + ((me >> 2) & 1) * 2 + (me & 1)
    place = place.reshape(1)
    piece_rows = 2 * width // 8 + 8
    keep, send = pl.pallas_call(
        functools.partial(late_kernel, scale=1.0 / math.sqrt(verts * peers)),
        out_shape=(shape(4, piece_rows, width), shape(4, piece_rows, width)),
        in_specs=[SMEM, SMEM] + [ANY] * 7 + [VMEM, VMEM],
        out_specs=(VMEM, VMEM),
        scratch_shapes=[
            pltpu.VMEM((BUFFERS, size, size), F32),
            pltpu.VMEM((2 * far_blocks, size, width), F32),
            pltpu.VMEM((verts, width), F32),
            pltpu.VMEM((verts, width), F32),
            pltpu.VMEM((verts, width), F32),
            pltpu.VMEM((verts, size), F32),
            pltpu.VMEM((2 * width, width), F32),
            pltpu.VMEM((8, width), F32),
            pltpu.VMEM((8, width), F32),
            pltpu.SemaphoreType.DMA((BUFFERS,)),
            pltpu.SemaphoreType.DMA((6,)),
        ],
        compiler_params=pltpu.CompilerParams(vmem_limit_bytes=VMEM_BYTES),
        cost_estimate=pl.CostEstimate(flops=12_000_000_000, bytes_accessed=20_000_000, transcendentals=0),
        name="late_tiles_and_gradients",
    )(
        late_list, place, far, far_other, acc, tile_weights, features, pre, aux,
        w_neigh, w_head.reshape(1, width),
    )

    held = keep + across(send, lambda i: core)
    reach = (0, 1, 4, 5)
    got = [held[0]] + [across(held[j], lambda i, j=j: reach[j]) for j in (1, 2, 3)]
    total = (got[0] + got[1]) + (got[2] + got[3])
    for low in range(3, bits, 2):
        masks = [1 << low] if low + 1 == bits else [k << low for k in (1, 2, 3)]
        more = [across(total, lambda i, m=m: m) for m in masks]
        total = total + more[0] if len(more) == 1 else (total + more[0]) + (more[1] + more[2])
    mine = jnp.stack([total] + [across(total, lambda i, j=j: reach[j]) for j in (1, 2, 3)])
    other = across(mine, lambda i: core)
    grad_self, grad_neigh, grad_bias, grad_head = pl.pallas_call(
        finish_kernel,
        out_shape=(shape(width, width), shape(width, width), shape(1, width), shape(1, width)),
        in_specs=[SMEM, VMEM, VMEM],
        out_specs=(VMEM, VMEM, VMEM, VMEM),
        name="assemble",
    )(place, mine, other)
    return (grad_self, grad_neigh, grad_bias.reshape(width), grad_head.reshape(width))


def solution(mesh):
    peers = math.prod(mesh.shape.values())
    in_specs = (
        P(AXES, None),
        P(),
        P(),
        P(),
        P(),
        P(AXES, None, None),
        P(AXES),
        P(AXES),
        P(AXES),
        P(AXES),
        P(AXES, None, None),
        P(AXES, None),
        P(AXES),
    )
    out_specs = (P(), P(), P(), P())
    return jax.shard_map(
        functools.partial(on_device, peers),
        mesh=mesh,
        in_specs=in_specs,
        out_specs=out_specs,
        check_vma=False,
    )
```

time: 334 us -> 130 us (0.39); the launches traced: 328 us -> 129 us
  waiting for transfers between devices: 123 us -> 18.6 us
  matrix products: 84 us -> 0 us
  blocking collectives: 39.2 us -> 0 us
  starting transfers between devices: 7.38 us -> 46.5 us
  Pallas kernels: 0 us -> 36.9 us
  local copies, waits for them, and re-layouts: 42 us -> 23.7 us
  other arithmetic: 16.6 us -> 0.89 us
  between operations: 15.8 us -> 2.16 us
    dot_general x9 -> x0, matrix products: 84 us -> none  [the longest x1 34.3 us: on_device(): jnp.einsum('tij,tjf->tif', tile_weights, picked, precision=FULL_PRECISION)]
    psum x1 -> x0, waiting for transfers between devices: 82.6 us -> none  [on_device(): lax.psum((local_self, local_neigh, local_bias, local_head), ('vert', 'row'))]
    ppermute x0 -> x20, starting transfers between devices: none -> 42.5 us  [across(): return lax.ppermute(x, AXES, [(i, i ^ mask_of(i)) for i in range(peers)])]
    all_gather x1 -> x0, waiting for transfers between devices: 40.7 us -> none  [on_device(): hub_blocks = lax.all_gather(hub_local, ('vert', 'row'), axis=0, tiled=True)]
    psum x1 -> x0, blocking collectives: 39.2 us -> none  [on_device(): lax.psum((local_self, local_neigh, local_bias, local_head), ('vert', 'row'))]
    pallas_call x0 -> x5, Pallas kernels: none -> 36.9 us  [the longest x1 16.1 us: on_device(): pl.pallas_call(functools.partial(late_kernel, scale=1.0 / math.sqrt(verts...]
    unnamed x24 -> x41, local copies, waits for them, and re-layouts: 3.52 us -> 22.6 us
    ppermute x0 -> x20, waiting for transfers between devices: none -> 18.6 us  [across(): return lax.ppermute(x, AXES, [(i, i ^ mask_of(i)) for i in range(peers)])]
  transfers between devices with their start and end apart: 3 -> 21, of which waited for: 2 -> 12; matrix products, arithmetic and copies ran while one was open for 7% -> 1% of each run, Pallas kernels for 0% -> 15%
where the time goes in v1:
time: 130 us; the launch traced here: 129 us
  starting transfers between devices  46.5 us (36%)
  Pallas kernels  36.9 us (28%)
  local copies, waits for them, and re-layouts  23.7 us (18%)
  waiting for transfers between devices  18.6 us (14%)
  between operations  2.16 us (2%)
    ppermute x20, starting transfers between devices, across(): return lax.ppermute(x, AXES, [(i, i ^ mask_of(i)) for i in range(peers)])  42.5 us
    unnamed x41, local copies, waits for them, and re-layouts  22.6 us
    ppermute x20, waiting for transfers between devices, across(): return lax.ppermute(x, AXES, [(i, i ^ mask_of(i)) for i in range(peers)])  18.6 us
    pallas_call x1, Pallas kernels, on_device(): pl.pallas_call(functools.partial(late_kernel, scale=1.0 / math.sqrt(verts...  16.1 us
    pallas_call x1, Pallas kernels, on_device(): pl.pallas_call(own_dense_kernel, out_shape=(shape(verts, width), shape(ve...  9.51 us
    pallas_call x1, Pallas kernels, on_device(): pl.pallas_call(own_kernel, out_shape=(shape(verts, width), shape(peers, s...  5.79 us
    all_to_all x1, starting transfers between devices, on_device(): lax.all_to_all(outgoing, AXES, split_axis=0, concat_axis=0, tiled=True)  3.97 us
    pallas_call x1, Pallas kernels, on_device(): pl.pallas_call(early_kernel, out_shape=shape(verts, width), in_specs=[SME...  3.55 us
  transfers between devices with their start and end apart: 21, of which 12 were waited for; matrix products, arithmetic and copies ran while one was open for 1% of the time, Pallas kernels for 15%

profile of v1, /device:TPU:0, one launch (start us, length us, event | category | flops | bytes accessed | tf_op | source)
XLA Modules:
  0.0 128.7 jit_solution(14457098810592111855)
XLA Ops:
  2.2 3.1 %collective-permute-start = (f32[1,128,256]{2,1,0:T(8,128)S(1)}, f32[1,128,256]{2,1,0:T(8,128)S(1)}, u32[]{:S(2)}, u32[]{:S(2)}) collective-permute-start(f32[1,128,256]{2,1,0:T(8,128)S(1)} %dynamic-slice_bitcast_fusion), channel_id=1, source_target_pairs={{0,8},{1,9},{2,10},{3,11},{4,12},{5,13},{6,14},{7,15},{8,0},{9,1},... | collective-permute-start | bytes 393224 | tf_op jit(solution)/shard_map/ppermute | solution.py:315
  5.3 2.6 %collective-permute-start.1 = (f32[1,128,256]{2,1,0:T(8,128)S(1)}, f32[1,128,256]{2,1,0:T(8,128)S(1)}, u32[]{:S(2)}, u32[]{:S(2)}) collective-permute-start(f32[1,128,256]{2,1,0:T(8,128)S(1)} %dynamic-slice_bitcast_fusion), channel_id=1, source_target_pairs={{0,16},{1,17},{2,18},{3,19},{4,20},{5,21},{6,22},{7,23},{8,24},{9,... | collective-permute-start | bytes 393224 | tf_op jit(solution)/shard_map/ppermute | solution.py:315
  10.1 2.2 %copy-done = f32[4096,256]{1,0:T(8,128)S(1)} copy-done((f32[4096,256]{1,0:T(8,128)S(1)}, f32[4096,256]{1,0:T(8,128)}, u32[]{:S(2)}) %copy-start) | copy-done | bytes 4194328
  13.6 5.8 %own_tiles.1 = (f32[4096,256]{1,0:T(8,128)S(1)}, f32[32,8,256]{2,1,0:T(8,128)}, s32[136]{0:T(256)S(1)}, s32[136]{0:T(256)S(1)}) custom-call(s32[128]{0:T(128)S(1)} %copy-done.9, s32[128]{0:T(128)S(1)} %compare_select_fusion.code_ref, s32[1]{0:T(128)S(6)} %copy.20.count_ref, s32[256]{0:T(256)S(1)} %reshape.38.rows_ref, s32[32]{0:T(128)S(1)} %bitcast.31, ...), custom_call_target="tpu_custom_call" | custom-call | flops 8000000000 | bytes 24000000 | tf_op jit(solution)/shard_map/own_tiles/pallas_call | solution.py:343
  19.4 2.0 %copy-done.11 = f32[4096,256]{1,0:T(8,128)} copy-done((f32[4096,256]{1,0:T(8,128)}, f32[4096,256]{1,0:T(8,128)S(1)}, u32[]{:S(2)}) %copy-start.11) | copy-done | bytes 4194328
  21.5 8.0 %collective-permute-start.3 = (f32[4,128,256]{2,1,0:T(8,128)S(1)}, f32[4,128,256]{2,1,0:T(8,128)S(1)}, u32[]{:S(2)}, u32[]{:S(2)}) collective-permute-start(f32[4,128,256]{2,1,0:T(8,128)S(1)} %pad_maximum_fusion.1), channel_id=1, source_target_pairs={{0,4},{1,5},{2,3},{3,2},{4,0},{5,1},{6,7},{7,6},{8,12},{9,13},{10,... | collective-permute-start | bytes 1572872 | tf_op jit(solution)/shard_map/ppermute | solution.py:315
  29.5 2.4 %collective-permute-start.4 = (f32[4,128,256]{2,1,0:T(8,128)S(1)}, f32[4,128,256]{2,1,0:T(8,128)S(1)}, u32[]{:S(2)}, u32[]{:S(2)}) collective-permute-start(f32[4,128,256]{2,1,0:T(8,128)S(1)} %pad_maximum_fusion.1), channel_id=1, source_target_pairs={{0,1},{1,0},{2,6},{3,7},{4,5},{5,4},{6,2},{7,3},{8,9},{9,8},{10,14... | collective-permute-start | bytes 1572872 | tf_op jit(solution)/shard_map/ppermute | solution.py:315
  31.8 4.0 %all-to-all-start = ((f32[32,8,256]{2,1,0:T(8,128)}), f32[32,8,256]{2,1,0:T(8,128)S(1)}, u32[]{:S(2)}, u32[]{:S(2)}) async-start(f32[32,8,256]{2,1,0:T(8,128)} %get-tuple-element.30), calls=%async_computation | async-start | bytes 524288 | tf_op jit(solution)/shard_map/all_to_all | solution.py:385
  35.8 2.2 %copy-done.1 = f32[4096,256]{1,0:T(8,128)S(1)} copy-done((f32[4096,256]{1,0:T(8,128)S(1)}, f32[4096,256]{1,0:T(8,128)}, u32[]{:S(2)}) %copy-start.1) | copy-done | bytes 4194328
  38.0 9.5 %own_dense.1 = (f32[4096,256]{1,0:T(8,128)S(1)}, f32[4096,128]{1,0:T(8,128)S(1)}) custom-call(s32[128]{0:T(128)S(1)} %copy-done.10, s32[1]{0:T(128)S(6)} %copy.20.count_ref, f32[4096,256]{1,0:T(8,128)S(1)} %copy-done.1, f32[128,128,128]{2,1,0:T(8,128)} %weights_ref.7, f32[256,256]{1,0:T(8,128)S(1)} %copy-done.3, f32[1,256]{1,0:T(1,128)S(1)} %bitcast.29, ...), custom_call_target="tpu_custom_call" | custom-call | flops 6000000000 | bytes 18000000 | tf_op jit(solution)/shard_map/own_dense/pallas_call | solution.py:367
  47.5 1.9 %copy-done.15 = f32[4096,256]{1,0:T(8,128)} copy-done((f32[4096,256]{1,0:T(8,128)}, f32[4096,256]{1,0:T(8,128)S(1)}, u32[]{:S(2)}) %copy-start.15) | copy-done | bytes 4194328
  51.5 1.8 %collective-permute-start.5 = (f32[4,128,256]{2,1,0:T(8,128)S(1)}, f32[4,128,256]{2,1,0:T(8,128)S(1)}, u32[]{:S(2)}, u32[]{:S(2)}) collective-permute-start(f32[4,128,256]{2,1,0:T(8,128)S(1)} %slice.15), channel_id=1, source_target_pairs={{0,1},{1,0},{2,6},{3,7},{4,5},{5,4},{6,2},{7,3},{8,9},{9,8},{10,14... | collective-permute-start | bytes 1572872 | tf_op jit(solution)/shard_map/ppermute | solution.py:315
  54.4 2.2 %copy-done.12 = f32[4096,256]{1,0:T(8,128)S(1)} copy-done((f32[4096,256]{1,0:T(8,128)S(1)}, f32[4096,256]{1,0:T(8,128)}, u32[]{:S(2)}) %copy-start.12) | copy-done | bytes 4194328
  56.6 3.5 %early_tiles.1.acc_in_ref = f32[4096,256]{1,0:T(8,128)S(1)} custom-call(s32[136]{0:T(256)S(1)} %get-tuple-element.34.list_ref, f32[2,128,256]{2,1,0:T(8,128)S(1)} %bitcast.27, f32[8,128,256]{2,1,0:T(8,128)S(1)} %pad_maximum_fusion.mine_ref, f32[4,128,256]{2,1,0:T(8,128)S(1)} %collective-permute-done.4.far_ref, ...), custom_call_target="tpu_custom_call", output_to_operand_aliasing={{}: (6, {})} | custom-call | flops 6000000000 | bytes 12000000 | tf_op jit(solution)/shard_map/early_tiles/pallas_call | solution.py:397
  60.2 2.0 %copy-done.13 = f32[4096,256]{1,0:T(8,128)} copy-done((f32[4096,256]{1,0:T(8,128)}, f32[4096,256]{1,0:T(8,128)S(1)}, u32[]{:S(2)}) %copy-start.13) | copy-done | bytes 4194328
  62.2 4.4 %collective-permute-start.8 = (f32[4,128,256]{2,1,0:T(8,128)S(1)}, f32[4,128,256]{2,1,0:T(8,128)S(1)}, u32[]{:S(2)}, u32[]{:S(2)}) collective-permute-start(f32[4,128,256]{2,1,0:T(8,128)S(1)} %collective-permute-done.5.mine_ref), channel_id=1, source_target_pairs={{0,2},{1,3},{2,0},{3,1},{4,6},{5,7},{6,4},{7,5},{8,10},{9,11},{10,... | collective-permute-start | bytes 1572872 | tf_op jit(solution)/shard_map/ppermute | solution.py:315
  66.6 1.5 %collective-permute-done.8.other_ref = f32[4,128,256]{2,1,0:T(8,128)S(1)} collective-permute-done((f32[4,128,256]{2,1,0:T(8,128)S(1)}, f32[4,128,256]{2,1,0:T(8,128)S(1)}, u32[]{:S(2)}, u32[]{:S(2)}) %collective-permute-start.8) | collective-permute-done | bytes 524320 | tf_op jit(solution)/shard_map/ppermute | solution.py:315
  68.2 2.2 %copy-done.2 = f32[4096,256]{1,0:T(8,128)S(1)} copy-done((f32[4096,256]{1,0:T(8,128)S(1)}, f32[4096,256]{1,0:T(8,128)}, u32[]{:S(2)}) %copy-start.2) | copy-done | bytes 4194328
  70.3 2.2 %copy-done.14 = f32[4096,256]{1,0:T(8,128)S(1)} copy-done((f32[4096,256]{1,0:T(8,128)S(1)}, f32[4096,256]{1,0:T(8,128)}, u32[]{:S(2)}) %copy-start.14) | copy-done | bytes 4194328
  72.5 1.6 %copy-done.17 = f32[4096,128]{1,0:T(8,128)S(1)} copy-done((f32[4096,128]{1,0:T(8,128)S(1)}, f32[4096,128]{1,0:T(8,128)}, u32[]{:S(2)}) %copy-start.17) | copy-done | bytes 2097176
  74.1 16.1 %late_tiles_and_gradients.1 = (f32[4,72,256]{2,1,0:T(8,128)S(1)}, f32[4,72,256]{2,1,0:T(8,128)S(1)}) custom-call(s32[136]{0:T(256)S(1)} %get-tuple-element.26.list_ref, s32[1]{0:T(128)} %bitcast.place_ref, f32[4,128,256]{2,1,0:T(8,128)S(1)} %collective-permute-done.5.mine_ref, f32[4,128,256]{2,1,0:T(8,128)S(1)} %collective-permute-done.8.other_ref, ...), custom_call_target="tpu_custom_call" | custom-call | flops 12000000000 | bytes 20000000 | tf_op jit(solution)/shard_map/late_tiles_and_gradients/pallas_call | solution.py:419
  91.9 2.3 %collective-permute-start.10 = (f32[72,256]{1,0:T(8,128)S(1)}, f32[72,256]{1,0:T(8,128)S(1)}, u32[]{:S(2)}, u32[]{:S(2)}) collective-permute-start(f32[72,256]{1,0:T(8,128)S(1)} %get-tuple-element.50), channel_id=1, source_target_pairs={{0,1},{1,0},{2,3},{3,2},{4,5},{5,4},{6,7},{7,6},{8,9},{9,8},{10,11... | collective-permute-start | bytes 221192 | tf_op jit(solution)/shard_map/ppermute | solution.py:315
  94.2 7.5 %collective-permute-start.11 = (f32[72,256]{1,0:T(8,128)S(1)}, f32[72,256]{1,0:T(8,128)S(1)}, u32[]{:S(2)}, u32[]{:S(2)}) collective-permute-start(f32[72,256]{1,0:T(8,128)S(1)} %get-tuple-element.49), channel_id=1, source_target_pairs={{0,4},{1,5},{2,6},{3,7},{4,0},{5,1},{6,2},{7,3},{8,12},{9,13},{10,... | collective-permute-start | bytes 221192 | tf_op jit(solution)/shard_map/ppermute | solution.py:315
  103.1 1.4 %collective-permute-done.11 = f32[72,256]{1,0:T(8,128)S(1)} collective-permute-done((f32[72,256]{1,0:T(8,128)S(1)}, f32[72,256]{1,0:T(8,128)S(1)}, u32[]{:S(2)}, u32[]{:S(2)}) %collective-permute-start.11) | collective-permute-done | bytes 73760 | tf_op jit(solution)/shard_map/ppermute | solution.py:315
  104.5 2.7 %collective-permute-done.12 = f32[72,256]{1,0:T(8,128)S(1)} collective-permute-done((f32[72,256]{1,0:T(8,128)S(1)}, f32[72,256]{1,0:T(8,128)S(1)}, u32[]{:S(2)}, u32[]{:S(2)}) %collective-permute-start.12) | collective-permute-done | bytes 73760 | tf_op jit(solution)/shard_map/ppermute | solution.py:315
  107.8 3.2 %collective-permute-start.14 = (f32[72,256]{1,0:T(8,128)S(1)}, f32[72,256]{1,0:T(8,128)S(1)}, u32[]{:S(2)}, u32[]{:S(2)}) collective-permute-start(f32[72,256]{1,0:T(8,128)S(1)} %fusion.1), channel_id=1, source_target_pairs={{0,16},{1,17},{2,18},{3,19},{4,20},{5,21},{6,22},{7,23},{8,24},{9,... | collective-permute-start | bytes 221192 | tf_op jit(solution)/shard_map/ppermute | solution.py:315
  111.9 2.5 %collective-permute-done.14 = f32[72,256]{1,0:T(8,128)S(1)} collective-permute-done((f32[72,256]{1,0:T(8,128)S(1)}, f32[72,256]{1,0:T(8,128)S(1)}, u32[]{:S(2)}, u32[]{:S(2)}) %collective-permute-start.14) | collective-permute-done | bytes 73760 | tf_op jit(solution)/shard_map/ppermute | solution.py:315
  114.5 2.6 %collective-permute-done.15 = f32[72,256]{1,0:T(8,128)S(1)} collective-permute-done((f32[72,256]{1,0:T(8,128)S(1)}, f32[72,256]{1,0:T(8,128)S(1)}, u32[]{:S(2)}, u32[]{:S(2)}) %collective-permute-start.15) | collective-permute-done | bytes 73760 | tf_op jit(solution)/shard_map/ppermute | solution.py:315
  119.1 1.6 %collective-permute-start.18 = (f32[72,256]{1,0:T(8,128)S(1)}, f32[72,256]{1,0:T(8,128)S(1)}, u32[]{:S(2)}, u32[]{:S(2)}) collective-permute-start(f32[72,256]{1,0:T(8,128)S(1)} %add_add_fusion), channel_id=1, source_target_pairs={{0,5},{1,4},{2,7},{3,6},{4,1},{5,0},{6,3},{7,2},{8,13},{9,12},{10,... | collective-permute-start | bytes 221192 | tf_op jit(solution)/shard_map/ppermute | solution.py:315
  122.2 2.2 %collective-permute-done.18 = f32[72,256]{1,0:T(8,128)S(1)} collective-permute-done((f32[72,256]{1,0:T(8,128)S(1)}, f32[72,256]{1,0:T(8,128)S(1)}, u32[]{:S(2)}, u32[]{:S(2)}) %collective-permute-start.18) | collective-permute-done | bytes 73760 | tf_op jit(solution)/shard_map/ppermute | solution.py:315
  124.5 1.6 %collective-permute-done.19.other_ref = f32[4,72,256]{2,1,0:T(8,128)S(1)} collective-permute-done((f32[4,72,256]{2,1,0:T(8,128)S(1)}, f32[4,72,256]{2,1,0:T(8,128)S(1)}, u32[]{:S(2)}, u32[]{:S(2)}) %collective-permute-start.19) | collective-permute-done | bytes 294944 | tf_op jit(solution)/shard_map/ppermute | solution.py:315
  126.8 2.0 %assemble.1 = (f32[256,256]{1,0:T(8,128)}, f32[256,256]{1,0:T(8,128)}, f32[1,256]{1,0:T(1,128)}, f32[1,256]{1,0:T(1,128)}) custom-call(s32[1]{0:T(128)} %bitcast.place_ref, f32[4,72,256]{2,1,0:T(8,128)} %copy-done.18, f32[4,72,256]{2,1,0:T(8,128)} %copy-done.19), custom_call_target="tpu_custom_call" | custom-call | tf_op jit(solution)/shard_map/assemble/pallas_call | solution.py:455
  (67 shorter events, 16.0 us)
Async XLA Ops:
  2.2 19.2 %collective-permute-start = (f32[1,128,256]{2,1,0:T(8,128)S(1)}, f32[1,128,256]{2,1,0:T(8,128)S(1)}, u32[]{:S(2)}, u32[]{:S(2)}) collective-permute-start(f32[1,128,256]{2,1,0:T(8,128)S(1)} %dynamic-slice_bitcast_fusion), channel_id=1, source_target_pairs={{0,8},{1,9},{2,10},{3,11},{4,12},{5,13},{6,14},{7,15},{8,0},{9,1},... | collective-permute-start | bytes 393224 | tf_op jit(solution)/shard_map/ppermute | solution.py:315
  5.3 16.1 %collective-permute-start.1 = (f32[1,128,256]{2,1,0:T(8,128)S(1)}, f32[1,128,256]{2,1,0:T(8,128)S(1)}, u32[]{:S(2)}, u32[]{:S(2)}) collective-permute-start(f32[1,128,256]{2,1,0:T(8,128)S(1)} %dynamic-slice_bitcast_fusion), channel_id=1, source_target_pairs={{0,16},{1,17},{2,18},{3,19},{4,20},{5,21},{6,22},{7,23},{8,24},{9,... | collective-permute-start | bytes 393224 | tf_op jit(solution)/shard_map/ppermute | solution.py:315
  7.9 13.5 %collective-permute-start.2 = (f32[1,128,256]{2,1,0:T(8,128)S(1)}, f32[1,128,256]{2,1,0:T(8,128)S(1)}, u32[]{:S(2)}, u32[]{:S(2)}) collective-permute-start(f32[1,128,256]{2,1,0:T(8,128)S(1)} %dynamic-slice_bitcast_fusion), channel_id=1, source_target_pairs={{0,24},{1,25},{2,26},{3,27},{4,28},{5,29},{6,30},{7,31},{8,16},{9,... | collective-permute-start | bytes 393224 | tf_op jit(solution)/shard_map/ppermute | solution.py:315
  10.1 2.2 %copy-start = (f32[4096,256]{1,0:T(8,128)S(1)}, f32[4096,256]{1,0:T(8,128)}, u32[]{:S(2)}) copy-start(f32[4096,256]{1,0:T(8,128)} %features_ref.5) | copy-start | bytes 12582916
  13.6 22.2 %copy-start.3 = (f32[256,256]{1,0:T(8,128)S(1)}, f32[256,256]{1,0:T(8,128)}, u32[]{:S(2)}) copy-start(f32[256,256]{1,0:T(8,128)} %w_self_ref.1) | copy-start | bytes 786436
  13.6 22.2 %copy-start.5 = (s32[4096]{0:T(1024)S(1)}, s32[4096]{0:T(1024)}, u32[]{:S(2)}) copy-start(s32[4096]{0:T(1024)} %param.25) | copy-start | bytes 49156
  13.6 22.2 %copy-start.6 = (f32[256]{0:T(256)S(1)}, f32[256]{0:T(256)}, u32[]{:S(2)}) copy-start(f32[256]{0:T(256)} %param.16) | copy-start | bytes 3076
  13.6 22.2 %copy-start.10 = (s32[128]{0:T(128)S(1)}, s32[128]{0:T(128)}, u32[]{:S(2)}) copy-start(s32[128]{0:T(128)} %dst_ref.3) | copy-start | bytes 1540
  21.5 29.4 %collective-permute-start.3 = (f32[4,128,256]{2,1,0:T(8,128)S(1)}, f32[4,128,256]{2,1,0:T(8,128)S(1)}, u32[]{:S(2)}, u32[]{:S(2)}) collective-permute-start(f32[4,128,256]{2,1,0:T(8,128)S(1)} %pad_maximum_fusion.1), channel_id=1, source_target_pairs={{0,4},{1,5},{2,3},{3,2},{4,0},{5,1},{6,7},{7,6},{8,12},{9,13},{10,... | collective-permute-start | bytes 1572872 | tf_op jit(solution)/shard_map/ppermute | solution.py:315
  29.5 21.5 %collective-permute-start.4 = (f32[4,128,256]{2,1,0:T(8,128)S(1)}, f32[4,128,256]{2,1,0:T(8,128)S(1)}, u32[]{:S(2)}, u32[]{:S(2)}) collective-permute-start(f32[4,128,256]{2,1,0:T(8,128)S(1)} %pad_maximum_fusion.1), channel_id=1, source_target_pairs={{0,1},{1,0},{2,6},{3,7},{4,5},{5,4},{6,2},{7,3},{8,9},{9,8},{10,14... | collective-permute-start | bytes 1572872 | tf_op jit(solution)/shard_map/ppermute | solution.py:315
  31.8 19.1 %all-to-all-start = ((f32[32,8,256]{2,1,0:T(8,128)}), f32[32,8,256]{2,1,0:T(8,128)S(1)}, u32[]{:S(2)}, u32[]{:S(2)}) async-start(f32[32,8,256]{2,1,0:T(8,128)} %get-tuple-element.30), calls=%async_computation | async-start | bytes 524288 | tf_op jit(solution)/shard_map/all_to_all | solution.py:385
  35.8 2.2 %copy-start.1 = (f32[4096,256]{1,0:T(8,128)S(1)}, f32[4096,256]{1,0:T(8,128)}, u32[]{:S(2)}) copy-start(f32[4096,256]{1,0:T(8,128)} %features_ref.5) | copy-start | bytes 12582916
  50.9 3.5 %collective-permute-start.6 = (f32[8,128,256]{2,1,0:T(8,128)S(1)}, f32[8,128,256]{2,1,0:T(8,128)S(1)}, u32[]{:S(2)}, u32[]{:S(2)}) collective-permute-start(f32[8,128,256]{2,1,0:T(8,128)S(1)} %pad_maximum_fusion.mine_ref), channel_id=1, source_target_pairs={{0,2},{1,3},{2,0},{3,1},{4,6},{5,7},{6,4},{7,5},{8,10},{9,11},{10,... | collective-permute-start | bytes 3145736 | tf_op jit(solution)/shard_map/ppermute | solution.py:315
  51.2 3.2 %collective-permute-start.7 = (f32[4,128,256]{2,1,0:T(8,128)S(1)}, f32[4,128,256]{2,1,0:T(8,128)S(1)}, u32[]{:S(2)}, u32[]{:S(2)}) collective-permute-start(f32[4,128,256]{2,1,0:T(8,128)S(1)} %collective-permute-done.4.far_ref), channel_id=1, source_target_pairs={{0,2},{1,3},{2,0},{3,1},{4,6},{5,7},{6,4},{7,5},{8,10},{9,11},{10,... | collective-permute-start | bytes 1572872 | tf_op jit(solution)/shard_map/ppermute | solution.py:315
  51.5 10.6 %collective-permute-start.5 = (f32[4,128,256]{2,1,0:T(8,128)S(1)}, f32[4,128,256]{2,1,0:T(8,128)S(1)}, u32[]{:S(2)}, u32[]{:S(2)}) collective-permute-start(f32[4,128,256]{2,1,0:T(8,128)S(1)} %slice.15), channel_id=1, source_target_pairs={{0,1},{1,0},{2,6},{3,7},{4,5},{5,4},{6,2},{7,3},{8,9},{9,8},{10,14... | collective-permute-start | bytes 1572872 | tf_op jit(solution)/shard_map/ppermute | solution.py:315
  54.4 2.2 %copy-start.12 = (f32[4096,256]{1,0:T(8,128)S(1)}, f32[4096,256]{1,0:T(8,128)}, u32[]{:S(2)}) copy-start(f32[4096,256]{1,0:T(8,128)} %copy-done.11) | copy-start | bytes 12582916
  56.6 11.6 %copy-start.4 = (f32[256,256]{1,0:T(8,128)S(1)}, f32[256,256]{1,0:T(8,128)}, u32[]{:S(2)}) copy-start(f32[256,256]{1,0:T(8,128)} %w_neigh_ref.1) | copy-start | bytes 786436
  56.6 11.6 %copy-start.7 = (f32[256]{0:T(256)S(1)}, f32[256]{0:T(256)}, u32[]{:S(2)}) copy-start(f32[256]{0:T(256)} %param.17) | copy-start | bytes 3076
  62.2 6.0 %collective-permute-start.8 = (f32[4,128,256]{2,1,0:T(8,128)S(1)}, f32[4,128,256]{2,1,0:T(8,128)S(1)}, u32[]{:S(2)}, u32[]{:S(2)}) collective-permute-start(f32[4,128,256]{2,1,0:T(8,128)S(1)} %collective-permute-done.5.mine_ref), channel_id=1, source_target_pairs={{0,2},{1,3},{2,0},{3,1},{4,6},{5,7},{6,4},{7,5},{8,10},{9,11},{10,... | collective-permute-start | bytes 1572872 | tf_op jit(solution)/shard_map/ppermute | solution.py:315
  68.2 2.2 %copy-start.2 = (f32[4096,256]{1,0:T(8,128)S(1)}, f32[4096,256]{1,0:T(8,128)}, u32[]{:S(2)}) copy-start(f32[4096,256]{1,0:T(8,128)} %features_ref.5) | copy-start | bytes 12582916
  70.3 2.2 %copy-start.14 = (f32[4096,256]{1,0:T(8,128)S(1)}, f32[4096,256]{1,0:T(8,128)}, u32[]{:S(2)}) copy-start(f32[4096,256]{1,0:T(8,128)} %copy-done.13) | copy-start | bytes 12582916
  90.2 1.6 %collective-permute-start.9 = (f32[4,72,256]{2,1,0:T(8,128)S(1)}, f32[4,72,256]{2,1,0:T(8,128)S(1)}, u32[]{:S(2)}, u32[]{:S(2)}) collective-permute-start(f32[4,72,256]{2,1,0:T(8,128)S(1)} %get-tuple-element.43), channel_id=1, source_target_pairs={{0,2},{1,3},{2,0},{3,1},{4,6},{5,7},{6,4},{7,5},{8,10},{9,11},{10,... | collective-permute-start | bytes 884744 | tf_op jit(solution)/shard_map/ppermute | solution.py:315
  91.9 11.2 %collective-permute-start.10 = (f32[72,256]{1,0:T(8,128)S(1)}, f32[72,256]{1,0:T(8,128)S(1)}, u32[]{:S(2)}, u32[]{:S(2)}) collective-permute-start(f32[72,256]{1,0:T(8,128)S(1)} %get-tuple-element.50), channel_id=1, source_target_pairs={{0,1},{1,0},{2,3},{3,2},{4,5},{5,4},{6,7},{7,6},{8,9},{9,8},{10,11... | collective-permute-start | bytes 221192 | tf_op jit(solution)/shard_map/ppermute | solution.py:315
  94.2 10.3 %collective-permute-start.11 = (f32[72,256]{1,0:T(8,128)S(1)}, f32[72,256]{1,0:T(8,128)S(1)}, u32[]{:S(2)}, u32[]{:S(2)}) collective-permute-start(f32[72,256]{1,0:T(8,128)S(1)} %get-tuple-element.49), channel_id=1, source_target_pairs={{0,4},{1,5},{2,6},{3,7},{4,0},{5,1},{6,2},{7,3},{8,12},{9,13},{10,... | collective-permute-start | bytes 221192 | tf_op jit(solution)/shard_map/ppermute | solution.py:315
  101.7 5.5 %collective-permute-start.12 = (f32[72,256]{1,0:T(8,128)S(1)}, f32[72,256]{1,0:T(8,128)S(1)}, u32[]{:S(2)}, u32[]{:S(2)}) collective-permute-start(f32[72,256]{1,0:T(8,128)S(1)} %get-tuple-element.48), channel_id=1, source_target_pairs={{0,5},{1,4},{2,7},{3,6},{4,1},{5,0},{6,3},{7,2},{8,13},{9,12},{10,... | collective-permute-start | bytes 221192 | tf_op jit(solution)/shard_map/ppermute | solution.py:315
  107.2 4.8 %collective-permute-start.13 = (f32[72,256]{1,0:T(8,128)S(1)}, f32[72,256]{1,0:T(8,128)S(1)}, u32[]{:S(2)}, u32[]{:S(2)}) collective-permute-start(f32[72,256]{1,0:T(8,128)S(1)} %fusion.1), channel_id=1, source_target_pairs={{0,8},{1,9},{2,10},{3,11},{4,12},{5,13},{6,14},{7,15},{8,0},{9,1},... | collective-permute-start | bytes 221192 | tf_op jit(solution)/shard_map/ppermute | solution.py:315
  107.8 6.7 %collective-permute-start.14 = (f32[72,256]{1,0:T(8,128)S(1)}, f32[72,256]{1,0:T(8,128)S(1)}, u32[]{:S(2)}, u32[]{:S(2)}) collective-permute-start(f32[72,256]{1,0:T(8,128)S(1)} %fusion.1), channel_id=1, source_target_pairs={{0,16},{1,17},{2,18},{3,19},{4,20},{5,21},{6,22},{7,23},{8,24},{9,... | collective-permute-start | bytes 221192 | tf_op jit(solution)/shard_map/ppermute | solution.py:315
  110.9 6.2 %collective-permute-start.15 = (f32[72,256]{1,0:T(8,128)S(1)}, f32[72,256]{1,0:T(8,128)S(1)}, u32[]{:S(2)}, u32[]{:S(2)}) collective-permute-start(f32[72,256]{1,0:T(8,128)S(1)} %fusion.1), channel_id=1, source_target_pairs={{0,24},{1,25},{2,26},{3,27},{4,28},{5,29},{6,30},{7,31},{8,16},{9,... | collective-permute-start | bytes 221192 | tf_op jit(solution)/shard_map/ppermute | solution.py:315
  117.1 4.4 %collective-permute-start.16 = (f32[72,256]{1,0:T(8,128)S(1)}, f32[72,256]{1,0:T(8,128)S(1)}, u32[]{:S(2)}, u32[]{:S(2)}) collective-permute-start(f32[72,256]{1,0:T(8,128)S(1)} %add_add_fusion), channel_id=1, source_target_pairs={{0,1},{1,0},{2,3},{3,2},{4,5},{5,4},{6,7},{7,6},{8,9},{9,8},{10,11... | collective-permute-start | bytes 221192 | tf_op jit(solution)/shard_map/ppermute | solution.py:315
  117.8 4.4 %collective-permute-start.17 = (f32[72,256]{1,0:T(8,128)S(1)}, f32[72,256]{1,0:T(8,128)S(1)}, u32[]{:S(2)}, u32[]{:S(2)}) collective-permute-start(f32[72,256]{1,0:T(8,128)S(1)} %add_add_fusion), channel_id=1, source_target_pairs={{0,4},{1,5},{2,6},{3,7},{4,0},{5,1},{6,2},{7,3},{8,12},{9,13},{10,... | collective-permute-start | bytes 221192 | tf_op jit(solution)/shard_map/ppermute | solution.py:315
  119.1 5.3 %collective-permute-start.18 = (f32[72,256]{1,0:T(8,128)S(1)}, f32[72,256]{1,0:T(8,128)S(1)}, u32[]{:S(2)}, u32[]{:S(2)}) collective-permute-start(f32[72,256]{1,0:T(8,128)S(1)} %add_add_fusion), channel_id=1, source_target_pairs={{0,5},{1,4},{2,7},{3,6},{4,1},{5,0},{6,3},{7,2},{8,13},{9,12},{10,... | collective-permute-start | bytes 221192 | tf_op jit(solution)/shard_map/ppermute | solution.py:315
  124.4 1.6 %collective-permute-start.19 = (f32[4,72,256]{2,1,0:T(8,128)S(1)}, f32[4,72,256]{2,1,0:T(8,128)S(1)}, u32[]{:S(2)}, u32[]{:S(2)}) collective-permute-start(f32[4,72,256]{2,1,0:T(8,128)S(1)} %pad_maximum_fusion.2.mine_ref), channel_id=1, source_target_pairs={{0,2},{1,3},{2,0},{3,1},{4,6},{5,7},{6,4},{7,5},{8,10},{9,11},{10,... | collective-permute-start | bytes 884744 | tf_op jit(solution)/shard_map/ppermute | solution.py:315
  (9 other events, 12.6 us)

commit v2 on v1

v2 whole, which is shorter than its diff:
```python
import functools
import math

import jax
import jax.numpy as jnp
from jax import lax
from jax.experimental import pallas as pl
from jax.experimental.pallas import tpu as pltpu
from jax.sharding import PartitionSpec as P

AXES = ("vert", "row")
F32 = jnp.float32
BF16 = jnp.bfloat16
LOADS = 8
GROUP = 8
CHUNK = 512
UNROLL = 4
COST = pl.CostEstimate(flops=1_000_000, bytes_accessed=100_000, transcendentals=0)
VMEM_BYTES = 44 * 1024 * 1024


def split(x):
    hi = x.astype(BF16)
    return hi, (x - hi.astype(F32)).astype(BF16)


def dot(a, b, contract=((1,), (0,))):
    return lax.dot_general(a, b, (contract, ((), ())), preferred_element_type=F32)


def dot3(a, b, contract=((1,), (0,))):
    (a_hi, a_lo), (b_hi, b_lo) = a, b
    return dot(a_hi, b_hi, contract) + dot(a_hi, b_lo, contract) + dot(a_lo, b_hi, contract)


def tile_product(weights, source):
    w_hi, w_lo = split(weights)
    s_hi, s_lo = split(source)
    wide = jnp.concatenate([w_hi, w_hi], 1)
    tall = jnp.concatenate([s_hi, s_lo], 0)
    return dot(wide, tall) + dot(w_lo, s_hi)


def add_tiles(list_ref, weights_ref, source_of, acc_ref, tile_of, ready):
    size = weights_ref.shape[1]
    total = list_ref[list_ref.shape[0] - 7]

    def step(group, carry):
        at = [group * GROUP + k for k in range(GROUP)]
        for i in at:
            ready(i, total)
        capped = [jnp.minimum(i, total - 1) for i in at]
        entries = [list_ref[i] for i in capped]
        products = [
            tile_product(weights_ref[tile_of(i, entry)], source_of(entry // 16384))
            for i, entry in zip(capped, entries)
        ]
        for i, entry, product in zip(at, entries, products):
            block = lax.rem(entry // 256, 64)
            where = pl.ds(pl.multiple_of(block * size, size), size)
            acc_ref[where, :] += jnp.where(i < total, product, 0.0)
        return carry

    lax.fori_loop(0, (total + GROUP - 1) // GROUP, step, 0)


def fetch_tiles(list_ref, weights_in_ref, weights_ref, sems):
    def copy(i):
        return pltpu.make_async_copy(
            weights_in_ref.at[lax.rem(list_ref[i], 256)], weights_ref.at[i], sems.at[i]
        )

    def start(i, carry):
        copy(i).start()
        return carry

    lax.fori_loop(0, list_ref[list_ref.shape[0] - 7], start, 0)

    def ready(i, total):
        @pl.when(i < total)
        def _():
            copy(i).wait()

    return ready


def own_kernel(
    dst_ref, code_ref, count_ref, rows_ref, used_ref, features_in_ref, weights_in_ref,
    acc_out_ref, outgoing_ref, early_ref, late_ref,
    own_ref, features_ref, weights_ref, acc_ref, sems,
):
    tiles, size, _ = weights_ref.shape
    loads = [
        pltpu.make_async_copy(features_in_ref, features_ref, sems.at[0]),
        pltpu.make_async_copy(features_in_ref, acc_ref, sems.at[1]),
    ]
    piece = tiles // LOADS
    for i in range(LOADS):
        part = pl.ds(i * piece, piece)
        loads.append(pltpu.make_async_copy(weights_in_ref.at[part], weights_ref.at[part], sems.at[i + 2]))
    for load in loads:
        load.start()
    _, peers, slots = rows_ref.shape
    lists = (own_ref, early_ref, late_ref)

    def sort(t, counts):
        code = code_ref[t]
        stage = code // 65536
        entry = (lax.rem(code, 65536) * 64 + dst_ref[t]) * 256 + t
        for ref, count in zip(lists, counts):
            ref[count] = entry
        return tuple(count + jnp.where(stage == i, 1, 0) for i, count in enumerate(counts))

    counts = lax.fori_loop(0, count_ref[0], sort, (jnp.int32(0),) * 3)
    for ref, count in zip(lists, counts):
        ref[tiles + 1] = count

    loads[0].wait()

    def gather(peer, carry):
        for k in range(slots):
            row = features_ref[pl.ds(rows_ref[0, peer, k], 1), :]
            outgoing_ref[peer, k : k + 1, :] = jnp.where(k < used_ref[0, peer], row, 0.0)
        return carry

    lax.fori_loop(0, peers, gather, 0)

    def source_of(block):
        return features_ref[pl.ds(pl.multiple_of(block * size, size), size), :]

    for load in loads[1:]:
        load.wait()
    add_tiles(own_ref, weights_ref, source_of, acc_ref, lambda i, entry: lax.rem(entry, 256), lambda i, total: None)
    store = pltpu.make_async_copy(acc_ref, acc_out_ref, sems.at[0])
    store.start()
    store.wait()


def own_dense_kernel(
    dst_ref, count_ref, features_in_ref, weights_in_ref, w_self_ref, bias_ref, labels_ref,
    pre_out_ref, aux_out_ref, done_ref,
    features_ref, weights_ref, pre_ref, aux_ref, weight_acc_ref, sems,
):
    done_ref[...] = jnp.zeros_like(done_ref)
    tiles, size, _ = weights_ref.shape
    blocks = weight_acc_ref.shape[0]
    loads = [
        pltpu.make_async_copy(features_in_ref, features_ref, sems.at[0]),
        pltpu.make_async_copy(weights_in_ref, weights_ref, sems.at[1]),
    ]
    for load in loads:
        load.start()
    weight_acc_ref[...] = jnp.zeros_like(weight_acc_ref)
    w_self = split(w_self_ref[...])
    loads[0].wait()

    def dense(i, carry):
        where = pl.ds(pl.multiple_of(i * CHUNK, CHUNK), CHUNK)
        pre_ref[where, :] = dot3(split(features_ref[where, :]), w_self) + bias_ref[...]
        return carry

    lax.fori_loop(0, features_ref.shape[0] // CHUNK, dense, 0, unroll=4)
    stores = [pltpu.make_async_copy(pre_ref, pre_out_ref, sems.at[0])]
    stores[0].start()
    loads[1].wait()

    def add(t, carry):
        weight_acc_ref[dst_ref[t]] += weights_ref[t]
        return carry

    lax.fori_loop(0, count_ref[0], add, 0)

    eye = lax.broadcasted_iota(jnp.int32, (size, size), 0) == lax.broadcasted_iota(jnp.int32, (size, size), 1)
    left = lax.broadcasted_iota(jnp.int32, (size, size), 1) < size // 2

    def columns(block, carry):
        inverse = 1.0 / (1.0 + jnp.sum(weight_acc_ref[block], axis=1, keepdims=True))
        target = 2.0 * labels_ref[pl.ds(block, 1), :].astype(F32) - 1.0
        target = jnp.sum(jnp.where(eye, jnp.broadcast_to(target, eye.shape), 0.0), axis=1, keepdims=True)
        aux_ref[pl.ds(pl.multiple_of(block * size, size), size), :] = jnp.where(left, inverse, target)
        return carry

    lax.fori_loop(0, blocks, columns, 0, unroll=4)
    stores.append(pltpu.make_async_copy(aux_ref, aux_out_ref, sems.at[1]))
    stores[1].start()
    for store in stores:
        store.wait()


def early_kernel(
    list_ref, border_ref, mine_ref, far_ref, other_ref, far_other_ref, acc_in_ref, weights_in_ref, before_ref,
    acc_out_ref, done_ref,
    weights_ref, acc_ref, sources_ref, sems, load_sems,
):
    del before_ref
    done_ref[...] = jnp.zeros_like(done_ref)
    at, copies = 0, [pltpu.make_async_copy(acc_in_ref, acc_ref, load_sems.at[5])]
    for i, part in enumerate((border_ref, mine_ref, far_ref, other_ref, far_other_ref)):
        blocks = part.shape[0]
        copies.append(pltpu.make_async_copy(part, sources_ref.at[pl.ds(at, blocks)], load_sems.at[i]))
        at += blocks
    for copy in copies:
        copy.start()
    ready = fetch_tiles(list_ref, weights_in_ref, weights_ref, sems)
    for copy in copies:
        copy.wait()
    add_tiles(list_ref, weights_ref, lambda i: sources_ref[i], acc_ref, lambda i, entry: i, ready)
    store = pltpu.make_async_copy(acc_ref, acc_out_ref, load_sems.at[0])
    store.start()
    store.wait()


def late_kernel(
    list_ref, place_ref, mine_ref, other_ref, acc_in_ref, weights_in_ref,
    features_in_ref, pre_in_ref, aux_in_ref, w_neigh_ref, w_head_ref, before_ref,
    keep_ref, send_ref,
    weights_ref, acc_ref, features_ref, pre_ref, aux_ref, sources_ref, total_ref, bias_ref, head_ref,
    sems, load_sems, chunk_sems, *, scale,
):
    del before_ref
    verts, width = features_ref.shape
    blocks = mine_ref.shape[0]
    loads = [
        (mine_ref, sources_ref.at[pl.ds(0, blocks)]),
        (other_ref, sources_ref.at[pl.ds(blocks, blocks)]),
        (acc_in_ref, acc_ref),
    ]
    copies = [pltpu.make_async_copy(a, b, load_sems.at[i]) for i, (a, b) in enumerate(loads)]
    for copy in copies:
        copy.start()
    ready = fetch_tiles(list_ref, weights_in_ref, weights_ref, sems)
    chunk_copies = []
    for i in range(verts // CHUNK):
        where = pl.ds(i * CHUNK, CHUNK)
        pairs = ((pre_in_ref, pre_ref), (aux_in_ref, aux_ref), (features_in_ref, features_ref))
        chunk_copies.append(
            [pltpu.make_async_copy(a.at[where], b.at[where], chunk_sems.at[i, j]) for j, (a, b) in enumerate(pairs)]
        )
        for copy in chunk_copies[-1]:
            copy.start()
    total_ref[...] = jnp.zeros_like(total_ref)
    bias_ref[...] = jnp.zeros_like(bias_ref)
    head_ref[...] = jnp.zeros_like(head_ref)
    w_neigh = split(w_neigh_ref[...])
    w_head = w_head_ref[...]
    for copy in copies:
        copy.wait()
    add_tiles(list_ref, weights_ref, lambda i: sources_ref[i], acc_ref, lambda i, entry: i, ready)
    half = aux_ref.shape[1] // 2

    def forward(i):
        where = pl.ds(i * CHUNK, CHUNK)
        columns = aux_ref[where, :]
        mean = split(acc_ref[where, :] * columns[:, 0:1])
        pre = pre_ref[where, :] + dot3(mean, w_neigh)
        sig = jax.nn.sigmoid(pre)
        hidden = pre * sig
        score = jnp.sum(hidden * w_head, axis=1, keepdims=True)
        dscore = (score - columns[:, half : half + 1]) * scale
        dpre = dscore * w_head * (sig * (1.0 + pre * (1.0 - sig)))
        bias_ref[...] += jnp.sum(dpre.reshape(CHUNK // 8, 8, width), axis=0)
        head_ref[...] += jnp.sum((hidden * dscore).reshape(CHUNK // 8, 8, width), axis=0)
        return where, mean, split(dpre)

    for first in range(0, verts // CHUNK, UNROLL):
        for i in range(first, first + UNROLL):
            for copy in chunk_copies[i]:
                copy.wait()
        parts = [forward(i) for i in range(first, first + UNROLL)]
        for where, mean, dpre in parts:
            total_ref[0:width, :] += dot3(split(features_ref[where, :]), dpre, ((0,), (0,)))
            total_ref[width : 2 * width, :] += dot3(mean, dpre, ((0,), (0,)))

    me = place_ref[0]
    rows = 2 * width // 8
    extra = keep_ref.shape[1] - rows
    row_ids = lax.broadcasted_iota(jnp.int32, (extra, width), 0)
    vectors = jnp.where(row_ids == 0, jnp.sum(bias_ref[...], axis=0, keepdims=True), 0.0)
    vectors = jnp.where(row_ids == 1, jnp.sum(head_ref[...], axis=0, keepdims=True), vectors)
    for ref, away in ((keep_ref, 0), (send_ref, 4)):
        for j in range(4):
            piece = me ^ (away + j)
            ref[j, 0:rows, :] = total_ref[pl.ds(pl.multiple_of(piece * rows, rows), rows), :]
            ref[j, rows:, :] = jnp.where(piece == 0, vectors, 0.0)


def finish_kernel(place_ref, mine_ref, other_ref, self_ref, neigh_ref, bias_ref, head_ref):
    me = place_ref[0]
    width = self_ref.shape[1]
    rows = 2 * width // 8
    for ref, away in ((mine_ref, 0), (other_ref, 4)):
        for j in range(4):
            piece = me ^ (away + j)
            part = ref[j, 0:rows, :]
            at = pl.ds(pl.multiple_of(lax.rem(piece, 4) * rows, rows), rows)

            @pl.when(piece < 4)
            def _():
                self_ref[at, :] = part

            @pl.when(piece >= 4)
            def _():
                neigh_ref[at, :] = part

            @pl.when(piece == 0)
            def _():
                bias_ref[...] = ref[j, rows : rows + 1, :]
                head_ref[...] = ref[j, rows + 1 : rows + 2, :]


def keep_in(space, *arrays):
    return [pltpu.with_memory_space_constraint(array, space) for array in arrays]


def shape(*dims, dtype=F32):
    return jax.ShapeDtypeStruct(dims, dtype)


SMEM = pl.BlockSpec(memory_space=pltpu.SMEM)
VMEM = pl.BlockSpec(memory_space=pltpu.VMEM)
ANY = pl.BlockSpec(memory_space=pl.ANY)
HBM = pl.BlockSpec(memory_space=pltpu.HBM)


def on_device(
    peers,
    features,
    w_self,
    w_neigh,
    bias,
    w_head,
    tile_weights,
    tile_dst,
    tile_src,
    tile_count,
    hub_block,
    send_rows,
    send_count,
    labels,
):
    tiles, size, _ = tile_weights.shape
    verts, width = features.shape
    blocks = verts // size
    slots = send_rows.shape[2]
    border_blocks = peers * slots // size
    me = (lax.axis_index("vert") * lax.axis_size("row") + lax.axis_index("row")).astype(jnp.int32)

    bits = peers.bit_length() - 1
    core = 2
    line = [k << (bits - 2) for k in (1, 2, 3)]
    plane = [1 << b for b in range(bits - 2) if 1 << b != core]
    order = (plane[::-1], plane)

    def across(x, mask_of):
        return lax.ppermute(x, AXES, [(i, i ^ mask_of(i)) for i in range(peers)])

    source = tile_src.astype(jnp.int32)
    hub = jnp.clip(source - blocks - border_blocks, 0, peers - 1)
    apart = hub ^ me
    place_in_line = apart >> (bits - 2)
    sender_core = (hub >> 1) & 1
    steps = len(plane)

    def differs(s):
        return jnp.where(sender_core == 0, apart & order[0][s], apart & order[1][s]) != 0

    held_blocks, far_blocks = peers // 4, peers // 8
    index = place_in_line
    for s in range(steps - 1):
        index = index + jnp.where(differs(s), 4 << s, 0)
    through = differs(steps - 1)
    late = through & (index >= far_blocks)
    early_code = 65536 + border_blocks + index + jnp.where(through, held_blocks, 0)
    early_code = early_code + jnp.where((apart & core) != 0, held_blocks + far_blocks, 0)
    late_code = 2 * 65536 + index - far_blocks + jnp.where((apart & core) != 0, far_blocks, 0)
    code = jnp.where(late, late_code, early_code)
    code = jnp.where(source < blocks + border_blocks, 65536 + source - blocks, code)
    code = jnp.where(source < blocks, source, code)

    mine = lax.dynamic_slice_in_dim(features, hub_block[0] * size, size, 0)[None]
    held = jnp.concatenate([mine] + [across(mine, lambda i, m=m: m) for m in line], 0)

    features, tile_weights = keep_in(pltpu.HBM, features, tile_weights)
    acc, outgoing, early_list, late_list = pl.pallas_call(
        own_kernel,
        out_shape=(
            pltpu.HBM((verts, width), F32),
            shape(peers, slots, width),
            shape(tiles + 8, dtype=jnp.int32),
            shape(tiles + 8, dtype=jnp.int32),
        ),
        in_specs=[SMEM] * 5 + [HBM, HBM],
        out_specs=(HBM, VMEM, SMEM, SMEM),
        scratch_shapes=[
            pltpu.SMEM((tiles + 8,), jnp.int32),
            pltpu.VMEM((verts, width), F32),
            pltpu.VMEM((tiles, size, size), F32),
            pltpu.VMEM((verts, width), F32),
            pltpu.SemaphoreType.DMA((LOADS + 2,)),
        ],
        compiler_params=pltpu.CompilerParams(vmem_limit_bytes=VMEM_BYTES),
        cost_estimate=COST,
        name="own_tiles",
    )(tile_dst, code, tile_count, send_rows, send_count, features, tile_weights)
    held, outgoing = lax.optimization_barrier((held, outgoing))

    pre, aux, done = pl.pallas_call(
        own_dense_kernel,
        out_shape=(pltpu.HBM((verts, width), F32), pltpu.HBM((verts, size), F32), shape(8, size)),
        in_specs=[SMEM] * 2 + [HBM, HBM, VMEM, VMEM, VMEM],
        out_specs=(HBM, HBM, VMEM),
        scratch_shapes=[
            pltpu.VMEM((verts, width), F32),
            pltpu.VMEM((tiles, size, size), F32),
            pltpu.VMEM((verts, width), F32),
            pltpu.VMEM((verts, size), F32),
            pltpu.VMEM((blocks, size, size), F32),
            pltpu.SemaphoreType.DMA((2,)),
        ],
        compiler_params=pltpu.CompilerParams(vmem_limit_bytes=VMEM_BYTES),
        cost_estimate=COST,
        name="own_dense",
    )(
        tile_dst, tile_count, features, tile_weights, w_self, bias.reshape(1, width),
        labels.reshape(blocks, size),
    )

    incoming = lax.all_to_all(outgoing, AXES, split_axis=0, concat_axis=0, tiled=True)
    border = incoming.reshape(border_blocks, size, width)

    for s in range(steps - 1):
        near = held
        held = jnp.concatenate([held, across(held, lambda i, s=s: order[(i >> 1) & 1][s])], 0)
    far_near = across(near, lambda i: order[(i >> 1) & 1][steps - 1])
    held, far_near, border, done = lax.optimization_barrier((held, far_near, border, done))
    far = across(held[far_blocks:], lambda i: order[(i >> 1) & 1][steps - 1])
    held_other = across(held, lambda i: core)
    far_near_other = across(far_near, lambda i: core)

    acc, done = pl.pallas_call(
        early_kernel,
        out_shape=(pltpu.HBM((verts, width), F32), shape(8, size)),
        in_specs=[SMEM] + [ANY] * 5 + [HBM, HBM, ANY],
        out_specs=(HBM, VMEM),
        scratch_shapes=[
            pltpu.VMEM((tiles, size, size), F32),
            pltpu.VMEM((verts, width), F32),
            pltpu.VMEM((border_blocks + 2 * (held_blocks + far_blocks), size, width), F32),
            pltpu.SemaphoreType.DMA((tiles,)),
            pltpu.SemaphoreType.DMA((6,)),
        ],
        compiler_params=pltpu.CompilerParams(vmem_limit_bytes=VMEM_BYTES),
        cost_estimate=COST,
        name="early_tiles",
    )(
        early_list, border, held, far_near, held_other, far_near_other,
        *keep_in(pltpu.HBM, acc), tile_weights, done,
    )
    far, done = lax.optimization_barrier((far, done))
    far_other = across(far, lambda i: core)

    place = ((me >> 1) & 1) * 4 + ((me >> 2) & 1) * 2 + (me & 1)
    place = place.reshape(1)
    piece_rows = 2 * width // 8 + 8
    keep, send = pl.pallas_call(
        functools.partial(late_kernel, scale=1.0 / math.sqrt(verts * peers)),
        out_shape=(shape(4, piece_rows, width), shape(4, piece_rows, width)),
        in_specs=[SMEM, SMEM, ANY, ANY] + [HBM] * 5 + [VMEM, VMEM, ANY],
        out_specs=(VMEM, VMEM),
        scratch_shapes=[
            pltpu.VMEM((tiles, size, size), F32),
            pltpu.VMEM((verts, width), F32),
            pltpu.VMEM((verts, width), F32),
            pltpu.VMEM((verts, width), F32),
            pltpu.VMEM((verts, size), F32),
            pltpu.VMEM((2 * far_blocks, size, width), F32),
            pltpu.VMEM((2 * width, width), F32),
            pltpu.VMEM((8, width), F32),
            pltpu.VMEM((8, width), F32),
            pltpu.SemaphoreType.DMA((tiles,)),
            pltpu.SemaphoreType.DMA((3,)),
            pltpu.SemaphoreType.DMA((verts // CHUNK, 3)),
        ],
        compiler_params=pltpu.CompilerParams(vmem_limit_bytes=VMEM_BYTES),
        cost_estimate=COST,
        name="late_tiles_and_gradients",
    )(
        late_list, place, far, far_other,
        *keep_in(pltpu.HBM, acc, tile_weights, features, pre, aux),
        w_neigh, w_head.reshape(1, width), done,
    )

    held = keep + across(send, lambda i: core)
    reach = (0, 1, 4, 5)
    got = [held[0]] + [across(held[j], lambda i, j=j: reach[j]) for j in (1, 2, 3)]
    total = (got[0] + got[1]) + (got[2] + got[3])
    for low in range(3, bits, 2):
        masks = [1 << low] if low + 1 == bits else [k << low for k in (1, 2, 3)]
        more = [across(total, lambda i, m=m: m) for m in masks]
        total = total + more[0] if len(more) == 1 else (total + more[0]) + (more[1] + more[2])
    mine = jnp.stack([total] + [across(total, lambda i, j=j: reach[j]) for j in (1, 2, 3)])
    other = across(mine, lambda i: core)
    grad_self, grad_neigh, grad_bias, grad_head = pl.pallas_call(
        finish_kernel,
        out_shape=(shape(width, width), shape(width, width), shape(1, width), shape(1, width)),
        in_specs=[SMEM, VMEM, VMEM],
        out_specs=(VMEM, VMEM, VMEM, VMEM),
        name="assemble",
    )(place, mine, other)
    return (grad_self, grad_neigh, grad_bias.reshape(width), grad_head.reshape(width))


def solution(mesh):
    peers = math.prod(mesh.shape.values())
    in_specs = (
        P(AXES, None),
        P(),
        P(),
        P(),
        P(),
        P(AXES, None, None),
        P(AXES),
        P(AXES),
        P(AXES),
        P(AXES),
        P(AXES, None, None),
        P(AXES, None),
        P(AXES),
    )
    out_specs = (P(), P(), P(), P())
    return jax.shard_map(
        functools.partial(on_device, peers),
        mesh=mesh,
        in_specs=in_specs,
        out_specs=out_specs,
        check_vma=False,
    )
```

time: 130 us -> 102 us (0.78)
  local copies, waits for them, and re-layouts: 23.7 us -> 3.77 us
  starting transfers between devices: 46.5 us -> 32.9 us
  waiting for transfers between devices: 18.6 us -> 21.7 us
  Pallas kernels: 36.9 us -> 39.4 us
    unnamed x41 -> x21, local copies, waits for them, and re-layouts: 22.6 us -> 2.8 us
    ppermute x20, starting transfers between devices: 42.5 us -> 29.4 us  [across(): return lax.ppermute(x, AXES, [(i, i ^ mask_of(i)) for i in range(peers)])]
    pallas_call x3, Pallas kernels: 18.8 us -> 24.7 us  [the longest x1 9.83 us: on_device(): pl.pallas_call(own_kernel, out_shape=(pltpu.HBM((verts, width), F32), sha...]
    pallas_call x1, Pallas kernels: 16.1 us -> 12.8 us  [on_device(): pl.pallas_call(functools.partial(late_kernel, scale=1.0 / math.sqrt(verts...]
    ppermute x20, waiting for transfers between devices: 18.6 us -> 20.5 us  [across(): return lax.ppermute(x, AXES, [(i, i ^ mask_of(i)) for i in range(peers)])]
  transfers between devices with their start and end apart: 21 -> 21, of which waited for: 12 -> 13; matrix products, arithmetic and copies ran while one was open for 1% -> 3% of each run, Pallas kernels for 15% -> 24%
where the time goes in v2:
time: 102 us
  Pallas kernels  39.4 us (39%)
  starting transfers between devices  32.9 us (32%)
  waiting for transfers between devices  21.7 us (21%)
  local copies, waits for them, and re-layouts  3.77 us (4%)
  between operations  2.13 us (2%)
  other arithmetic  1.93 us (2%)
    ppermute x20, starting transfers between devices, across(): return lax.ppermute(x, AXES, [(i, i ^ mask_of(i)) for i in range(peers)])  29.4 us
    ppermute x20, waiting for transfers between devices, across(): return lax.ppermute(x, AXES, [(i, i ^ mask_of(i)) for i in range(peers)])  20.5 us
    pallas_call x1, Pallas kernels, on_device(): pl.pallas_call(functools.partial(late_kernel, scale=1.0 / math.sqrt(verts...  12.8 us
    pallas_call x1, Pallas kernels, on_device(): pl.pallas_call(own_kernel, out_shape=(pltpu.HBM((verts, width), F32), sha...  9.83 us
    pallas_call x1, Pallas kernels, on_device(): pl.pallas_call(own_dense_kernel, out_shape=(pltpu.HBM((verts, width), F32...  8.37 us
    pallas_call x1, Pallas kernels, on_device(): pl.pallas_call(early_kernel, out_shape=(pltpu.HBM((verts, width), F32), s...  6.47 us
    all_to_all x1, starting transfers between devices, on_device(): lax.all_to_all(outgoing, AXES, split_axis=0, concat_axis=0, tiled=True)  3.48 us
    unnamed x21, local copies, waits for them, and re-layouts  2.8 us
  transfers between devices with their start and end apart: 21, of which 13 were waited for; matrix products, arithmetic and copies ran while one was open for 3% of the time, Pallas kernels for 24%

profile of v2, /device:TPU:0, one launch (start us, length us, event | category | flops | bytes accessed | tf_op | source)
XLA Modules:
  0.0 101.8 jit_solution(2329436214588212778)
XLA Ops:
  1.3 0.9 dynamic-slice_bitcast_fusion
  2.2 3.1 %collective-permute-start = (f32[1,128,256]{2,1,0:T(8,128)S(1)}, f32[1,128,256]{2,1,0:T(8,128)S(1)}, u32[]{:S(2)}, u32[]{:S(2)}) collective-permute-start(f32[1,128,256]{2,1,0:T(8,128)S(1)} %dynamic-slice_bitcast_fusion), channel_id=1, source_target_pairs={{0,8},{1,9},{2,10},{3,11},{4,12},{5,13},{6,14},{7,15},{8,0},{9,1},... | collective-permute-start | bytes 393224 | tf_op jit(solution)/shard_map/ppermute | solution.py:355
  5.3 2.6 %collective-permute-start.1 = (f32[1,128,256]{2,1,0:T(8,128)S(1)}, f32[1,128,256]{2,1,0:T(8,128)S(1)}, u32[]{:S(2)}, u32[]{:S(2)}) collective-permute-start(f32[1,128,256]{2,1,0:T(8,128)S(1)} %dynamic-slice_bitcast_fusion), channel_id=1, source_target_pairs={{0,16},{1,17},{2,18},{3,19},{4,20},{5,21},{6,22},{7,23},{8,24},{9,... | collective-permute-start | bytes 393224 | tf_op jit(solution)/shard_map/ppermute | solution.py:355
  11.3 9.8 %own_tiles.1 = (f32[4096,256]{1,0:T(8,128)}, f32[32,8,256]{2,1,0:T(8,128)}, s32[136]{0:T(256)S(1)}, s32[136]{0:T(256)S(1)}) custom-call(s32[128]{0:T(128)S(1)} %copy-done.3, s32[128]{0:T(128)S(1)} %compare_select_fusion.code_ref, s32[1]{0:T(128)S(6)} %copy.18.count_ref, s32[1,32,8]{2,1,0:T(8,128)S(1)} %copy.17.rows_ref, s32[1,32]{1,0:T(1,128)S(1)} %copy-done.7, ...), custom_call_target="tpu_custom_call" | custom-call | flops 1000000 | bytes 100000 | tf_op jit(solution)/shard_map/own_tiles/pallas_call | solution.py:384
  21.2 2.2 %collective-permute-start.3 = (f32[4,128,256]{2,1,0:T(8,128)S(1)}, f32[4,128,256]{2,1,0:T(8,128)}, u32[]{:S(2)}, u32[]{:S(2)}) collective-permute-start(f32[4,128,256]{2,1,0:T(8,128)S(1)} %pad_maximum_fusion.1), channel_id=1, source_target_pairs={{0,4},{1,5},{2,3},{3,2},{4,0},{5,1},{6,7},{7,6},{8,12},{9,13},{10,... | collective-permute-start | bytes 1572872 | tf_op jit(solution)/shard_map/ppermute | solution.py:355
  23.5 4.8 %collective-permute-start.4 = (f32[4,128,256]{2,1,0:T(8,128)S(1)}, f32[4,128,256]{2,1,0:T(8,128)S(1)}, u32[]{:S(2)}, u32[]{:S(2)}) collective-permute-start(f32[4,128,256]{2,1,0:T(8,128)S(1)} %pad_maximum_fusion.1), channel_id=1, source_target_pairs={{0,1},{1,0},{2,6},{3,7},{4,5},{5,4},{6,2},{7,3},{8,9},{9,8},{10,14... | collective-permute-start | bytes 1572872 | tf_op jit(solution)/shard_map/ppermute | solution.py:355
  28.2 3.5 %all-to-all-start = ((f32[32,8,256]{2,1,0:T(8,128)}), f32[32,8,256]{2,1,0:T(8,128)S(1)}, u32[]{:S(2)}, u32[]{:S(2)}) async-start(f32[32,8,256]{2,1,0:T(8,128)} %get-tuple-element.30), calls=%async_computation | async-start | bytes 524288 | tf_op jit(solution)/shard_map/all_to_all | solution.py:428
  31.7 8.4 %own_dense.1 = (f32[4096,256]{1,0:T(8,128)}, f32[4096,128]{1,0:T(8,128)}, f32[8,128]{1,0:T(8,128)S(1)}) custom-call(s32[128]{0:T(128)S(1)} %copy-done.4, s32[1]{0:T(128)S(6)} %copy.18.count_ref, f32[4096,256]{1,0:T(8,128)} %features_in_ref.5, f32[128,128,128]{2,1,0:T(8,128)} %weights_in_ref.7, f32[256,256]{1,0:T(8,128)S(1)} %copy-done.1, ...), custom_call_target="tpu_custom_call" | custom-call | flops 1000000 | bytes 100000 | tf_op jit(solution)/shard_map/own_dense/pallas_call | solution.py:407
  40.1 1.1 %pad_maximum_fusion.mine_ref = f32[8,128,256]{2,1,0:T(8,128)S(1)} fusion(f32[4,128,256]{2,1,0:T(8,128)} %collective-permute-done.3, f32[4,128,256]{2,1,0:T(8,128)S(1)} %pad_maximum_fusion.1), kind=kLoop, calls=%fused_computation | loop fusion | flops 262144 | bytes 2097152 | tf_op jit(solution)/shard_map/concatenate | solution.py:433
  41.2 1.1 %all-to-all-done = f32[32,8,256]{2,1,0:T(8,128)S(1)} async-done(((f32[32,8,256]{2,1,0:T(8,128)}), f32[32,8,256]{2,1,0:T(8,128)S(1)}, u32[]{:S(2)}, u32[]{:S(2)}) %all-to-all-start) | async-done | bytes 262176 | tf_op jit(solution)/shard_map/all_to_all | solution.py:428
  42.9 0.9 collective-permute-start.5
  43.9 1.9 %collective-permute-done.7.far_other_ref = f32[4,128,256]{2,1,0:T(8,128)S(1)} collective-permute-done((f32[4,128,256]{2,1,0:T(8,128)S(1)}, f32[4,128,256]{2,1,0:T(8,128)S(1)}, u32[]{:S(2)}, u32[]{:S(2)}) %collective-permute-start.7) | collective-permute-done | bytes 524320 | tf_op jit(solution)/shard_map/ppermute | solution.py:355
  45.8 6.5 %early_tiles.1 = (f32[4096,256]{1,0:T(8,128)}, f32[8,128]{1,0:T(8,128)S(1)}) custom-call(s32[136]{0:T(256)S(1)} %get-tuple-element.33.list_ref, f32[2,128,256]{2,1,0:T(8,128)S(1)} %bitcast.26, f32[8,128,256]{2,1,0:T(8,128)S(1)} %pad_maximum_fusion.mine_ref, f32[4,128,256]{2,1,0:T(8,128)S(1)} %collective-permute-done.4.far_ref, ...), custom_call_target="tpu_custom_call" | custom-call | flops 1000000 | bytes 100000 | tf_op jit(solution)/shard_map/early_tiles/pallas_call | solution.py:440
  52.3 1.2 %collective-permute-start.8 = (f32[4,128,256]{2,1,0:T(8,128)S(1)}, f32[4,128,256]{2,1,0:T(8,128)S(1)}, u32[]{:S(2)}, u32[]{:S(2)}) collective-permute-start(f32[4,128,256]{2,1,0:T(8,128)S(1)} %collective-permute-done.5.mine_ref), channel_id=1, source_target_pairs={{0,2},{1,3},{2,0},{3,1},{4,6},{5,7},{6,4},{7,5},{8,10},{9,11},{10,... | collective-permute-start | bytes 1572872 | tf_op jit(solution)/shard_map/ppermute | solution.py:355
  53.5 1.5 %collective-permute-done.8.other_ref = f32[4,128,256]{2,1,0:T(8,128)S(1)} collective-permute-done((f32[4,128,256]{2,1,0:T(8,128)S(1)}, f32[4,128,256]{2,1,0:T(8,128)S(1)}, u32[]{:S(2)}, u32[]{:S(2)}) %collective-permute-start.8) | collective-permute-done | bytes 524320 | tf_op jit(solution)/shard_map/ppermute | solution.py:355
  55.0 12.8 %late_tiles_and_gradients.1 = (f32[4,72,256]{2,1,0:T(8,128)S(1)}, f32[4,72,256]{2,1,0:T(8,128)S(1)}) custom-call(s32[136]{0:T(256)S(1)} %get-tuple-element.27.list_ref, s32[1]{0:T(128)} %bitcast.place_ref, f32[4,128,256]{2,1,0:T(8,128)S(1)} %collective-permute-done.5.mine_ref, f32[4,128,256]{2,1,0:T(8,128)S(1)} %collective-permute-done.8.other_ref, ...), custom_call_target="tpu_custom_call" | custom-call | flops 1000000 | bytes 100000 | tf_op jit(solution)/shard_map/late_tiles_and_gradients/pallas_call | solution.py:465
  68.3 1.2 %collective-permute-done.9 = f32[4,72,256]{2,1,0:T(8,128)S(1)} collective-permute-done((f32[4,72,256]{2,1,0:T(8,128)S(1)}, f32[4,72,256]{2,1,0:T(8,128)S(1)}, u32[]{:S(2)}, u32[]{:S(2)}) %collective-permute-start.9) | collective-permute-done | bytes 294944 | tf_op jit(solution)/shard_map/ppermute | solution.py:355
  69.8 5.3 %collective-permute-start.11 = (f32[72,256]{1,0:T(8,128)S(1)}, f32[72,256]{1,0:T(8,128)S(1)}, u32[]{:S(2)}, u32[]{:S(2)}) collective-permute-start(f32[72,256]{1,0:T(8,128)S(1)} %get-tuple-element.51), channel_id=1, source_target_pairs={{0,4},{1,5},{2,6},{3,7},{4,0},{5,1},{6,2},{7,3},{8,12},{9,13},{10,... | collective-permute-start | bytes 221192 | tf_op jit(solution)/shard_map/ppermute | solution.py:355
  75.1 2.7 %collective-permute-done.11 = f32[72,256]{1,0:T(8,128)S(1)} collective-permute-done((f32[72,256]{1,0:T(8,128)S(1)}, f32[72,256]{1,0:T(8,128)S(1)}, u32[]{:S(2)}, u32[]{:S(2)}) %collective-permute-start.11) | collective-permute-done | bytes 73760 | tf_op jit(solution)/shard_map/ppermute | solution.py:355
  77.8 2.5 %collective-permute-done.12 = f32[72,256]{1,0:T(8,128)S(1)} collective-permute-done((f32[72,256]{1,0:T(8,128)S(1)}, f32[72,256]{1,0:T(8,128)S(1)}, u32[]{:S(2)}, u32[]{:S(2)}) %collective-permute-start.12) | collective-permute-done | bytes 73760 | tf_op jit(solution)/shard_map/ppermute | solution.py:355
  80.4 0.9 collective-permute-start.13
  81.3 2.4 %collective-permute-start.14 = (f32[72,256]{1,0:T(8,128)S(1)}, f32[72,256]{1,0:T(8,128)S(1)}, u32[]{:S(2)}, u32[]{:S(2)}) collective-permute-start(f32[72,256]{1,0:T(8,128)S(1)} %fusion.1), channel_id=1, source_target_pairs={{0,16},{1,17},{2,18},{3,19},{4,20},{5,21},{6,22},{7,23},{8,24},{9,... | collective-permute-start | bytes 221192 | tf_op jit(solution)/shard_map/ppermute | solution.py:355
  83.7 1.1 %collective-permute-start.15 = (f32[72,256]{1,0:T(8,128)S(1)}, f32[72,256]{1,0:T(8,128)S(1)}, u32[]{:S(2)}, u32[]{:S(2)}) collective-permute-start(f32[72,256]{1,0:T(8,128)S(1)} %fusion.1), channel_id=1, source_target_pairs={{0,24},{1,25},{2,26},{3,27},{4,28},{5,29},{6,30},{7,31},{8,16},{9,... | collective-permute-start | bytes 221192 | tf_op jit(solution)/shard_map/ppermute | solution.py:355
  85.1 3.3 %collective-permute-done.14 = f32[72,256]{1,0:T(8,128)S(1)} collective-permute-done((f32[72,256]{1,0:T(8,128)S(1)}, f32[72,256]{1,0:T(8,128)S(1)}, u32[]{:S(2)}, u32[]{:S(2)}) %collective-permute-start.14) | collective-permute-done | bytes 73760 | tf_op jit(solution)/shard_map/ppermute | solution.py:355
  88.4 1.6 %collective-permute-done.15 = f32[72,256]{1,0:T(8,128)S(1)} collective-permute-done((f32[72,256]{1,0:T(8,128)S(1)}, f32[72,256]{1,0:T(8,128)S(1)}, u32[]{:S(2)}, u32[]{:S(2)}) %collective-permute-start.15) | collective-permute-done | bytes 73760 | tf_op jit(solution)/shard_map/ppermute | solution.py:355
  90.0 1.9 %collective-permute-start.16 = (f32[72,256]{1,0:T(8,128)S(1)}, f32[72,256]{1,0:T(8,128)S(1)}, u32[]{:S(2)}, u32[]{:S(2)}) collective-permute-start(f32[72,256]{1,0:T(8,128)S(1)} %add_add_fusion), channel_id=1, source_target_pairs={{0,1},{1,0},{2,3},{3,2},{4,5},{5,4},{6,7},{7,6},{8,9},{9,8},{10,11... | collective-permute-start | bytes 221192 | tf_op jit(solution)/shard_map/ppermute | solution.py:355
  92.2 1.4 %collective-permute-start.18 = (f32[72,256]{1,0:T(8,128)S(1)}, f32[72,256]{1,0:T(8,128)S(1)}, u32[]{:S(2)}, u32[]{:S(2)}) collective-permute-start(f32[72,256]{1,0:T(8,128)S(1)} %add_add_fusion), channel_id=1, source_target_pairs={{0,5},{1,4},{2,7},{3,6},{4,1},{5,0},{6,3},{7,2},{8,13},{9,12},{10,... | collective-permute-start | bytes 221192 | tf_op jit(solution)/shard_map/ppermute | solution.py:355
  93.5 1.1 %collective-permute-done.16 = f32[72,256]{1,0:T(8,128)S(1)} collective-permute-done((f32[72,256]{1,0:T(8,128)S(1)}, f32[72,256]{1,0:T(8,128)S(1)}, u32[]{:S(2)}, u32[]{:S(2)}) %collective-permute-start.16) | collective-permute-done | bytes 73760 | tf_op jit(solution)/shard_map/ppermute | solution.py:355
  94.6 1.6 %collective-permute-done.17 = f32[72,256]{1,0:T(8,128)S(1)} collective-permute-done((f32[72,256]{1,0:T(8,128)S(1)}, f32[72,256]{1,0:T(8,128)S(1)}, u32[]{:S(2)}, u32[]{:S(2)}) %collective-permute-start.17) | collective-permute-done | bytes 73760 | tf_op jit(solution)/shard_map/ppermute | solution.py:355
  96.2 1.2 %collective-permute-done.18 = f32[72,256]{1,0:T(8,128)S(1)} collective-permute-done((f32[72,256]{1,0:T(8,128)S(1)}, f32[72,256]{1,0:T(8,128)S(1)}, u32[]{:S(2)}, u32[]{:S(2)}) %collective-permute-start.18) | collective-permute-done | bytes 73760 | tf_op jit(solution)/shard_map/ppermute | solution.py:355
  97.5 1.6 %collective-permute-done.19.other_ref = f32[4,72,256]{2,1,0:T(8,128)S(1)} collective-permute-done((f32[4,72,256]{2,1,0:T(8,128)S(1)}, f32[4,72,256]{2,1,0:T(8,128)S(1)}, u32[]{:S(2)}, u32[]{:S(2)}) %collective-permute-start.19) | collective-permute-done | bytes 294944 | tf_op jit(solution)/shard_map/ppermute | solution.py:355
  99.8 2.0 %assemble.1 = (f32[256,256]{1,0:T(8,128)}, f32[256,256]{1,0:T(8,128)}, f32[1,256]{1,0:T(1,128)}, f32[1,256]{1,0:T(1,128)}) custom-call(s32[1]{0:T(128)} %bitcast.place_ref, f32[4,72,256]{2,1,0:T(8,128)} %copy-done.8, f32[4,72,256]{2,1,0:T(8,128)} %copy-done.9), custom_call_target="tpu_custom_call" | custom-call | tf_op jit(solution)/shard_map/assemble/pallas_call | solution.py:503
  (46 shorter events, 5.6 us)
Async XLA Ops:
  2.2 18.9 %collective-permute-start = (f32[1,128,256]{2,1,0:T(8,128)S(1)}, f32[1,128,256]{2,1,0:T(8,128)S(1)}, u32[]{:S(2)}, u32[]{:S(2)}) collective-permute-start(f32[1,128,256]{2,1,0:T(8,128)S(1)} %dynamic-slice_bitcast_fusion), channel_id=1, source_target_pairs={{0,8},{1,9},{2,10},{3,11},{4,12},{5,13},{6,14},{7,15},{8,0},{9,1},... | collective-permute-start | bytes 393224 | tf_op jit(solution)/shard_map/ppermute | solution.py:355
  5.3 15.9 %collective-permute-start.1 = (f32[1,128,256]{2,1,0:T(8,128)S(1)}, f32[1,128,256]{2,1,0:T(8,128)S(1)}, u32[]{:S(2)}, u32[]{:S(2)}) collective-permute-start(f32[1,128,256]{2,1,0:T(8,128)S(1)} %dynamic-slice_bitcast_fusion), channel_id=1, source_target_pairs={{0,16},{1,17},{2,18},{3,19},{4,20},{5,21},{6,22},{7,23},{8,24},{9,... | collective-permute-start | bytes 393224 | tf_op jit(solution)/shard_map/ppermute | solution.py:355
  7.9 13.3 %collective-permute-start.2 = (f32[1,128,256]{2,1,0:T(8,128)S(1)}, f32[1,128,256]{2,1,0:T(8,128)S(1)}, u32[]{:S(2)}, u32[]{:S(2)}) collective-permute-start(f32[1,128,256]{2,1,0:T(8,128)S(1)} %dynamic-slice_bitcast_fusion), channel_id=1, source_target_pairs={{0,24},{1,25},{2,26},{3,27},{4,28},{5,29},{6,30},{7,31},{8,16},{9,... | collective-permute-start | bytes 393224 | tf_op jit(solution)/shard_map/ppermute | solution.py:355
  10.0 0.7 copy-start.3
  10.6 0.7 copy-start.7
  11.3 20.4 %copy-start.1 = (f32[256,256]{1,0:T(8,128)S(1)}, f32[256,256]{1,0:T(8,128)}, u32[]{:S(2)}) copy-start(f32[256,256]{1,0:T(8,128)} %w_self_ref.1) | copy-start | bytes 786436
  11.3 20.4 %copy-start.2 = (s32[4096]{0:T(1024)S(1)}, s32[4096]{0:T(1024)}, u32[]{:S(2)}) copy-start(s32[4096]{0:T(1024)} %param.25) | copy-start | bytes 49156
  11.3 20.4 %copy-start.4 = (s32[128]{0:T(128)S(1)}, s32[128]{0:T(128)}, u32[]{:S(2)}) copy-start(s32[128]{0:T(128)} %dst_ref.3) | copy-start | bytes 1540
  11.3 20.4 %copy-start.6 = (f32[256]{0:T(256)S(1)}, f32[256]{0:T(256)}, u32[]{:S(2)}) copy-start(f32[256]{0:T(256)} %param.16) | copy-start | bytes 3076
  21.2 18.9 %collective-permute-start.3 = (f32[4,128,256]{2,1,0:T(8,128)S(1)}, f32[4,128,256]{2,1,0:T(8,128)}, u32[]{:S(2)}, u32[]{:S(2)}) collective-permute-start(f32[4,128,256]{2,1,0:T(8,128)S(1)} %pad_maximum_fusion.1), channel_id=1, source_target_pairs={{0,4},{1,5},{2,3},{3,2},{4,0},{5,1},{6,7},{7,6},{8,12},{9,13},{10,... | collective-permute-start | bytes 1572872 | tf_op jit(solution)/shard_map/ppermute | solution.py:355
  23.5 18.9 %collective-permute-start.4 = (f32[4,128,256]{2,1,0:T(8,128)S(1)}, f32[4,128,256]{2,1,0:T(8,128)S(1)}, u32[]{:S(2)}, u32[]{:S(2)}) collective-permute-start(f32[4,128,256]{2,1,0:T(8,128)S(1)} %pad_maximum_fusion.1), channel_id=1, source_target_pairs={{0,1},{1,0},{2,6},{3,7},{4,5},{5,4},{6,2},{7,3},{8,9},{9,8},{10,14... | collective-permute-start | bytes 1572872 | tf_op jit(solution)/shard_map/ppermute | solution.py:355
  28.2 14.2 %all-to-all-start = ((f32[32,8,256]{2,1,0:T(8,128)}), f32[32,8,256]{2,1,0:T(8,128)S(1)}, u32[]{:S(2)}, u32[]{:S(2)}) async-start(f32[32,8,256]{2,1,0:T(8,128)} %get-tuple-element.30), calls=%async_computation | async-start | bytes 524288 | tf_op jit(solution)/shard_map/all_to_all | solution.py:428
  42.4 3.4 %collective-permute-start.6 = (f32[8,128,256]{2,1,0:T(8,128)S(1)}, f32[8,128,256]{2,1,0:T(8,128)S(1)}, u32[]{:S(2)}, u32[]{:S(2)}) collective-permute-start(f32[8,128,256]{2,1,0:T(8,128)S(1)} %pad_maximum_fusion.mine_ref), channel_id=1, source_target_pairs={{0,2},{1,3},{2,0},{3,1},{4,6},{5,7},{6,4},{7,5},{8,10},{9,11},{10,... | collective-permute-start | bytes 3145736 | tf_op jit(solution)/shard_map/ppermute | solution.py:355
  42.5 3.3 %collective-permute-start.7 = (f32[4,128,256]{2,1,0:T(8,128)S(1)}, f32[4,128,256]{2,1,0:T(8,128)S(1)}, u32[]{:S(2)}, u32[]{:S(2)}) collective-permute-start(f32[4,128,256]{2,1,0:T(8,128)S(1)} %collective-permute-done.4.far_ref), channel_id=1, source_target_pairs={{0,2},{1,3},{2,0},{3,1},{4,6},{5,7},{6,4},{7,5},{8,10},{9,11},{10,... | collective-permute-start | bytes 1572872 | tf_op jit(solution)/shard_map/ppermute | solution.py:355
  42.9 9.3 %collective-permute-start.5 = (f32[4,128,256]{2,1,0:T(8,128)S(1)}, f32[4,128,256]{2,1,0:T(8,128)S(1)}, u32[]{:S(2)}, u32[]{:S(2)}) collective-permute-start(f32[4,128,256]{2,1,0:T(8,128)S(1)} %slice.15), channel_id=1, source_target_pairs={{0,1},{1,0},{2,6},{3,7},{4,5},{5,4},{6,2},{7,3},{8,9},{9,8},{10,14... | collective-permute-start | bytes 1572872 | tf_op jit(solution)/shard_map/ppermute | solution.py:355
  45.8 9.2 %copy-start = (f32[256,256]{1,0:T(8,128)S(1)}, f32[256,256]{1,0:T(8,128)}, u32[]{:S(2)}) copy-start(f32[256,256]{1,0:T(8,128)} %w_neigh_ref.1) | copy-start | bytes 786436
  45.8 9.2 %copy-start.5 = (f32[256]{0:T(256)S(1)}, f32[256]{0:T(256)}, u32[]{:S(2)}) copy-start(f32[256]{0:T(256)} %param.17) | copy-start | bytes 3076
  52.3 2.7 %collective-permute-start.8 = (f32[4,128,256]{2,1,0:T(8,128)S(1)}, f32[4,128,256]{2,1,0:T(8,128)S(1)}, u32[]{:S(2)}, u32[]{:S(2)}) collective-permute-start(f32[4,128,256]{2,1,0:T(8,128)S(1)} %collective-permute-done.5.mine_ref), channel_id=1, source_target_pairs={{0,2},{1,3},{2,0},{3,1},{4,6},{5,7},{6,4},{7,5},{8,10},{9,11},{10,... | collective-permute-start | bytes 1572872 | tf_op jit(solution)/shard_map/ppermute | solution.py:355
  67.8 1.7 %collective-permute-start.9 = (f32[4,72,256]{2,1,0:T(8,128)S(1)}, f32[4,72,256]{2,1,0:T(8,128)S(1)}, u32[]{:S(2)}, u32[]{:S(2)}) collective-permute-start(f32[4,72,256]{2,1,0:T(8,128)S(1)} %get-tuple-element.45), channel_id=1, source_target_pairs={{0,2},{1,3},{2,0},{3,1},{4,6},{5,7},{6,4},{7,5},{8,10},{9,11},{10,... | collective-permute-start | bytes 884744 | tf_op jit(solution)/shard_map/ppermute | solution.py:355
  69.6 5.5 %collective-permute-start.10 = (f32[72,256]{1,0:T(8,128)S(1)}, f32[72,256]{1,0:T(8,128)S(1)}, u32[]{:S(2)}, u32[]{:S(2)}) collective-permute-start(f32[72,256]{1,0:T(8,128)S(1)} %get-tuple-element.52), channel_id=1, source_target_pairs={{0,1},{1,0},{2,3},{3,2},{4,5},{5,4},{6,7},{7,6},{8,9},{9,8},{10,11... | collective-permute-start | bytes 221192 | tf_op jit(solution)/shard_map/ppermute | solution.py:355
  69.8 8.0 %collective-permute-start.11 = (f32[72,256]{1,0:T(8,128)S(1)}, f32[72,256]{1,0:T(8,128)S(1)}, u32[]{:S(2)}, u32[]{:S(2)}) collective-permute-start(f32[72,256]{1,0:T(8,128)S(1)} %get-tuple-element.51), channel_id=1, source_target_pairs={{0,4},{1,5},{2,6},{3,7},{4,0},{5,1},{6,2},{7,3},{8,12},{9,13},{10,... | collective-permute-start | bytes 221192 | tf_op jit(solution)/shard_map/ppermute | solution.py:355
  75.1 5.3 %collective-permute-start.12 = (f32[72,256]{1,0:T(8,128)S(1)}, f32[72,256]{1,0:T(8,128)S(1)}, u32[]{:S(2)}, u32[]{:S(2)}) collective-permute-start(f32[72,256]{1,0:T(8,128)S(1)} %get-tuple-element.50), channel_id=1, source_target_pairs={{0,5},{1,4},{2,7},{3,6},{4,1},{5,0},{6,3},{7,2},{8,13},{9,12},{10,... | collective-permute-start | bytes 221192 | tf_op jit(solution)/shard_map/ppermute | solution.py:355
  80.4 4.7 %collective-permute-start.13 = (f32[72,256]{1,0:T(8,128)S(1)}, f32[72,256]{1,0:T(8,128)S(1)}, u32[]{:S(2)}, u32[]{:S(2)}) collective-permute-start(f32[72,256]{1,0:T(8,128)S(1)} %fusion.1), channel_id=1, source_target_pairs={{0,8},{1,9},{2,10},{3,11},{4,12},{5,13},{6,14},{7,15},{8,0},{9,1},... | collective-permute-start | bytes 221192 | tf_op jit(solution)/shard_map/ppermute | solution.py:355
  81.3 7.1 %collective-permute-start.14 = (f32[72,256]{1,0:T(8,128)S(1)}, f32[72,256]{1,0:T(8,128)S(1)}, u32[]{:S(2)}, u32[]{:S(2)}) collective-permute-start(f32[72,256]{1,0:T(8,128)S(1)} %fusion.1), channel_id=1, source_target_pairs={{0,16},{1,17},{2,18},{3,19},{4,20},{5,21},{6,22},{7,23},{8,24},{9,... | collective-permute-start | bytes 221192 | tf_op jit(solution)/shard_map/ppermute | solution.py:355
  83.7 6.2 %collective-permute-start.15 = (f32[72,256]{1,0:T(8,128)S(1)}, f32[72,256]{1,0:T(8,128)S(1)}, u32[]{:S(2)}, u32[]{:S(2)}) collective-permute-start(f32[72,256]{1,0:T(8,128)S(1)} %fusion.1), channel_id=1, source_target_pairs={{0,24},{1,25},{2,26},{3,27},{4,28},{5,29},{6,30},{7,31},{8,16},{9,... | collective-permute-start | bytes 221192 | tf_op jit(solution)/shard_map/ppermute | solution.py:355
  90.0 4.7 %collective-permute-start.16 = (f32[72,256]{1,0:T(8,128)S(1)}, f32[72,256]{1,0:T(8,128)S(1)}, u32[]{:S(2)}, u32[]{:S(2)}) collective-permute-start(f32[72,256]{1,0:T(8,128)S(1)} %add_add_fusion), channel_id=1, source_target_pairs={{0,1},{1,0},{2,3},{3,2},{4,5},{5,4},{6,7},{7,6},{8,9},{9,8},{10,11... | collective-permute-start | bytes 221192 | tf_op jit(solution)/shard_map/ppermute | solution.py:355
  91.9 4.4 %collective-permute-start.17 = (f32[72,256]{1,0:T(8,128)S(1)}, f32[72,256]{1,0:T(8,128)S(1)}, u32[]{:S(2)}, u32[]{:S(2)}) collective-permute-start(f32[72,256]{1,0:T(8,128)S(1)} %add_add_fusion), channel_id=1, source_target_pairs={{0,4},{1,5},{2,6},{3,7},{4,0},{5,1},{6,2},{7,3},{8,12},{9,13},{10,... | collective-permute-start | bytes 221192 | tf_op jit(solution)/shard_map/ppermute | solution.py:355
  92.2 5.3 %collective-permute-start.18 = (f32[72,256]{1,0:T(8,128)S(1)}, f32[72,256]{1,0:T(8,128)S(1)}, u32[]{:S(2)}, u32[]{:S(2)}) collective-permute-start(f32[72,256]{1,0:T(8,128)S(1)} %add_add_fusion), channel_id=1, source_target_pairs={{0,5},{1,4},{2,7},{3,6},{4,1},{5,0},{6,3},{7,2},{8,13},{9,12},{10,... | collective-permute-start | bytes 221192 | tf_op jit(solution)/shard_map/ppermute | solution.py:355
  97.4 1.7 %copy-start.8 = (f32[4,72,256]{2,1,0:T(8,128)}, f32[4,72,256]{2,1,0:T(8,128)S(1)}, u32[]{:S(2)}) copy-start(f32[4,72,256]{2,1,0:T(8,128)S(1)} %pad_maximum_fusion.2.mine_ref) | copy-start | bytes 884740
  97.4 1.6 %collective-permute-start.19 = (f32[4,72,256]{2,1,0:T(8,128)S(1)}, f32[4,72,256]{2,1,0:T(8,128)S(1)}, u32[]{:S(2)}, u32[]{:S(2)}) collective-permute-start(f32[4,72,256]{2,1,0:T(8,128)S(1)} %pad_maximum_fusion.2.mine_ref), channel_id=1, source_target_pairs={{0,2},{1,3},{2,0},{3,1},{4,6},{5,7},{6,4},{7,5},{8,10},{9,11},{10,... | collective-permute-start | bytes 884744 | tf_op jit(solution)/shard_map/ppermute | solution.py:355
  99.1 0.7 copy-start.9

commit v3 on v2

v3 whole, which is shorter than its diff:
```python
import functools
import math

import jax
import jax.numpy as jnp
from jax import lax
from jax.experimental import pallas as pl
from jax.experimental.pallas import tpu as pltpu
from jax.sharding import PartitionSpec as P

AXES = ("vert", "row")
F32 = jnp.float32
BF16 = jnp.bfloat16
GROUP = 8
CHUNK = 512
COST = pl.CostEstimate(flops=1_000_000, bytes_accessed=100_000, transcendentals=0)
UNROLL = 4
VMEM_BYTES = 44 * 1024 * 1024


def split(x):
    hi = x.astype(BF16)
    return hi, (x - hi.astype(F32)).astype(BF16)


def dot(a, b, contract=((1,), (0,))):
    return lax.dot_general(a, b, (contract, ((), ())), preferred_element_type=F32)


def dot3(a, b, contract=((1,), (0,))):
    (a_hi, a_lo), (b_hi, b_lo) = a, b
    return dot(a_hi, b_hi, contract) + dot(a_hi, b_lo, contract) + dot(a_lo, b_hi, contract)


def tile_product(weights, source):
    w_hi, w_lo = split(weights)
    s_hi, s_lo = split(source)
    wide = jnp.concatenate([w_hi, w_hi], 1)
    tall = jnp.concatenate([s_hi, s_lo], 0)
    return dot(wide, tall) + dot(w_lo, s_hi)


def add_tiles(list_ref, weights_ref, source_of, acc_ref, weight_acc_ref, ready):
    size = weights_ref.shape[1]
    total = list_ref[list_ref.shape[0] - 7]

    def step(group, carry):
        ready(group)
        at = [group * GROUP + k for k in range(GROUP)]
        entries = [list_ref[jnp.minimum(i, total - 1)] for i in at]
        products = [
            tile_product(weights_ref[i], source_of(entry >> 14))
            for i, entry in zip(at, entries)
        ]
        for i, entry, product in zip(at, entries, products):
            block = (entry >> 8) & 63
            where = pl.ds(pl.multiple_of(block * size, size), size)
            acc_ref[where, :] += jnp.where(i < total, product, 0.0)
            weight_acc_ref[block] += jnp.where(i < total, weights_ref[i], 0.0)
        return carry

    lax.fori_loop(0, (total + GROUP - 1) // GROUP, step, 0)


def row_sums(weight_acc_ref, sums_ref):
    blocks, size, _ = weight_acc_ref.shape

    def step(block, carry):
        column = jnp.sum(weight_acc_ref[block], axis=1, keepdims=True)
        sums_ref[pl.ds(block, 1), :] = jnp.sum(jnp.where(diagonal(size), column, 0.0), axis=0, keepdims=True)
        return carry

    lax.fori_loop(0, blocks, step, 0, unroll=4)


def diagonal(size):
    at = lambda axis: lax.broadcasted_iota(jnp.int32, (size, size), axis)
    return at(0) == at(1)


def as_columns(rows):
    size = rows.shape[1]
    parts = [
        jnp.sum(jnp.where(diagonal(size), rows[i : i + 1, :], 0.0), axis=1, keepdims=True)
        for i in range(rows.shape[0])
    ]
    return jnp.concatenate(parts, 0)


def fetch_tiles(list_ref, weights_in_ref, weights_ref, sems):
    total = list_ref[list_ref.shape[0] - 7]

    def start(group, carry):
        for k in range(GROUP):
            i = group * GROUP + k
            tile = list_ref[jnp.minimum(i, total - 1)] & 255
            pltpu.make_async_copy(weights_in_ref.at[tile], weights_ref.at[i], sems.at[group]).start()
        return carry

    lax.fori_loop(0, (total + GROUP - 1) // GROUP, start, 0)

    def ready(group):
        part = weights_ref.at[pl.ds(pl.multiple_of(group * GROUP, GROUP), GROUP)]
        pltpu.make_async_copy(weights_in_ref.at[pl.ds(0, GROUP)], part, sems.at[group]).wait()

    return ready


def prepare_kernel(
    plan_ref, rows_ref, count_ref, features_in_ref,
    outgoing_ref, own_ref, early_ref, late_ref,
    features_ref, load_sems,
):
    load = pltpu.make_async_copy(features_in_ref, features_ref, load_sems.at[0])
    load.start()
    tiles = plan_ref.shape[0]
    peers, slots, _ = outgoing_ref.shape
    lists = (own_ref, early_ref, late_ref)

    def sort(t, counts):
        plan = plan_ref[t]
        stage = plan >> 28
        entry = (plan & ((1 << 28) - 1)) | t
        for ref, count in zip(lists, counts):
            ref[count] = entry
        return tuple(count + (stage == i).astype(jnp.int32) for i, count in enumerate(counts))

    counts = lax.fori_loop(0, count_ref[0], sort, (jnp.int32(0),) * 3)
    for ref, count in zip(lists, counts):
        ref[tiles + 1] = count
    load.wait()

    def gather(peer, carry):
        for k in range(slots):
            at = rows_ref[peer * slots + k]
            row = features_ref[pl.ds(jnp.maximum(at, 0), 1), :]
            outgoing_ref[peer, k : k + 1, :] = jnp.where(at >= 0, row, 0.0)
        return carry

    lax.fori_loop(0, peers, gather, 0)


def own_kernel(
    list_ref, features_in_ref, weights_in_ref,
    acc_out_ref, sums_ref,
    features_ref, weights_ref, acc_ref, weight_acc_ref, sems, load_sems,
):
    size = weights_ref.shape[1]
    load = pltpu.make_async_copy(features_in_ref, features_ref, load_sems.at[0])
    load.start()
    ready = fetch_tiles(list_ref, weights_in_ref, weights_ref, sems)
    acc_ref[...] = jnp.zeros_like(acc_ref)
    weight_acc_ref[...] = jnp.zeros_like(weight_acc_ref)
    load.wait()

    def source_of(block):
        return features_ref[pl.ds(pl.multiple_of(block * size, size), size), :]

    add_tiles(list_ref, weights_ref, source_of, acc_ref, weight_acc_ref, ready)
    store = pltpu.make_async_copy(acc_ref, acc_out_ref, load_sems.at[0])
    store.start()
    row_sums(weight_acc_ref, sums_ref)
    store.wait()


def early_kernel(
    list_ref, border_ref, mine_ref, far_ref, other_ref, far_other_ref, weights_in_ref,
    acc_out_ref, sums_ref,
    weights_ref, acc_ref, weight_acc_ref, sources_ref, sems, load_sems,
):
    at, copies = 0, []
    for i, part in enumerate((border_ref, mine_ref, far_ref, other_ref, far_other_ref)):
        blocks = part.shape[0]
        copies.append(pltpu.make_async_copy(part, sources_ref.at[pl.ds(at, blocks)], load_sems.at[i]))
        at += blocks
    for copy in copies:
        copy.start()
    ready = fetch_tiles(list_ref, weights_in_ref, weights_ref, sems)
    acc_ref[...] = jnp.zeros_like(acc_ref)
    weight_acc_ref[...] = jnp.zeros_like(weight_acc_ref)
    for copy in copies:
        copy.wait()
    add_tiles(list_ref, weights_ref, lambda i: sources_ref[i], acc_ref, weight_acc_ref, ready)
    store = pltpu.make_async_copy(acc_ref, acc_out_ref, load_sems.at[0])
    store.start()
    row_sums(weight_acc_ref, sums_ref)
    store.wait()


def late_kernel(
    list_ref, place_ref, mine_ref, other_ref, own_in_ref, early_in_ref, weights_in_ref, features_in_ref,
    own_sums_ref, early_sums_ref, labels_ref, w_self_ref, w_neigh_ref, bias_in_ref, w_head_ref,
    keep_ref, send_ref,
    weights_ref, weight_acc_ref, acc_ref, own_ref, early_ref, features_ref, sources_ref, sums_ref, total_ref, bias_ref, head_ref,
    sems, load_sems, chunk_sems, *, scale,
):
    verts, width = features_ref.shape
    size = weights_ref.shape[1]
    blocks = mine_ref.shape[0]
    loads = [
        (mine_ref, sources_ref.at[pl.ds(0, blocks)]),
        (other_ref, sources_ref.at[pl.ds(blocks, blocks)]),
    ]
    copies = [pltpu.make_async_copy(a, b, load_sems.at[i]) for i, (a, b) in enumerate(loads)]
    for copy in copies:
        copy.start()
    ready = fetch_tiles(list_ref, weights_in_ref, weights_ref, sems)
    chunk_copies = []
    for i in range(verts // CHUNK):
        where = pl.ds(i * CHUNK, CHUNK)
        pairs = ((own_in_ref, own_ref), (early_in_ref, early_ref), (features_in_ref, features_ref))
        chunk_copies.append(
            [pltpu.make_async_copy(a.at[where], b.at[where], chunk_sems.at[i, j]) for j, (a, b) in enumerate(pairs)]
        )
        for copy in chunk_copies[-1]:
            copy.start()
    acc_ref[...] = jnp.zeros_like(acc_ref)
    weight_acc_ref[...] = jnp.zeros_like(weight_acc_ref)
    total_ref[...] = jnp.zeros_like(total_ref)
    bias_ref[...] = jnp.zeros_like(bias_ref)
    head_ref[...] = jnp.zeros_like(head_ref)
    w_self = split(w_self_ref[...])
    w_neigh = split(w_neigh_ref[...])
    w_head = w_head_ref[...]
    for copy in copies:
        copy.wait()
    add_tiles(list_ref, weights_ref, lambda i: sources_ref[i], acc_ref, weight_acc_ref, ready)
    row_sums(weight_acc_ref, sums_ref)
    inverse = 1.0 / (1.0 + (own_sums_ref[...] + early_sums_ref[...] + sums_ref[...]))
    target = 2.0 * labels_ref[...].astype(F32) - 1.0
    step = CHUNK // size

    def forward(i):
        where = pl.ds(i * CHUNK, CHUNK)
        own = features_ref[where, :]
        mean = (own + (acc_ref[where, :] + own_ref[where, :] + early_ref[where, :])) * as_columns(inverse[i * step : (i + 1) * step, :])
        own, mean = split(own), split(mean)
        pre = dot3(own, w_self) + dot3(mean, w_neigh) + bias_in_ref[...]
        sig = jax.nn.sigmoid(pre)
        hidden = pre * sig
        score = jnp.sum(hidden * w_head, axis=1, keepdims=True)
        dscore = (score - as_columns(target[i * step : (i + 1) * step, :])) * scale
        dpre = dscore * w_head * (sig * (1.0 + pre * (1.0 - sig)))
        bias_ref[...] += jnp.sum(dpre.reshape(CHUNK // 8, 8, width), axis=0)
        head_ref[...] += jnp.sum((hidden * dscore).reshape(CHUNK // 8, 8, width), axis=0)
        return own, mean, split(dpre)

    def backward(own, mean, dpre):
        total_ref[0:width, :] += dot3(own, dpre, ((0,), (0,)))
        total_ref[width : 2 * width, :] += dot3(mean, dpre, ((0,), (0,)))

    for first in range(0, verts // CHUNK, UNROLL):
        for i in range(first, first + UNROLL):
            for copy in chunk_copies[i]:
                copy.wait()
        for parts in [forward(i) for i in range(first, first + UNROLL)]:
            backward(*parts)

    me = place_ref[0]
    rows = 2 * width // 8
    extra = keep_ref.shape[1] - rows
    row_ids = lax.broadcasted_iota(jnp.int32, (extra, width), 0)
    vectors = jnp.where(row_ids == 0, jnp.sum(bias_ref[...], axis=0, keepdims=True), 0.0)
    vectors = jnp.where(row_ids == 1, jnp.sum(head_ref[...], axis=0, keepdims=True), vectors)
    for ref, away in ((keep_ref, 0), (send_ref, 4)):
        for j in range(4):
            piece = me ^ (away + j)
            ref[j, 0:rows, :] = total_ref[pl.ds(pl.multiple_of(piece * rows, rows), rows), :]
            ref[j, rows:, :] = jnp.where(piece == 0, vectors, 0.0)


def finish_kernel(place_ref, mine_ref, other_ref, self_ref, neigh_ref, bias_ref, head_ref):
    me = place_ref[0]
    width = self_ref.shape[1]
    rows = 2 * width // 8
    for ref, away in ((mine_ref, 0), (other_ref, 4)):
        for j in range(4):
            piece = me ^ (away + j)
            part = ref[j, 0:rows, :]
            at = pl.ds(pl.multiple_of(lax.rem(piece, 4) * rows, rows), rows)

            @pl.when(piece < 4)
            def _():
                self_ref[at, :] = part

            @pl.when(piece >= 4)
            def _():
                neigh_ref[at, :] = part

            @pl.when(piece == 0)
            def _():
                bias_ref[...] = ref[j, rows : rows + 1, :]
                head_ref[...] = ref[j, rows + 1 : rows + 2, :]


def keep_in(space, *arrays):
    return [pltpu.with_memory_space_constraint(array, space) for array in arrays]


def shape(*dims, dtype=F32):
    return jax.ShapeDtypeStruct(dims, dtype)


SMEM = pl.BlockSpec(memory_space=pltpu.SMEM)
VMEM = pl.BlockSpec(memory_space=pltpu.VMEM)
ANY = pl.BlockSpec(memory_space=pl.ANY)
HBM = pl.BlockSpec(memory_space=pltpu.HBM)


def on_device(
    peers,
    features,
    w_self,
    w_neigh,
    bias,
    w_head,
    tile_weights,
    tile_dst,
    tile_src,
    tile_count,
    hub_block,
    send_rows,
    send_count,
    labels,
):
    tiles, size, _ = tile_weights.shape
    verts, width = features.shape
    blocks = verts // size
    slots = send_rows.shape[2]
    border_blocks = peers * slots // size
    me = (lax.axis_index("vert") * lax.axis_size("row") + lax.axis_index("row")).astype(jnp.int32)

    bits = peers.bit_length() - 1
    core = 2
    line = [k << (bits - 2) for k in (1, 2, 3)]
    plane = [1 << b for b in range(bits - 2) if 1 << b != core]
    order = (plane[::-1], plane)

    def across(x, mask_of):
        return lax.ppermute(x, AXES, [(i, i ^ mask_of(i)) for i in range(peers)])

    source = tile_src.astype(jnp.int32)
    hub = jnp.clip(source - blocks - border_blocks, 0, peers - 1)
    apart = hub ^ me
    place_in_line = apart >> (bits - 2)
    sender_core = (hub >> 1) & 1
    steps = len(plane)

    def differs(s):
        return jnp.where(sender_core == 0, apart & order[0][s], apart & order[1][s]) != 0

    held_blocks, far_blocks = peers // 4, peers // 8
    index = place_in_line
    for s in range(steps - 1):
        index = index + jnp.where(differs(s), 4 << s, 0)
    through = differs(steps - 1)
    late = through & (index >= far_blocks)
    early_slot = border_blocks + index + jnp.where(through, held_blocks, 0)
    early_slot = early_slot + jnp.where((apart & core) != 0, held_blocks + far_blocks, 0)
    late_slot = index - far_blocks + jnp.where((apart & core) != 0, far_blocks, 0)
    stage = jnp.where(late, 2, 1)
    slot = jnp.where(late, late_slot, early_slot)
    at_border = source < blocks + border_blocks
    stage = jnp.where(source < blocks, 0, jnp.where(at_border, 1, stage))
    slot = jnp.where(source < blocks, source, jnp.where(at_border, source - blocks, slot))
    plan = (stage << 28) | (slot << 14) | (tile_dst << 8)
    alive = jnp.arange(slots, dtype=jnp.int32)[None, :] < send_count[0][:, None]
    listed = jnp.where(alive, send_rows[0], -1).reshape(-1)

    mine = lax.dynamic_slice_in_dim(features, hub_block[0] * size, size, 0)[None]
    held = jnp.concatenate([mine] + [across(mine, lambda i, m=m: m) for m in line], 0)

    features, tile_weights = keep_in(pltpu.HBM, features, tile_weights)
    index_list = shape(tiles + 8, dtype=jnp.int32)
    outgoing, own_list, early_list, late_list = pl.pallas_call(
        prepare_kernel,
        out_shape=(shape(peers, slots, width),) + (index_list,) * 3,
        in_specs=[SMEM] * 3 + [HBM],
        out_specs=(VMEM, SMEM, SMEM, SMEM),
        scratch_shapes=[pltpu.VMEM((verts, width), F32), pltpu.SemaphoreType.DMA((1,))],
        compiler_params=pltpu.CompilerParams(vmem_limit_bytes=VMEM_BYTES),
        cost_estimate=COST,
        name="prepare",
    )(*keep_in(pltpu.HBM, plan, listed), tile_count, features)
    held, outgoing, own_list = lax.optimization_barrier((held, outgoing, own_list))

    own_acc, own_sums = pl.pallas_call(
        own_kernel,
        out_shape=(pltpu.HBM((verts, width), F32), shape(blocks, size)),
        in_specs=[SMEM, HBM, HBM],
        out_specs=(HBM, VMEM),
        scratch_shapes=[
            pltpu.VMEM((verts, width), F32),
            pltpu.VMEM((tiles, size, size), F32),
            pltpu.VMEM((verts, width), F32),
            pltpu.VMEM((blocks, size, size), F32),
            pltpu.SemaphoreType.DMA((tiles // GROUP,)),
            pltpu.SemaphoreType.DMA((1,)),
        ],
        compiler_params=pltpu.CompilerParams(vmem_limit_bytes=VMEM_BYTES),
        cost_estimate=COST,
        name="own_tiles",
    )(own_list, features, tile_weights)

    incoming = lax.all_to_all(outgoing, AXES, split_axis=0, concat_axis=0, tiled=True)
    border = incoming.reshape(border_blocks, size, width)

    for s in range(steps - 1):
        near = held
        held = jnp.concatenate([held, across(held, lambda i, s=s: order[(i >> 1) & 1][s])], 0)
    far_near = across(near, lambda i: order[(i >> 1) & 1][steps - 1])
    held, far_near, border, own_sums = lax.optimization_barrier((held, far_near, border, own_sums))
    far = across(held[far_blocks:], lambda i: order[(i >> 1) & 1][steps - 1])
    held_other = across(held, lambda i: core)
    far_near_other = across(far_near, lambda i: core)

    early_acc, early_sums = pl.pallas_call(
        early_kernel,
        out_shape=(pltpu.HBM((verts, width), F32), shape(blocks, size)),
        in_specs=[SMEM] + [ANY] * 5 + [HBM],
        out_specs=(HBM, VMEM),
        scratch_shapes=[
            pltpu.VMEM((tiles, size, size), F32),
            pltpu.VMEM((verts, width), F32),
            pltpu.VMEM((blocks, size, size), F32),
            pltpu.VMEM((border_blocks + 2 * (held_blocks + far_blocks), size, width), F32),
            pltpu.SemaphoreType.DMA((tiles // GROUP,)),
            pltpu.SemaphoreType.DMA((5,)),
        ],
        compiler_params=pltpu.CompilerParams(vmem_limit_bytes=VMEM_BYTES),
        cost_estimate=COST,
        name="early_tiles",
    )(early_list, border, held, far_near, held_other, far_near_other, tile_weights)
    far, early_sums = lax.optimization_barrier((far, early_sums))
    far_other = across(far, lambda i: core)

    place = ((me >> 1) & 1) * 4 + ((me >> 2) & 1) * 2 + (me & 1)
    place = place.reshape(1)
    piece_rows = 2 * width // 8 + 8
    keep, send = pl.pallas_call(
        functools.partial(late_kernel, scale=1.0 / math.sqrt(verts * peers)),
        out_shape=(shape(4, piece_rows, width), shape(4, piece_rows, width)),
        in_specs=[SMEM, SMEM, ANY, ANY] + [HBM] * 4 + [VMEM] * 7,
        out_specs=(VMEM, VMEM),
        scratch_shapes=[
            pltpu.VMEM((tiles, size, size), F32),
            pltpu.VMEM((blocks, size, size), F32),
            pltpu.VMEM((verts, width), F32),
            pltpu.VMEM((verts, width), F32),
            pltpu.VMEM((verts, width), F32),
            pltpu.VMEM((verts, width), F32),
            pltpu.VMEM((2 * far_blocks, size, width), F32),
            pltpu.VMEM((blocks, size), F32),
            pltpu.VMEM((2 * width, width), F32),
            pltpu.VMEM((8, width), F32),
            pltpu.VMEM((8, width), F32),
            pltpu.SemaphoreType.DMA((tiles // GROUP,)),
            pltpu.SemaphoreType.DMA((2,)),
            pltpu.SemaphoreType.DMA((verts // CHUNK, 3)),
        ],
        compiler_params=pltpu.CompilerParams(vmem_limit_bytes=VMEM_BYTES),
        cost_estimate=COST,
        name="late_tiles_and_gradients",
    )(
        late_list, place, far, far_other,
        *keep_in(pltpu.HBM, own_acc, early_acc), tile_weights, features,
        own_sums, early_sums, labels.reshape(blocks, size),
        w_self, w_neigh, bias.reshape(1, width), w_head.reshape(1, width),
    )

    held = keep + across(send, lambda i: core)
    reach = (0, 1, 4, 5)
    got = [held[0]] + [across(held[j], lambda i, j=j: reach[j]) for j in (1, 2, 3)]
    total = (got[0] + got[1]) + (got[2] + got[3])
    for low in range(3, bits, 2):
        masks = [1 << low] if low + 1 == bits else [k << low for k in (1, 2, 3)]
        more = [across(total, lambda i, m=m: m) for m in masks]
        total = total + more[0] if len(more) == 1 else (total + more[0]) + (more[1] + more[2])
    mine = jnp.stack([total] + [across(total, lambda i, j=j: reach[j]) for j in (1, 2, 3)])
    other = across(mine, lambda i: core)
    grad_self, grad_neigh, grad_bias, grad_head = pl.pallas_call(
        finish_kernel,
        out_shape=(shape(width, width), shape(width, width), shape(1, width), shape(1, width)),
        in_specs=[SMEM, VMEM, VMEM],
        out_specs=(VMEM, VMEM, VMEM, VMEM),
        name="assemble",
    )(place, *keep_in(pltpu.VMEM, mine, other))
    return (grad_self, grad_neigh, grad_bias.reshape(width), grad_head.reshape(width))


def solution(mesh):
    peers = math.prod(mesh.shape.values())
    in_specs = (
        P(AXES, None),
        P(),
        P(),
        P(),
        P(),
        P(AXES, None, None),
        P(AXES),
        P(AXES),
        P(AXES),
        P(AXES),
        P(AXES, None, None),
        P(AXES, None),
        P(AXES),
    )
    out_specs = (P(), P(), P(), P())
    return jax.shard_map(
        functools.partial(on_device, peers),
        mesh=mesh,
        in_specs=in_specs,
        out_specs=out_specs,
        check_vma=False,
    )
```

time: 102 us -> 91.7 us (0.90)
  Pallas kernels: 39.4 us -> 29.1 us
  waiting for transfers between devices: 21.7 us -> 28.1 us
  starting transfers between devices: 32.9 us -> 27.1 us
  local copies, waits for them, and re-layouts: 3.77 us -> 1.94 us
    ppermute x20, starting transfers between devices: 29.4 us -> 23.7 us  [across(): return lax.ppermute(x, AXES, [(i, i ^ mask_of(i)) for i in range(peers)])]
    ppermute x20, waiting for transfers between devices: 20.5 us -> 26 us  [across(): return lax.ppermute(x, AXES, [(i, i ^ mask_of(i)) for i in range(peers)])]
    pallas_call x1, Pallas kernels: 9.83 us -> 5.42 us  [on_device(): pl.pallas_call(own_kernel, out_shape=(pltpu.HBM((verts, width), F32), sha...]
    pallas_call x1, Pallas kernels: 8.37 us -> 4.59 us  [on_device(): pl.pallas_call(prepare_kernel, out_shape=(shape(peers, slots, width),) +...]
    unnamed x21 -> x11, local copies, waits for them, and re-layouts: 2.8 us -> 0.79 us
    pallas_call x1, Pallas kernels: 6.47 us -> 4.59 us  [on_device(): pl.pallas_call(early_kernel, out_shape=(pltpu.HBM((verts, width), F32), s...]
    or x0 -> x1, other arithmetic: none -> 1.2 us  [on_device(): plan = stage << 28 | slot << 14 | tile_dst << 8]
    concatenate x1, other arithmetic: 1.11 us -> 0.07 us  [on_device(): jnp.concatenate([held, across(held, lambda i, s=s: order[i >> 1 & 1][s])]...]
  transfers between devices with their start and end apart: 21 -> 21, of which waited for: 13 -> 16; matrix products, arithmetic and copies ran while one was open for 3% -> 4% of each run, Pallas kernels for 24% -> 16%
where the time goes in v3:
time: 91.7 us; the launch traced here: 91 us
  Pallas kernels  29.1 us (32%)
  waiting for transfers between devices  28.1 us (31%)
  starting transfers between devices  27.1 us (30%)
  other arithmetic  2.72 us (3%)
  between operations  2.11 us (2%)
  local copies, waits for them, and re-layouts  1.94 us (2%)
    ppermute x20, waiting for transfers between devices, across(): return lax.ppermute(x, AXES, [(i, i ^ mask_of(i)) for i in range(peers)])  26 us
    ppermute x20, starting transfers between devices, across(): return lax.ppermute(x, AXES, [(i, i ^ mask_of(i)) for i in range(peers)])  23.7 us
    pallas_call x1, Pallas kernels, on_device(): pl.pallas_call(functools.partial(late_kernel, scale=1.0 / math.sqrt(verts...  13.5 us
    pallas_call x1, Pallas kernels, on_device(): pl.pallas_call(own_kernel, out_shape=(pltpu.HBM((verts, width), F32), sha...  5.42 us
    pallas_call x1, Pallas kernels, on_device(): pl.pallas_call(early_kernel, out_shape=(pltpu.HBM((verts, width), F32), s...  4.59 us
    pallas_call x1, Pallas kernels, on_device(): pl.pallas_call(prepare_kernel, out_shape=(shape(peers, slots, width),) +...  4.59 us
    all_to_all x1, starting transfers between devices, on_device(): lax.all_to_all(outgoing, AXES, split_axis=0, concat_axis=0, tiled=True)  3.34 us
    all_to_all x1, waiting for transfers between devices, on_device(): lax.all_to_all(outgoing, AXES, split_axis=0, concat_axis=0, tiled=True)  2.11 us
  transfers between devices with their start and end apart: 21, of which 16 were waited for; matrix products, arithmetic and copies ran while one was open for 4% of the time, Pallas kernels for 16%

profile of v3, /device:TPU:0, one launch (start us, length us, event | category | flops | bytes accessed | tf_op | source)
XLA Modules:
  0.0 91.0 jit_solution(12395484586041954282)
XLA Ops:
  2.2 3.1 %collective-permute-start = (f32[1,128,256]{2,1,0:T(8,128)S(1)}, f32[1,128,256]{2,1,0:T(8,128)S(1)}, u32[]{:S(2)}, u32[]{:S(2)}) collective-permute-start(f32[1,128,256]{2,1,0:T(8,128)S(1)} %dynamic-slice_bitcast_fusion), channel_id=1, source_target_pairs={{0,8},{1,9},{2,10},{3,11},{4,12},{5,13},{6,14},{7,15},{8,0},{9,1},... | collective-permute-start | bytes 393224 | tf_op jit(solution)/shard_map/ppermute | solution.py:340
  5.3 2.6 %collective-permute-start.1 = (f32[1,128,256]{2,1,0:T(8,128)S(1)}, f32[1,128,256]{2,1,0:T(8,128)S(1)}, u32[]{:S(2)}, u32[]{:S(2)}) collective-permute-start(f32[1,128,256]{2,1,0:T(8,128)S(1)} %dynamic-slice_bitcast_fusion), channel_id=1, source_target_pairs={{0,16},{1,17},{2,18},{3,19},{4,20},{5,21},{6,22},{7,23},{8,24},{9,... | collective-permute-start | bytes 393224 | tf_op jit(solution)/shard_map/ppermute | solution.py:340
  10.8 1.2 %shift-left_or_fusion.plan_ref = s32[128]{0:T(128)} fusion(s32[128]{0:T(128)} %param.19, s32[128]{0:T(128)} %param.20, s32[]{:T(128)S(6)} %add.53), kind=kLoop, calls=%fused_computation.28 | loop fusion | flops 5248 | bytes 1540 | tf_op jit(solution)/shard_map/or | solution.py:366
  12.0 4.6 %prepare.1 = (f32[32,8,256]{2,1,0:T(8,128)}, s32[136]{0:T(256)S(1)}, s32[136]{0:T(256)S(1)}, s32[136]{0:T(256)S(1)}) custom-call(s32[128]{0:T(128)} %shift-left_or_fusion.plan_ref, s32[256]{0:T(256)} %broadcast_select_fusion.rows_ref, s32[1]{0:T(128)S(6)} %copy.18.count_ref, f32[4096,256]{1,0:T(8,128)} %features_in_ref.5), custom_call_target="tpu_custom_call" | custom-call | flops 1000000 | bytes 100000 | tf_op jit(solution)/shard_map/prepare/pallas_call | solution.py:375
  16.6 1.6 %collective-permute-done.1 = f32[1,128,256]{2,1,0:T(8,128)S(1)} collective-permute-done((f32[1,128,256]{2,1,0:T(8,128)S(1)}, f32[1,128,256]{2,1,0:T(8,128)S(1)}, u32[]{:S(2)}, u32[]{:S(2)}) %collective-permute-start.1) | collective-permute-done | bytes 131104 | tf_op jit(solution)/shard_map/ppermute | solution.py:340
  18.3 1.6 %collective-permute-start.3 = (f32[4,128,256]{2,1,0:T(8,128)S(1)}, f32[4,128,256]{2,1,0:T(8,128)S(1)}, u32[]{:S(2)}, u32[]{:S(2)}) collective-permute-start(f32[4,128,256]{2,1,0:T(8,128)S(1)} %pad_maximum_fusion.1), channel_id=1, source_target_pairs={{0,4},{1,5},{2,3},{3,2},{4,0},{5,1},{6,7},{7,6},{8,12},{9,13},{10,... | collective-permute-start | bytes 1572872 | tf_op jit(solution)/shard_map/ppermute | solution.py:340
  19.8 1.5 %collective-permute-start.4 = (f32[4,128,256]{2,1,0:T(8,128)S(1)}, f32[4,128,256]{2,1,0:T(8,128)S(1)}, u32[]{:S(2)}, u32[]{:S(2)}) collective-permute-start(f32[4,128,256]{2,1,0:T(8,128)S(1)} %pad_maximum_fusion.1), channel_id=1, source_target_pairs={{0,1},{1,0},{2,6},{3,7},{4,5},{5,4},{6,2},{7,3},{8,9},{9,8},{10,14... | collective-permute-start | bytes 1572872 | tf_op jit(solution)/shard_map/ppermute | solution.py:340
  21.3 3.3 %all-to-all-start = ((f32[32,8,256]{2,1,0:T(8,128)}), f32[32,8,256]{2,1,0:T(8,128)S(1)}, u32[]{:S(2)}, u32[]{:S(2)}) async-start(f32[32,8,256]{2,1,0:T(8,128)} %get-tuple-element.31), calls=%async_computation | async-start | bytes 524288 | tf_op jit(solution)/shard_map/all_to_all | solution.py:405
  24.7 5.4 %own_tiles.1 = (f32[4096,256]{1,0:T(8,128)}, f32[32,128]{1,0:T(8,128)S(1)}) custom-call(s32[136]{0:T(256)S(1)} %get-tuple-element.32.list_ref, f32[4096,256]{1,0:T(8,128)} %features_in_ref.5, f32[128,128,128]{2,1,0:T(8,128)} %weights_in_ref.5), custom_call_target="tpu_custom_call" | custom-call | flops 1000000 | bytes 100000 | tf_op jit(solution)/shard_map/own_tiles/pallas_call | solution.py:387
  30.1 3.1 %collective-permute-done.3 = f32[4,128,256]{2,1,0:T(8,128)S(1)} collective-permute-done((f32[4,128,256]{2,1,0:T(8,128)S(1)}, f32[4,128,256]{2,1,0:T(8,128)S(1)}, u32[]{:S(2)}, u32[]{:S(2)}) %collective-permute-start.3) | collective-permute-done | bytes 524320 | tf_op jit(solution)/shard_map/ppermute | solution.py:340
  33.3 2.1 %all-to-all-done = f32[32,8,256]{2,1,0:T(8,128)S(1)} async-done(((f32[32,8,256]{2,1,0:T(8,128)}), f32[32,8,256]{2,1,0:T(8,128)S(1)}, u32[]{:S(2)}, u32[]{:S(2)}) %all-to-all-start) | async-done | bytes 262176 | tf_op jit(solution)/shard_map/all_to_all | solution.py:405
  36.8 2.0 %collective-permute-done.7.far_other_ref = f32[4,128,256]{2,1,0:T(8,128)S(1)} collective-permute-done((f32[4,128,256]{2,1,0:T(8,128)S(1)}, f32[4,128,256]{2,1,0:T(8,128)S(1)}, u32[]{:S(2)}, u32[]{:S(2)}) %collective-permute-start.7) | collective-permute-done | bytes 524320 | tf_op jit(solution)/shard_map/ppermute | solution.py:340
  38.8 4.6 %early_tiles.1 = (f32[4096,256]{1,0:T(8,128)}, f32[32,128]{1,0:T(8,128)S(1)}) custom-call(s32[136]{0:T(256)S(1)} %get-tuple-element.35.list_ref, f32[2,128,256]{2,1,0:T(8,128)S(1)} %bitcast.27, f32[8,128,256]{2,1,0:T(8,128)S(1)} %pad_maximum_fusion.mine_ref, f32[4,128,256]{2,1,0:T(8,128)S(1)} %collective-permute-done.4.far_ref, ...), custom_call_target="tpu_custom_call" | custom-call | flops 1000000 | bytes 100000 | tf_op jit(solution)/shard_map/early_tiles/pallas_call | solution.py:417
  43.4 1.8 %collective-permute-done.5.mine_ref = f32[4,128,256]{2,1,0:T(8,128)S(1)} collective-permute-done((f32[4,128,256]{2,1,0:T(8,128)S(1)}, f32[4,128,256]{2,1,0:T(8,128)S(1)}, u32[]{:S(2)}, u32[]{:S(2)}) %collective-permute-start.5) | collective-permute-done | bytes 524320 | tf_op jit(solution)/shard_map/ppermute | solution.py:340
  45.2 1.9 %collective-permute-done.8.other_ref = f32[4,128,256]{2,1,0:T(8,128)S(1)} collective-permute-done((f32[4,128,256]{2,1,0:T(8,128)S(1)}, f32[4,128,256]{2,1,0:T(8,128)S(1)}, u32[]{:S(2)}, u32[]{:S(2)}) %collective-permute-start.8) | collective-permute-done | bytes 524320 | tf_op jit(solution)/shard_map/ppermute | solution.py:340
  47.1 13.5 %late_tiles_and_gradients.1 = (f32[4,72,256]{2,1,0:T(8,128)S(1)}, f32[4,72,256]{2,1,0:T(8,128)S(1)}) custom-call(s32[136]{0:T(256)S(1)} %get-tuple-element.27.list_ref, s32[1]{0:T(128)} %bitcast.place_ref, f32[4,128,256]{2,1,0:T(8,128)S(1)} %collective-permute-done.5.mine_ref, f32[4,128,256]{2,1,0:T(8,128)S(1)} %collective-permute-done.8.other_ref, ...), custom_call_target="tpu_custom_call" | custom-call | flops 1000000 | bytes 100000 | tf_op jit(solution)/shard_map/late_tiles_and_gradients/pallas_call | solution.py:440
  60.7 1.6 %collective-permute-done.9 = f32[4,72,256]{2,1,0:T(8,128)S(1)} collective-permute-done((f32[4,72,256]{2,1,0:T(8,128)S(1)}, f32[4,72,256]{2,1,0:T(8,128)S(1)}, u32[]{:S(2)}, u32[]{:S(2)}) %collective-permute-start.9) | collective-permute-done | bytes 294944 | tf_op jit(solution)/shard_map/ppermute | solution.py:340
  62.4 2.7 %collective-permute-start.10 = (f32[72,256]{1,0:T(8,128)S(1)}, f32[72,256]{1,0:T(8,128)S(1)}, u32[]{:S(2)}, u32[]{:S(2)}) collective-permute-start(f32[72,256]{1,0:T(8,128)S(1)} %get-tuple-element.52), channel_id=1, source_target_pairs={{0,1},{1,0},{2,3},{3,2},{4,5},{5,4},{6,7},{7,6},{8,9},{9,8},{10,11... | collective-permute-start | bytes 221192 | tf_op jit(solution)/shard_map/ppermute | solution.py:340
  65.1 1.5 %collective-permute-start.12 = (f32[72,256]{1,0:T(8,128)S(1)}, f32[72,256]{1,0:T(8,128)S(1)}, u32[]{:S(2)}, u32[]{:S(2)}) collective-permute-start(f32[72,256]{1,0:T(8,128)S(1)} %get-tuple-element.50), channel_id=1, source_target_pairs={{0,5},{1,4},{2,7},{3,6},{4,1},{5,0},{6,3},{7,2},{8,13},{9,12},{10,... | collective-permute-start | bytes 221192 | tf_op jit(solution)/shard_map/ppermute | solution.py:340
  66.6 1.3 %collective-permute-done.10 = f32[72,256]{1,0:T(8,128)S(1)} collective-permute-done((f32[72,256]{1,0:T(8,128)S(1)}, f32[72,256]{1,0:T(8,128)S(1)}, u32[]{:S(2)}, u32[]{:S(2)}) %collective-permute-start.10) | collective-permute-done | bytes 73760 | tf_op jit(solution)/shard_map/ppermute | solution.py:340
  67.9 2.2 %collective-permute-done.11 = f32[72,256]{1,0:T(8,128)S(1)} collective-permute-done((f32[72,256]{1,0:T(8,128)S(1)}, f32[72,256]{1,0:T(8,128)S(1)}, u32[]{:S(2)}, u32[]{:S(2)}) %collective-permute-start.11) | collective-permute-done | bytes 73760 | tf_op jit(solution)/shard_map/ppermute | solution.py:340
  70.7 1.9 %collective-permute-start.13 = (f32[72,256]{1,0:T(8,128)S(1)}, f32[72,256]{1,0:T(8,128)S(1)}, u32[]{:S(2)}, u32[]{:S(2)}) collective-permute-start(f32[72,256]{1,0:T(8,128)S(1)} %fusion.1), channel_id=1, source_target_pairs={{0,8},{1,9},{2,10},{3,11},{4,12},{5,13},{6,14},{7,15},{8,0},{9,1},... | collective-permute-start | bytes 221192 | tf_op jit(solution)/shard_map/ppermute | solution.py:340
  72.6 2.4 %collective-permute-start.14 = (f32[72,256]{1,0:T(8,128)S(1)}, f32[72,256]{1,0:T(8,128)S(1)}, u32[]{:S(2)}, u32[]{:S(2)}) collective-permute-start(f32[72,256]{1,0:T(8,128)S(1)} %fusion.1), channel_id=1, source_target_pairs={{0,16},{1,17},{2,18},{3,19},{4,20},{5,21},{6,22},{7,23},{8,24},{9,... | collective-permute-start | bytes 221192 | tf_op jit(solution)/shard_map/ppermute | solution.py:340
  75.0 1.4 %collective-permute-start.15 = (f32[72,256]{1,0:T(8,128)S(1)}, f32[72,256]{1,0:T(8,128)S(1)}, u32[]{:S(2)}, u32[]{:S(2)}) collective-permute-start(f32[72,256]{1,0:T(8,128)S(1)} %fusion.1), channel_id=1, source_target_pairs={{0,24},{1,25},{2,26},{3,27},{4,28},{5,29},{6,30},{7,31},{8,16},{9,... | collective-permute-start | bytes 221192 | tf_op jit(solution)/shard_map/ppermute | solution.py:340
  76.4 3.7 %collective-permute-done.14 = f32[72,256]{1,0:T(8,128)S(1)} collective-permute-done((f32[72,256]{1,0:T(8,128)S(1)}, f32[72,256]{1,0:T(8,128)S(1)}, u32[]{:S(2)}, u32[]{:S(2)}) %collective-permute-start.14) | collective-permute-done | bytes 73760 | tf_op jit(solution)/shard_map/ppermute | solution.py:340
  80.1 1.1 %collective-permute-done.15 = f32[72,256]{1,0:T(8,128)S(1)} collective-permute-done((f32[72,256]{1,0:T(8,128)S(1)}, f32[72,256]{1,0:T(8,128)S(1)}, u32[]{:S(2)}, u32[]{:S(2)}) %collective-permute-start.15) | collective-permute-done | bytes 73760 | tf_op jit(solution)/shard_map/ppermute | solution.py:340
  81.3 1.2 %collective-permute-start.16 = (f32[72,256]{1,0:T(8,128)S(1)}, f32[72,256]{1,0:T(8,128)S(1)}, u32[]{:S(2)}, u32[]{:S(2)}) collective-permute-start(f32[72,256]{1,0:T(8,128)S(1)} %add_add_fusion), channel_id=1, source_target_pairs={{0,1},{1,0},{2,3},{3,2},{4,5},{5,4},{6,7},{7,6},{8,9},{9,8},{10,11... | collective-permute-start | bytes 221192 | tf_op jit(solution)/shard_map/ppermute | solution.py:340
  83.1 1.7 %collective-permute-start.18 = (f32[72,256]{1,0:T(8,128)S(1)}, f32[72,256]{1,0:T(8,128)S(1)}, u32[]{:S(2)}, u32[]{:S(2)}) collective-permute-start(f32[72,256]{1,0:T(8,128)S(1)} %add_add_fusion), channel_id=1, source_target_pairs={{0,5},{1,4},{2,7},{3,6},{4,1},{5,0},{6,3},{7,2},{8,13},{9,12},{10,... | collective-permute-start | bytes 221192 | tf_op jit(solution)/shard_map/ppermute | solution.py:340
  85.7 1.1 %collective-permute-done.17 = f32[72,256]{1,0:T(8,128)S(1)} collective-permute-done((f32[72,256]{1,0:T(8,128)S(1)}, f32[72,256]{1,0:T(8,128)S(1)}, u32[]{:S(2)}, u32[]{:S(2)}) %collective-permute-start.17) | collective-permute-done | bytes 73760 | tf_op jit(solution)/shard_map/ppermute | solution.py:340
  86.8 1.5 %collective-permute-done.18 = f32[72,256]{1,0:T(8,128)S(1)} collective-permute-done((f32[72,256]{1,0:T(8,128)S(1)}, f32[72,256]{1,0:T(8,128)S(1)}, u32[]{:S(2)}, u32[]{:S(2)}) %collective-permute-start.18) | collective-permute-done | bytes 73760 | tf_op jit(solution)/shard_map/ppermute | solution.py:340
  88.5 1.6 %collective-permute-done.19.other_ref = f32[4,72,256]{2,1,0:T(8,128)S(1)} collective-permute-done((f32[4,72,256]{2,1,0:T(8,128)S(1)}, f32[4,72,256]{2,1,0:T(8,128)S(1)}, u32[]{:S(2)}, u32[]{:S(2)}) %collective-permute-start.19) | collective-permute-done | bytes 294944 | tf_op jit(solution)/shard_map/ppermute | solution.py:340
  90.0 0.9 %assemble.1 = (f32[256,256]{1,0:T(8,128)}, f32[256,256]{1,0:T(8,128)}, f32[1,256]{1,0:T(1,128)}, f32[1,256]{1,0:T(1,128)}) custom-call(s32[1]{0:T(128)} %bitcast.place_ref, f32[4,72,256]{2,1,0:T(8,128)S(1)} %pad_maximum_fusion.2.mine_ref, f32[4,72,256]{2,1,0:T(8,128)S(1)} %collective-permute-done.19.other_ref), custom_call_target="tpu_custom_call" | custom-call | tf_op jit(solution)/shard_map/assemble/pallas_call | solution.py:481
  (40 shorter events, 7.1 us)
Async XLA Ops:
  2.2 14.4 %collective-permute-start = (f32[1,128,256]{2,1,0:T(8,128)S(1)}, f32[1,128,256]{2,1,0:T(8,128)S(1)}, u32[]{:S(2)}, u32[]{:S(2)}) collective-permute-start(f32[1,128,256]{2,1,0:T(8,128)S(1)} %dynamic-slice_bitcast_fusion), channel_id=1, source_target_pairs={{0,8},{1,9},{2,10},{3,11},{4,12},{5,13},{6,14},{7,15},{8,0},{9,1},... | collective-permute-start | bytes 393224 | tf_op jit(solution)/shard_map/ppermute | solution.py:340
  5.3 12.9 %collective-permute-start.1 = (f32[1,128,256]{2,1,0:T(8,128)S(1)}, f32[1,128,256]{2,1,0:T(8,128)S(1)}, u32[]{:S(2)}, u32[]{:S(2)}) collective-permute-start(f32[1,128,256]{2,1,0:T(8,128)S(1)} %dynamic-slice_bitcast_fusion), channel_id=1, source_target_pairs={{0,16},{1,17},{2,18},{3,19},{4,20},{5,21},{6,22},{7,23},{8,24},{9,... | collective-permute-start | bytes 393224 | tf_op jit(solution)/shard_map/ppermute | solution.py:340
  7.9 10.3 %collective-permute-start.2 = (f32[1,128,256]{2,1,0:T(8,128)S(1)}, f32[1,128,256]{2,1,0:T(8,128)S(1)}, u32[]{:S(2)}, u32[]{:S(2)}) collective-permute-start(f32[1,128,256]{2,1,0:T(8,128)S(1)} %dynamic-slice_bitcast_fusion), channel_id=1, source_target_pairs={{0,24},{1,25},{2,26},{3,27},{4,28},{5,29},{6,30},{7,31},{8,16},{9,... | collective-permute-start | bytes 393224 | tf_op jit(solution)/shard_map/ppermute | solution.py:340
  18.3 14.9 %collective-permute-start.3 = (f32[4,128,256]{2,1,0:T(8,128)S(1)}, f32[4,128,256]{2,1,0:T(8,128)S(1)}, u32[]{:S(2)}, u32[]{:S(2)}) collective-permute-start(f32[4,128,256]{2,1,0:T(8,128)S(1)} %pad_maximum_fusion.1), channel_id=1, source_target_pairs={{0,4},{1,5},{2,3},{3,2},{4,0},{5,1},{6,7},{7,6},{8,12},{9,13},{10,... | collective-permute-start | bytes 1572872 | tf_op jit(solution)/shard_map/ppermute | solution.py:340
  19.8 15.6 %collective-permute-start.4 = (f32[4,128,256]{2,1,0:T(8,128)S(1)}, f32[4,128,256]{2,1,0:T(8,128)S(1)}, u32[]{:S(2)}, u32[]{:S(2)}) collective-permute-start(f32[4,128,256]{2,1,0:T(8,128)S(1)} %pad_maximum_fusion.1), channel_id=1, source_target_pairs={{0,1},{1,0},{2,6},{3,7},{4,5},{5,4},{6,2},{7,3},{8,9},{9,8},{10,14... | collective-permute-start | bytes 1572872 | tf_op jit(solution)/shard_map/ppermute | solution.py:340
  21.3 14.0 %all-to-all-start = ((f32[32,8,256]{2,1,0:T(8,128)}), f32[32,8,256]{2,1,0:T(8,128)S(1)}, u32[]{:S(2)}, u32[]{:S(2)}) async-start(f32[32,8,256]{2,1,0:T(8,128)} %get-tuple-element.31), calls=%async_computation | async-start | bytes 524288 | tf_op jit(solution)/shard_map/all_to_all | solution.py:405
  35.4 3.4 %collective-permute-start.6 = (f32[8,128,256]{2,1,0:T(8,128)S(1)}, f32[8,128,256]{2,1,0:T(8,128)S(1)}, u32[]{:S(2)}, u32[]{:S(2)}) collective-permute-start(f32[8,128,256]{2,1,0:T(8,128)S(1)} %pad_maximum_fusion.mine_ref), channel_id=1, source_target_pairs={{0,2},{1,3},{2,0},{3,1},{4,6},{5,7},{6,4},{7,5},{8,10},{9,11},{10,... | collective-permute-start | bytes 3145736 | tf_op jit(solution)/shard_map/ppermute | solution.py:340
  35.5 3.3 %collective-permute-start.7 = (f32[4,128,256]{2,1,0:T(8,128)S(1)}, f32[4,128,256]{2,1,0:T(8,128)S(1)}, u32[]{:S(2)}, u32[]{:S(2)}) collective-permute-start(f32[4,128,256]{2,1,0:T(8,128)S(1)} %collective-permute-done.4.far_ref), channel_id=1, source_target_pairs={{0,2},{1,3},{2,0},{3,1},{4,6},{5,7},{6,4},{7,5},{8,10},{9,11},{10,... | collective-permute-start | bytes 1572872 | tf_op jit(solution)/shard_map/ppermute | solution.py:340
  35.9 9.2 %collective-permute-start.5 = (f32[4,128,256]{2,1,0:T(8,128)S(1)}, f32[4,128,256]{2,1,0:T(8,128)S(1)}, u32[]{:S(2)}, u32[]{:S(2)}) collective-permute-start(f32[4,128,256]{2,1,0:T(8,128)S(1)} %slice.15), channel_id=1, source_target_pairs={{0,1},{1,0},{2,6},{3,7},{4,5},{5,4},{6,2},{7,3},{8,9},{9,8},{10,14... | collective-permute-start | bytes 1572872 | tf_op jit(solution)/shard_map/ppermute | solution.py:340
  38.8 8.3 %copy-start = (f32[256,256]{1,0:T(8,128)S(1)}, f32[256,256]{1,0:T(8,128)}, u32[]{:S(2)}) copy-start(f32[256,256]{1,0:T(8,128)} %w_self_ref.1) | copy-start | bytes 786436
  38.8 8.3 %copy-start.1 = (f32[256,256]{1,0:T(8,128)S(1)}, f32[256,256]{1,0:T(8,128)}, u32[]{:S(2)}) copy-start(f32[256,256]{1,0:T(8,128)} %w_neigh_ref.1) | copy-start | bytes 786436
  38.8 8.3 %copy-start.2 = (s32[4096]{0:T(1024)S(1)}, s32[4096]{0:T(1024)}, u32[]{:S(2)}) copy-start(s32[4096]{0:T(1024)} %param.25) | copy-start | bytes 49156
  38.8 8.3 %copy-start.3 = (f32[256]{0:T(256)S(1)}, f32[256]{0:T(256)}, u32[]{:S(2)}) copy-start(f32[256]{0:T(256)} %param.16) | copy-start | bytes 3076
  38.8 8.3 %copy-start.4 = (f32[256]{0:T(256)S(1)}, f32[256]{0:T(256)}, u32[]{:S(2)}) copy-start(f32[256]{0:T(256)} %param.17) | copy-start | bytes 3076
  45.2 1.9 %collective-permute-start.8 = (f32[4,128,256]{2,1,0:T(8,128)S(1)}, f32[4,128,256]{2,1,0:T(8,128)S(1)}, u32[]{:S(2)}, u32[]{:S(2)}) collective-permute-start(f32[4,128,256]{2,1,0:T(8,128)S(1)} %collective-permute-done.5.mine_ref), channel_id=1, source_target_pairs={{0,2},{1,3},{2,0},{3,1},{4,6},{5,7},{6,4},{7,5},{8,10},{9,11},{10,... | collective-permute-start | bytes 1572872 | tf_op jit(solution)/shard_map/ppermute | solution.py:340
  60.7 1.6 %collective-permute-start.9 = (f32[4,72,256]{2,1,0:T(8,128)S(1)}, f32[4,72,256]{2,1,0:T(8,128)S(1)}, u32[]{:S(2)}, u32[]{:S(2)}) collective-permute-start(f32[4,72,256]{2,1,0:T(8,128)S(1)} %get-tuple-element.45), channel_id=1, source_target_pairs={{0,2},{1,3},{2,0},{3,1},{4,6},{5,7},{6,4},{7,5},{8,10},{9,11},{10,... | collective-permute-start | bytes 884744 | tf_op jit(solution)/shard_map/ppermute | solution.py:340
  62.4 5.5 %collective-permute-start.10 = (f32[72,256]{1,0:T(8,128)S(1)}, f32[72,256]{1,0:T(8,128)S(1)}, u32[]{:S(2)}, u32[]{:S(2)}) collective-permute-start(f32[72,256]{1,0:T(8,128)S(1)} %get-tuple-element.52), channel_id=1, source_target_pairs={{0,1},{1,0},{2,3},{3,2},{4,5},{5,4},{6,7},{7,6},{8,9},{9,8},{10,11... | collective-permute-start | bytes 221192 | tf_op jit(solution)/shard_map/ppermute | solution.py:340
  65.1 5.0 %collective-permute-start.11 = (f32[72,256]{1,0:T(8,128)S(1)}, f32[72,256]{1,0:T(8,128)S(1)}, u32[]{:S(2)}, u32[]{:S(2)}) collective-permute-start(f32[72,256]{1,0:T(8,128)S(1)} %get-tuple-element.51), channel_id=1, source_target_pairs={{0,4},{1,5},{2,6},{3,7},{4,0},{5,1},{6,2},{7,3},{8,12},{9,13},{10,... | collective-permute-start | bytes 221192 | tf_op jit(solution)/shard_map/ppermute | solution.py:340
  65.1 5.6 %collective-permute-start.12 = (f32[72,256]{1,0:T(8,128)S(1)}, f32[72,256]{1,0:T(8,128)S(1)}, u32[]{:S(2)}, u32[]{:S(2)}) collective-permute-start(f32[72,256]{1,0:T(8,128)S(1)} %get-tuple-element.50), channel_id=1, source_target_pairs={{0,5},{1,4},{2,7},{3,6},{4,1},{5,0},{6,3},{7,2},{8,13},{9,12},{10,... | collective-permute-start | bytes 221192 | tf_op jit(solution)/shard_map/ppermute | solution.py:340
  70.7 5.7 %collective-permute-start.13 = (f32[72,256]{1,0:T(8,128)S(1)}, f32[72,256]{1,0:T(8,128)S(1)}, u32[]{:S(2)}, u32[]{:S(2)}) collective-permute-start(f32[72,256]{1,0:T(8,128)S(1)} %fusion.1), channel_id=1, source_target_pairs={{0,8},{1,9},{2,10},{3,11},{4,12},{5,13},{6,14},{7,15},{8,0},{9,1},... | collective-permute-start | bytes 221192 | tf_op jit(solution)/shard_map/ppermute | solution.py:340
  72.6 7.6 %collective-permute-start.14 = (f32[72,256]{1,0:T(8,128)S(1)}, f32[72,256]{1,0:T(8,128)S(1)}, u32[]{:S(2)}, u32[]{:S(2)}) collective-permute-start(f32[72,256]{1,0:T(8,128)S(1)} %fusion.1), channel_id=1, source_target_pairs={{0,16},{1,17},{2,18},{3,19},{4,20},{5,21},{6,22},{7,23},{8,24},{9,... | collective-permute-start | bytes 221192 | tf_op jit(solution)/shard_map/ppermute | solution.py:340
  75.0 6.3 %collective-permute-start.15 = (f32[72,256]{1,0:T(8,128)S(1)}, f32[72,256]{1,0:T(8,128)S(1)}, u32[]{:S(2)}, u32[]{:S(2)}) collective-permute-start(f32[72,256]{1,0:T(8,128)S(1)} %fusion.1), channel_id=1, source_target_pairs={{0,24},{1,25},{2,26},{3,27},{4,28},{5,29},{6,30},{7,31},{8,16},{9,... | collective-permute-start | bytes 221192 | tf_op jit(solution)/shard_map/ppermute | solution.py:340
  81.3 4.4 %collective-permute-start.16 = (f32[72,256]{1,0:T(8,128)S(1)}, f32[72,256]{1,0:T(8,128)S(1)}, u32[]{:S(2)}, u32[]{:S(2)}) collective-permute-start(f32[72,256]{1,0:T(8,128)S(1)} %add_add_fusion), channel_id=1, source_target_pairs={{0,1},{1,0},{2,3},{3,2},{4,5},{5,4},{6,7},{7,6},{8,9},{9,8},{10,11... | collective-permute-start | bytes 221192 | tf_op jit(solution)/shard_map/ppermute | solution.py:340
  82.5 4.4 %collective-permute-start.17 = (f32[72,256]{1,0:T(8,128)S(1)}, f32[72,256]{1,0:T(8,128)S(1)}, u32[]{:S(2)}, u32[]{:S(2)}) collective-permute-start(f32[72,256]{1,0:T(8,128)S(1)} %add_add_fusion), channel_id=1, source_target_pairs={{0,4},{1,5},{2,6},{3,7},{4,0},{5,1},{6,2},{7,3},{8,12},{9,13},{10,... | collective-permute-start | bytes 221192 | tf_op jit(solution)/shard_map/ppermute | solution.py:340
  83.1 5.3 %collective-permute-start.18 = (f32[72,256]{1,0:T(8,128)S(1)}, f32[72,256]{1,0:T(8,128)S(1)}, u32[]{:S(2)}, u32[]{:S(2)}) collective-permute-start(f32[72,256]{1,0:T(8,128)S(1)} %add_add_fusion), channel_id=1, source_target_pairs={{0,5},{1,4},{2,7},{3,6},{4,1},{5,0},{6,3},{7,2},{8,13},{9,12},{10,... | collective-permute-start | bytes 221192 | tf_op jit(solution)/shard_map/ppermute | solution.py:340
  88.4 1.6 %collective-permute-start.19 = (f32[4,72,256]{2,1,0:T(8,128)S(1)}, f32[4,72,256]{2,1,0:T(8,128)S(1)}, u32[]{:S(2)}, u32[]{:S(2)}) collective-permute-start(f32[4,72,256]{2,1,0:T(8,128)S(1)} %pad_maximum_fusion.2.mine_ref), channel_id=1, source_target_pairs={{0,2},{1,3},{2,0},{3,1},{4,6},{5,7},{6,4},{7,5},{8,10},{9,11},{10,... | collective-permute-start | bytes 884744 | tf_op jit(solution)/shard_map/ppermute | solution.py:340

commit v4 on v3

--- a/solution.py
+++ b/solution.py
@@ -40,14 +40,21 @@
     return dot(wide, tall) + dot(w_lo, s_hi)
 
 
-def add_tiles(list_ref, weights_ref, source_of, acc_ref, weight_acc_ref, ready):
+def listed_at(list_ref, i):
+    tiles = list_ref.shape[0] - 8
+    total, lower = list_ref[tiles + 1], list_ref[tiles + 2]
+    i = jnp.minimum(i, total - 1)
+    return list_ref[i + jnp.where(i >= lower, tiles - total, 0)]
+
+
+def add_tiles(list_ref, weights_ref, source_of, acc_ref, weight_acc_ref, ready, lower_done=None):
     size = weights_ref.shape[1]
     total = list_ref[list_ref.shape[0] - 7]
 
     def step(group, carry):
         ready(group)
         at = [group * GROUP + k for k in range(GROUP)]
-        entries = [list_ref[jnp.minimum(i, total - 1)] for i in at]
+        entries = [listed_at(list_ref, i) for i in at]
         products = [
             tile_product(weights_ref[i], source_of(entry >> 14))
             for i, entry in zip(at, entries)
@@ -59,7 +66,20 @@
             weight_acc_ref[block] += jnp.where(i < total, weights_ref[i], 0.0)
         return carry
 
-    lax.fori_loop(0, (total + GROUP - 1) // GROUP, step, 0)
+    groups = (total + GROUP - 1) // GROUP
+    if lower_done is None:
+        lax.fori_loop(0, groups, step, 0)
+    else:
+        lower = (list_ref[list_ref.shape[0] - 6] + GROUP - 1) // GROUP
+        lax.fori_loop(0, lower, step, 0)
+        lower_done()
+        lax.fori_loop(lower, groups, step, 0)
+
+
+def halves_out(acc_ref, out_ref, sems):
+    half = acc_ref.shape[0] // 2
+    parts = [pl.ds(i * half, half) for i in range(2)]
+    return [pltpu.make_async_copy(acc_ref.at[part], out_ref.at[part], sems.at[i]) for i, part in enumerate(parts)]
 
 
 def row_sums(weight_acc_ref, sums_ref):
@@ -93,7 +113,7 @@
     def start(group, carry):
         for k in range(GROUP):
             i = group * GROUP + k
-            tile = list_ref[jnp.minimum(i, total - 1)] & 255
+            tile = listed_at(list_ref, i) & 255
             pltpu.make_async_copy(weights_in_ref.at[tile], weights_ref.at[i], sems.at[group]).start()
         return carry
 
@@ -109,7 +129,7 @@
 def prepare_kernel(
     plan_ref, rows_ref, count_ref, features_in_ref,
     outgoing_ref, own_ref, early_ref, late_ref,
-    features_ref, load_sems,
+    features_ref, load_sems, *, size,
 ):
     load = pltpu.make_async_copy(features_in_ref, features_ref, load_sems.at[0])
     load.start()
@@ -117,17 +137,24 @@
     peers, slots, _ = outgoing_ref.shape
     lists = (own_ref, early_ref, late_ref)
 
+    lower_blocks = features_ref.shape[0] // (2 * size)
+
     def sort(t, counts):
         plan = plan_ref[t]
         stage = plan >> 28
         entry = (plan & ((1 << 28) - 1)) | t
-        for ref, count in zip(lists, counts):
-            ref[count] = entry
-        return tuple(count + (stage == i).astype(jnp.int32) for i, count in enumerate(counts))
-
-    counts = lax.fori_loop(0, count_ref[0], sort, (jnp.int32(0),) * 3)
-    for ref, count in zip(lists, counts):
-        ref[tiles + 1] = count
+        upper = (((plan >> 8) & 63) >= lower_blocks).astype(jnp.int32)
+        after = []
+        for i, (ref, (low, high)) in enumerate(zip(lists, counts)):
+            ref[jnp.where(upper == 1, tiles - 1 - high, low)] = entry
+            mine = (stage == i).astype(jnp.int32)
+            after.append((low + (mine & (1 - upper)), high + (mine & upper)))
+        return tuple(after)
+
+    counts = lax.fori_loop(0, count_ref[0], sort, ((jnp.int32(0), jnp.int32(0)),) * 3)
+    for ref, (low, high) in zip(lists, counts):
+        ref[tiles + 1] = low + high
+        ref[tiles + 2] = low
     load.wait()
 
     def gather(peer, carry):
@@ -156,11 +183,12 @@
     def source_of(block):
         return features_ref[pl.ds(pl.multiple_of(block * size, size), size), :]
 
-    add_tiles(list_ref, weights_ref, source_of, acc_ref, weight_acc_ref, ready)
-    store = pltpu.make_async_copy(acc_ref, acc_out_ref, load_sems.at[0])
-    store.start()
+    stores = halves_out(acc_ref, acc_out_ref, load_sems)
+    add_tiles(list_ref, weights_ref, source_of, acc_ref, weight_acc_ref, ready, stores[0].start)
+    stores[1].start()
     row_sums(weight_acc_ref, sums_ref)
-    store.wait()
+    for store in stores:
+        store.wait()
 
 
 def early_kernel(
@@ -180,11 +208,12 @@
     weight_acc_ref[...] = jnp.zeros_like(weight_acc_ref)
     for copy in copies:
         copy.wait()
-    add_tiles(list_ref, weights_ref, lambda i: sources_ref[i], acc_ref, weight_acc_ref, ready)
-    store = pltpu.make_async_copy(acc_ref, acc_out_ref, load_sems.at[0])
-    store.start()
+    stores = halves_out(acc_ref, acc_out_ref, load_sems)
+    add_tiles(list_ref, weights_ref, lambda i: sources_ref[i], acc_ref, weight_acc_ref, ready, stores[0].start)
+    stores[1].start()
     row_sums(weight_acc_ref, sums_ref)
-    store.wait()
+    for store in stores:
+        store.wait()
 
 
 def late_kernel(
@@ -373,7 +402,7 @@
     features, tile_weights = keep_in(pltpu.HBM, features, tile_weights)
     index_list = shape(tiles + 8, dtype=jnp.int32)
     outgoing, own_list, early_list, late_list = pl.pallas_call(
-        prepare_kernel,
+        functools.partial(prepare_kernel, size=size),
         out_shape=(shape(peers, slots, width),) + (index_list,) * 3,
         in_specs=[SMEM] * 3 + [HBM],
         out_specs=(VMEM, SMEM, SMEM, SMEM),
@@ -395,7 +424,7 @@
             pltpu.VMEM((verts, width), F32),
             pltpu.VMEM((blocks, size, size), F32),
             pltpu.SemaphoreType.DMA((tiles // GROUP,)),
-            pltpu.SemaphoreType.DMA((1,)),
+            pltpu.SemaphoreType.DMA((2,)),
         ],
         compiler_params=pltpu.CompilerParams(vmem_limit_bytes=VMEM_BYTES),
         cost_estimate=COST,

time: 91.7 us -> 90.8 us (level)
  transfers between devices with their start and end apart: 21 -> 21, of which waited for: 16 -> 15; matrix products, arithmetic and copies ran while one was open for 4% -> 4% of each run, Pallas kernels for 16% -> 17%
where the time goes in v4:
time: 90.8 us
  Pallas kernels  29.6 us (33%)
  waiting for transfers between devices  27.5 us (30%)
  starting transfers between devices  26.9 us (30%)
  other arithmetic  2.72 us (3%)
  between operations  2.11 us (2%)
  local copies, waits for them, and re-layouts  1.94 us (2%)
    ppermute x20, waiting for transfers between devices, across(): return lax.ppermute(x, AXES, [(i, i ^ mask_of(i)) for i in range(peers)])  25.4 us
    ppermute x20, starting transfers between devices, across(): return lax.ppermute(x, AXES, [(i, i ^ mask_of(i)) for i in range(peers)])  23.6 us
    pallas_call x1, Pallas kernels, on_device(): pl.pallas_call(functools.partial(late_kernel, scale=1.0 / math.sqrt(verts...  13.6 us
    pallas_call x1, Pallas kernels, on_device(): pl.pallas_call(own_kernel, out_shape=(pltpu.HBM((verts, width), F32), sha...  5.97 us
    pallas_call x1, Pallas kernels, on_device(): pl.pallas_call(early_kernel, out_shape=(pltpu.HBM((verts, width), F32), s...  4.6 us
    pallas_call x1, Pallas kernels, on_device(): pl.pallas_call(functools.partial(prepare_kernel, size=size), out_shape=(s...  4.59 us
    all_to_all x1, starting transfers between devices, on_device(): lax.all_to_all(outgoing, AXES, split_axis=0, concat_axis=0, tiled=True)  3.34 us
    all_to_all x1, waiting for transfers between devices, on_device(): lax.all_to_all(outgoing, AXES, split_axis=0, concat_axis=0, tiled=True)  2.11 us
  transfers between devices with their start and end apart: 21, of which 15 were waited for; matrix products, arithmetic and copies ran while one was open for 4% of the time, Pallas kernels for 17%

profile of v4, /device:TPU:0, one launch (start us, length us, event | category | flops | bytes accessed | tf_op | source)
XLA Modules:
  0.0 90.8 jit_solution(2689002827299186952)
XLA Ops:
  2.2 3.1 %collective-permute-start = (f32[1,128,256]{2,1,0:T(8,128)S(1)}, f32[1,128,256]{2,1,0:T(8,128)S(1)}, u32[]{:S(2)}, u32[]{:S(2)}) collective-permute-start(f32[1,128,256]{2,1,0:T(8,128)S(1)} %dynamic-slice_bitcast_fusion), channel_id=1, source_target_pairs={{0,8},{1,9},{2,10},{3,11},{4,12},{5,13},{6,14},{7,15},{8,0},{9,1},... | collective-permute-start | bytes 393224 | tf_op jit(solution)/shard_map/ppermute | solution.py:369
  5.3 2.6 %collective-permute-start.1 = (f32[1,128,256]{2,1,0:T(8,128)S(1)}, f32[1,128,256]{2,1,0:T(8,128)S(1)}, u32[]{:S(2)}, u32[]{:S(2)}) collective-permute-start(f32[1,128,256]{2,1,0:T(8,128)S(1)} %dynamic-slice_bitcast_fusion), channel_id=1, source_target_pairs={{0,16},{1,17},{2,18},{3,19},{4,20},{5,21},{6,22},{7,23},{8,24},{9,... | collective-permute-start | bytes 393224 | tf_op jit(solution)/shard_map/ppermute | solution.py:369
  10.8 1.2 %shift-left_or_fusion.plan_ref = s32[128]{0:T(128)} fusion(s32[128]{0:T(128)} %param.19, s32[128]{0:T(128)} %param.20, s32[]{:T(128)S(6)} %add.53), kind=kLoop, calls=%fused_computation.28 | loop fusion | flops 5248 | bytes 1540 | tf_op jit(solution)/shard_map/or | solution.py:395
  12.0 4.6 %prepare.1 = (f32[32,8,256]{2,1,0:T(8,128)}, s32[136]{0:T(256)S(1)}, s32[136]{0:T(256)S(1)}, s32[136]{0:T(256)S(1)}) custom-call(s32[128]{0:T(128)} %shift-left_or_fusion.plan_ref, s32[256]{0:T(256)} %broadcast_select_fusion.rows_ref, s32[1]{0:T(128)S(6)} %copy.18.count_ref, f32[4096,256]{1,0:T(8,128)} %features_in_ref.5), custom_call_target="tpu_custom_call" | custom-call | flops 1000000 | bytes 100000 | tf_op jit(solution)/shard_map/prepare/pallas_call | solution.py:404
  16.6 1.6 %collective-permute-done.1 = f32[1,128,256]{2,1,0:T(8,128)S(1)} collective-permute-done((f32[1,128,256]{2,1,0:T(8,128)S(1)}, f32[1,128,256]{2,1,0:T(8,128)S(1)}, u32[]{:S(2)}, u32[]{:S(2)}) %collective-permute-start.1) | collective-permute-done | bytes 131104 | tf_op jit(solution)/shard_map/ppermute | solution.py:369
  18.3 1.6 %collective-permute-start.3 = (f32[4,128,256]{2,1,0:T(8,128)S(1)}, f32[4,128,256]{2,1,0:T(8,128)S(1)}, u32[]{:S(2)}, u32[]{:S(2)}) collective-permute-start(f32[4,128,256]{2,1,0:T(8,128)S(1)} %pad_maximum_fusion.1), channel_id=1, source_target_pairs={{0,4},{1,5},{2,3},{3,2},{4,0},{5,1},{6,7},{7,6},{8,12},{9,13},{10,... | collective-permute-start | bytes 1572872 | tf_op jit(solution)/shard_map/ppermute | solution.py:369
  19.8 1.5 %collective-permute-start.4 = (f32[4,128,256]{2,1,0:T(8,128)S(1)}, f32[4,128,256]{2,1,0:T(8,128)S(1)}, u32[]{:S(2)}, u32[]{:S(2)}) collective-permute-start(f32[4,128,256]{2,1,0:T(8,128)S(1)} %pad_maximum_fusion.1), channel_id=1, source_target_pairs={{0,1},{1,0},{2,6},{3,7},{4,5},{5,4},{6,2},{7,3},{8,9},{9,8},{10,14... | collective-permute-start | bytes 1572872 | tf_op jit(solution)/shard_map/ppermute | solution.py:369
  21.3 3.3 %all-to-all-start = ((f32[32,8,256]{2,1,0:T(8,128)}), f32[32,8,256]{2,1,0:T(8,128)S(1)}, u32[]{:S(2)}, u32[]{:S(2)}) async-start(f32[32,8,256]{2,1,0:T(8,128)} %get-tuple-element.31), calls=%async_computation | async-start | bytes 524288 | tf_op jit(solution)/shard_map/all_to_all | solution.py:434
  24.7 6.0 %own_tiles.1 = (f32[4096,256]{1,0:T(8,128)}, f32[32,128]{1,0:T(8,128)S(1)}) custom-call(s32[136]{0:T(256)S(1)} %get-tuple-element.32.list_ref, f32[4096,256]{1,0:T(8,128)} %features_in_ref.5, f32[128,128,128]{2,1,0:T(8,128)} %weights_in_ref.5), custom_call_target="tpu_custom_call" | custom-call | flops 1000000 | bytes 100000 | tf_op jit(solution)/shard_map/own_tiles/pallas_call | solution.py:416
  30.7 2.5 %collective-permute-done.3 = f32[4,128,256]{2,1,0:T(8,128)S(1)} collective-permute-done((f32[4,128,256]{2,1,0:T(8,128)S(1)}, f32[4,128,256]{2,1,0:T(8,128)S(1)}, u32[]{:S(2)}, u32[]{:S(2)}) %collective-permute-start.3) | collective-permute-done | bytes 524320 | tf_op jit(solution)/shard_map/ppermute | solution.py:369
  33.3 2.1 %all-to-all-done = f32[32,8,256]{2,1,0:T(8,128)S(1)} async-done(((f32[32,8,256]{2,1,0:T(8,128)}), f32[32,8,256]{2,1,0:T(8,128)S(1)}, u32[]{:S(2)}, u32[]{:S(2)}) %all-to-all-start) | async-done | bytes 262176 | tf_op jit(solution)/shard_map/all_to_all | solution.py:434
  36.8 2.0 %collective-permute-done.7.far_other_ref = f32[4,128,256]{2,1,0:T(8,128)S(1)} collective-permute-done((f32[4,128,256]{2,1,0:T(8,128)S(1)}, f32[4,128,256]{2,1,0:T(8,128)S(1)}, u32[]{:S(2)}, u32[]{:S(2)}) %collective-permute-start.7) | collective-permute-done | bytes 524320 | tf_op jit(solution)/shard_map/ppermute | solution.py:369
  38.8 4.6 %early_tiles.1 = (f32[4096,256]{1,0:T(8,128)}, f32[32,128]{1,0:T(8,128)S(1)}) custom-call(s32[136]{0:T(256)S(1)} %get-tuple-element.35.list_ref, f32[2,128,256]{2,1,0:T(8,128)S(1)} %bitcast.27, f32[8,128,256]{2,1,0:T(8,128)S(1)} %pad_maximum_fusion.mine_ref, f32[4,128,256]{2,1,0:T(8,128)S(1)} %collective-permute-done.4.far_ref, ...), custom_call_target="tpu_custom_call" | custom-call | flops 1000000 | bytes 100000 | tf_op jit(solution)/shard_map/early_tiles/pallas_call | solution.py:446
  43.4 1.7 %collective-permute-done.5.mine_ref = f32[4,128,256]{2,1,0:T(8,128)S(1)} collective-permute-done((f32[4,128,256]{2,1,0:T(8,128)S(1)}, f32[4,128,256]{2,1,0:T(8,128)S(1)}, u32[]{:S(2)}, u32[]{:S(2)}) %collective-permute-start.5) | collective-permute-done | bytes 524320 | tf_op jit(solution)/shard_map/ppermute | solution.py:369
  45.2 1.9 %collective-permute-done.8.other_ref = f32[4,128,256]{2,1,0:T(8,128)S(1)} collective-permute-done((f32[4,128,256]{2,1,0:T(8,128)S(1)}, f32[4,128,256]{2,1,0:T(8,128)S(1)}, u32[]{:S(2)}, u32[]{:S(2)}) %collective-permute-start.8) | collective-permute-done | bytes 524320 | tf_op jit(solution)/shard_map/ppermute | solution.py:369
  47.1 13.6 %late_tiles_and_gradients.1 = (f32[4,72,256]{2,1,0:T(8,128)S(1)}, f32[4,72,256]{2,1,0:T(8,128)S(1)}) custom-call(s32[136]{0:T(256)S(1)} %get-tuple-element.27.list_ref, s32[1]{0:T(128)} %bitcast.place_ref, f32[4,128,256]{2,1,0:T(8,128)S(1)} %collective-permute-done.5.mine_ref, f32[4,128,256]{2,1,0:T(8,128)S(1)} %collective-permute-done.8.other_ref, ...), custom_call_target="tpu_custom_call" | custom-call | flops 1000000 | bytes 100000 | tf_op jit(solution)/shard_map/late_tiles_and_gradients/pallas_call | solution.py:469
  60.8 1.6 %collective-permute-done.9 = f32[4,72,256]{2,1,0:T(8,128)S(1)} collective-permute-done((f32[4,72,256]{2,1,0:T(8,128)S(1)}, f32[4,72,256]{2,1,0:T(8,128)S(1)}, u32[]{:S(2)}, u32[]{:S(2)}) %collective-permute-start.9) | collective-permute-done | bytes 294944 | tf_op jit(solution)/shard_map/ppermute | solution.py:369
  62.7 1.2 %collective-permute-start.11 = (f32[72,256]{1,0:T(8,128)S(1)}, f32[72,256]{1,0:T(8,128)S(1)}, u32[]{:S(2)}, u32[]{:S(2)}) collective-permute-start(f32[72,256]{1,0:T(8,128)S(1)} %get-tuple-element.51), channel_id=1, source_target_pairs={{0,4},{1,5},{2,6},{3,7},{4,0},{5,1},{6,2},{7,3},{8,12},{9,13},{10,... | collective-permute-start | bytes 221192 | tf_op jit(solution)/shard_map/ppermute | solution.py:369
  63.9 2.1 %collective-permute-start.12 = (f32[72,256]{1,0:T(8,128)S(1)}, f32[72,256]{1,0:T(8,128)S(1)}, u32[]{:S(2)}, u32[]{:S(2)}) collective-permute-start(f32[72,256]{1,0:T(8,128)S(1)} %get-tuple-element.50), channel_id=1, source_target_pairs={{0,5},{1,4},{2,7},{3,6},{4,1},{5,0},{6,3},{7,2},{8,13},{9,12},{10,... | collective-permute-start | bytes 221192 | tf_op jit(solution)/shard_map/ppermute | solution.py:369
  66.8 1.0 %collective-permute-done.11 = f32[72,256]{1,0:T(8,128)S(1)} collective-permute-done((f32[72,256]{1,0:T(8,128)S(1)}, f32[72,256]{1,0:T(8,128)S(1)}, u32[]{:S(2)}, u32[]{:S(2)}) %collective-permute-start.11) | collective-permute-done | bytes 73760 | tf_op jit(solution)/shard_map/ppermute | solution.py:369
  67.8 1.7 %collective-permute-done.12 = f32[72,256]{1,0:T(8,128)S(1)} collective-permute-done((f32[72,256]{1,0:T(8,128)S(1)}, f32[72,256]{1,0:T(8,128)S(1)}, u32[]{:S(2)}, u32[]{:S(2)}) %collective-permute-start.12) | collective-permute-done | bytes 73760 | tf_op jit(solution)/shard_map/ppermute | solution.py:369
  69.6 2.8 %collective-permute-start.13 = (f32[72,256]{1,0:T(8,128)S(1)}, f32[72,256]{1,0:T(8,128)S(1)}, u32[]{:S(2)}, u32[]{:S(2)}) collective-permute-start(f32[72,256]{1,0:T(8,128)S(1)} %fusion.1), channel_id=1, source_target_pairs={{0,8},{1,9},{2,10},{3,11},{4,12},{5,13},{6,14},{7,15},{8,0},{9,1},... | collective-permute-start | bytes 221192 | tf_op jit(solution)/shard_map/ppermute | solution.py:369
  72.4 2.0 %collective-permute-start.14 = (f32[72,256]{1,0:T(8,128)S(1)}, f32[72,256]{1,0:T(8,128)S(1)}, u32[]{:S(2)}, u32[]{:S(2)}) collective-permute-start(f32[72,256]{1,0:T(8,128)S(1)} %fusion.1), channel_id=1, source_target_pairs={{0,16},{1,17},{2,18},{3,19},{4,20},{5,21},{6,22},{7,23},{8,24},{9,... | collective-permute-start | bytes 221192 | tf_op jit(solution)/shard_map/ppermute | solution.py:369
  74.4 1.4 %collective-permute-start.15 = (f32[72,256]{1,0:T(8,128)S(1)}, f32[72,256]{1,0:T(8,128)S(1)}, u32[]{:S(2)}, u32[]{:S(2)}) collective-permute-start(f32[72,256]{1,0:T(8,128)S(1)} %fusion.1), channel_id=1, source_target_pairs={{0,24},{1,25},{2,26},{3,27},{4,28},{5,29},{6,30},{7,31},{8,16},{9,... | collective-permute-start | bytes 221192 | tf_op jit(solution)/shard_map/ppermute | solution.py:369
  75.8 4.8 %collective-permute-done.14 = f32[72,256]{1,0:T(8,128)S(1)} collective-permute-done((f32[72,256]{1,0:T(8,128)S(1)}, f32[72,256]{1,0:T(8,128)S(1)}, u32[]{:S(2)}, u32[]{:S(2)}) %collective-permute-start.14) | collective-permute-done | bytes 73760 | tf_op jit(solution)/shard_map/ppermute | solution.py:369
  80.6 1.2 %collective-permute-start.16 = (f32[72,256]{1,0:T(8,128)S(1)}, f32[72,256]{1,0:T(8,128)S(1)}, u32[]{:S(2)}, u32[]{:S(2)}) collective-permute-start(f32[72,256]{1,0:T(8,128)S(1)} %add_add_fusion), channel_id=1, source_target_pairs={{0,1},{1,0},{2,3},{3,2},{4,5},{5,4},{6,7},{7,6},{8,9},{9,8},{10,11... | collective-permute-start | bytes 221192 | tf_op jit(solution)/shard_map/ppermute | solution.py:369
  81.8 1.2 %collective-permute-start.17 = (f32[72,256]{1,0:T(8,128)S(1)}, f32[72,256]{1,0:T(8,128)S(1)}, u32[]{:S(2)}, u32[]{:S(2)}) collective-permute-start(f32[72,256]{1,0:T(8,128)S(1)} %add_add_fusion), channel_id=1, source_target_pairs={{0,4},{1,5},{2,6},{3,7},{4,0},{5,1},{6,2},{7,3},{8,12},{9,13},{10,... | collective-permute-start | bytes 221192 | tf_op jit(solution)/shard_map/ppermute | solution.py:369
  83.0 1.2 %collective-permute-start.18 = (f32[72,256]{1,0:T(8,128)S(1)}, f32[72,256]{1,0:T(8,128)S(1)}, u32[]{:S(2)}, u32[]{:S(2)}) collective-permute-start(f32[72,256]{1,0:T(8,128)S(1)} %add_add_fusion), channel_id=1, source_target_pairs={{0,5},{1,4},{2,7},{3,6},{4,1},{5,0},{6,3},{7,2},{8,13},{9,12},{10,... | collective-permute-start | bytes 221192 | tf_op jit(solution)/shard_map/ppermute | solution.py:369
  85.0 1.2 %collective-permute-done.17 = f32[72,256]{1,0:T(8,128)S(1)} collective-permute-done((f32[72,256]{1,0:T(8,128)S(1)}, f32[72,256]{1,0:T(8,128)S(1)}, u32[]{:S(2)}, u32[]{:S(2)}) %collective-permute-start.17) | collective-permute-done | bytes 73760 | tf_op jit(solution)/shard_map/ppermute | solution.py:369
  86.2 2.1 %collective-permute-done.18 = f32[72,256]{1,0:T(8,128)S(1)} collective-permute-done((f32[72,256]{1,0:T(8,128)S(1)}, f32[72,256]{1,0:T(8,128)S(1)}, u32[]{:S(2)}, u32[]{:S(2)}) %collective-permute-start.18) | collective-permute-done | bytes 73760 | tf_op jit(solution)/shard_map/ppermute | solution.py:369
  88.3 1.6 %collective-permute-done.19.other_ref = f32[4,72,256]{2,1,0:T(8,128)S(1)} collective-permute-done((f32[4,72,256]{2,1,0:T(8,128)S(1)}, f32[4,72,256]{2,1,0:T(8,128)S(1)}, u32[]{:S(2)}, u32[]{:S(2)}) %collective-permute-start.19) | collective-permute-done | bytes 294944 | tf_op jit(solution)/shard_map/ppermute | solution.py:369
  89.9 0.9 %assemble.1 = (f32[256,256]{1,0:T(8,128)}, f32[256,256]{1,0:T(8,128)}, f32[1,256]{1,0:T(1,128)}, f32[1,256]{1,0:T(1,128)}) custom-call(s32[1]{0:T(128)} %bitcast.place_ref, f32[4,72,256]{2,1,0:T(8,128)S(1)} %pad_maximum_fusion.2.mine_ref, f32[4,72,256]{2,1,0:T(8,128)S(1)} %collective-permute-done.19.other_ref), custom_call_target="tpu_custom_call" | custom-call | tf_op jit(solution)/shard_map/assemble/pallas_call | solution.py:510
  (40 shorter events, 7.0 us)
Async XLA Ops:
  2.2 14.4 %collective-permute-start = (f32[1,128,256]{2,1,0:T(8,128)S(1)}, f32[1,128,256]{2,1,0:T(8,128)S(1)}, u32[]{:S(2)}, u32[]{:S(2)}) collective-permute-start(f32[1,128,256]{2,1,0:T(8,128)S(1)} %dynamic-slice_bitcast_fusion), channel_id=1, source_target_pairs={{0,8},{1,9},{2,10},{3,11},{4,12},{5,13},{6,14},{7,15},{8,0},{9,1},... | collective-permute-start | bytes 393224 | tf_op jit(solution)/shard_map/ppermute | solution.py:369
  5.3 12.9 %collective-permute-start.1 = (f32[1,128,256]{2,1,0:T(8,128)S(1)}, f32[1,128,256]{2,1,0:T(8,128)S(1)}, u32[]{:S(2)}, u32[]{:S(2)}) collective-permute-start(f32[1,128,256]{2,1,0:T(8,128)S(1)} %dynamic-slice_bitcast_fusion), channel_id=1, source_target_pairs={{0,16},{1,17},{2,18},{3,19},{4,20},{5,21},{6,22},{7,23},{8,24},{9,... | collective-permute-start | bytes 393224 | tf_op jit(solution)/shard_map/ppermute | solution.py:369
  7.9 10.3 %collective-permute-start.2 = (f32[1,128,256]{2,1,0:T(8,128)S(1)}, f32[1,128,256]{2,1,0:T(8,128)S(1)}, u32[]{:S(2)}, u32[]{:S(2)}) collective-permute-start(f32[1,128,256]{2,1,0:T(8,128)S(1)} %dynamic-slice_bitcast_fusion), channel_id=1, source_target_pairs={{0,24},{1,25},{2,26},{3,27},{4,28},{5,29},{6,30},{7,31},{8,16},{9,... | collective-permute-start | bytes 393224 | tf_op jit(solution)/shard_map/ppermute | solution.py:369
  18.3 14.9 %collective-permute-start.3 = (f32[4,128,256]{2,1,0:T(8,128)S(1)}, f32[4,128,256]{2,1,0:T(8,128)S(1)}, u32[]{:S(2)}, u32[]{:S(2)}) collective-permute-start(f32[4,128,256]{2,1,0:T(8,128)S(1)} %pad_maximum_fusion.1), channel_id=1, source_target_pairs={{0,4},{1,5},{2,3},{3,2},{4,0},{5,1},{6,7},{7,6},{8,12},{9,13},{10,... | collective-permute-start | bytes 1572872 | tf_op jit(solution)/shard_map/ppermute | solution.py:369
  19.8 15.6 %collective-permute-start.4 = (f32[4,128,256]{2,1,0:T(8,128)S(1)}, f32[4,128,256]{2,1,0:T(8,128)S(1)}, u32[]{:S(2)}, u32[]{:S(2)}) collective-permute-start(f32[4,128,256]{2,1,0:T(8,128)S(1)} %pad_maximum_fusion.1), channel_id=1, source_target_pairs={{0,1},{1,0},{2,6},{3,7},{4,5},{5,4},{6,2},{7,3},{8,9},{9,8},{10,14... | collective-permute-start | bytes 1572872 | tf_op jit(solution)/shard_map/ppermute | solution.py:369
  21.3 14.0 %all-to-all-start = ((f32[32,8,256]{2,1,0:T(8,128)}), f32[32,8,256]{2,1,0:T(8,128)S(1)}, u32[]{:S(2)}, u32[]{:S(2)}) async-start(f32[32,8,256]{2,1,0:T(8,128)} %get-tuple-element.31), calls=%async_computation | async-start | bytes 524288 | tf_op jit(solution)/shard_map/all_to_all | solution.py:434
  35.4 3.4 %collective-permute-start.6 = (f32[8,128,256]{2,1,0:T(8,128)S(1)}, f32[8,128,256]{2,1,0:T(8,128)S(1)}, u32[]{:S(2)}, u32[]{:S(2)}) collective-permute-start(f32[8,128,256]{2,1,0:T(8,128)S(1)} %pad_maximum_fusion.mine_ref), channel_id=1, source_target_pairs={{0,2},{1,3},{2,0},{3,1},{4,6},{5,7},{6,4},{7,5},{8,10},{9,11},{10,... | collective-permute-start | bytes 3145736 | tf_op jit(solution)/shard_map/ppermute | solution.py:369
  35.5 3.3 %collective-permute-start.7 = (f32[4,128,256]{2,1,0:T(8,128)S(1)}, f32[4,128,256]{2,1,0:T(8,128)S(1)}, u32[]{:S(2)}, u32[]{:S(2)}) collective-permute-start(f32[4,128,256]{2,1,0:T(8,128)S(1)} %collective-permute-done.4.far_ref), channel_id=1, source_target_pairs={{0,2},{1,3},{2,0},{3,1},{4,6},{5,7},{6,4},{7,5},{8,10},{9,11},{10,... | collective-permute-start | bytes 1572872 | tf_op jit(solution)/shard_map/ppermute | solution.py:369
  35.9 9.2 %collective-permute-start.5 = (f32[4,128,256]{2,1,0:T(8,128)S(1)}, f32[4,128,256]{2,1,0:T(8,128)S(1)}, u32[]{:S(2)}, u32[]{:S(2)}) collective-permute-start(f32[4,128,256]{2,1,0:T(8,128)S(1)} %slice.15), channel_id=1, source_target_pairs={{0,1},{1,0},{2,6},{3,7},{4,5},{5,4},{6,2},{7,3},{8,9},{9,8},{10,14... | collective-permute-start | bytes 1572872 | tf_op jit(solution)/shard_map/ppermute | solution.py:369
  38.8 8.3 %copy-start = (f32[256,256]{1,0:T(8,128)S(1)}, f32[256,256]{1,0:T(8,128)}, u32[]{:S(2)}) copy-start(f32[256,256]{1,0:T(8,128)} %w_self_ref.1) | copy-start | bytes 786436
  38.8 8.3 %copy-start.1 = (f32[256,256]{1,0:T(8,128)S(1)}, f32[256,256]{1,0:T(8,128)}, u32[]{:S(2)}) copy-start(f32[256,256]{1,0:T(8,128)} %w_neigh_ref.1) | copy-start | bytes 786436
  38.8 8.3 %copy-start.2 = (s32[4096]{0:T(1024)S(1)}, s32[4096]{0:T(1024)}, u32[]{:S(2)}) copy-start(s32[4096]{0:T(1024)} %param.25) | copy-start | bytes 49156
  38.8 8.3 %copy-start.3 = (f32[256]{0:T(256)S(1)}, f32[256]{0:T(256)}, u32[]{:S(2)}) copy-start(f32[256]{0:T(256)} %param.16) | copy-start | bytes 3076
  38.8 8.3 %copy-start.4 = (f32[256]{0:T(256)S(1)}, f32[256]{0:T(256)}, u32[]{:S(2)}) copy-start(f32[256]{0:T(256)} %param.17) | copy-start | bytes 3076
  45.2 1.9 %collective-permute-start.8 = (f32[4,128,256]{2,1,0:T(8,128)S(1)}, f32[4,128,256]{2,1,0:T(8,128)S(1)}, u32[]{:S(2)}, u32[]{:S(2)}) collective-permute-start(f32[4,128,256]{2,1,0:T(8,128)S(1)} %collective-permute-done.5.mine_ref), channel_id=1, source_target_pairs={{0,2},{1,3},{2,0},{3,1},{4,6},{5,7},{6,4},{7,5},{8,10},{9,11},{10,... | collective-permute-start | bytes 1572872 | tf_op jit(solution)/shard_map/ppermute | solution.py:369
  60.7 1.6 %collective-permute-start.9 = (f32[4,72,256]{2,1,0:T(8,128)S(1)}, f32[4,72,256]{2,1,0:T(8,128)S(1)}, u32[]{:S(2)}, u32[]{:S(2)}) collective-permute-start(f32[4,72,256]{2,1,0:T(8,128)S(1)} %get-tuple-element.45), channel_id=1, source_target_pairs={{0,2},{1,3},{2,0},{3,1},{4,6},{5,7},{6,4},{7,5},{8,10},{9,11},{10,... | collective-permute-start | bytes 884744 | tf_op jit(solution)/shard_map/ppermute | solution.py:369
  62.4 4.4 %collective-permute-start.10 = (f32[72,256]{1,0:T(8,128)S(1)}, f32[72,256]{1,0:T(8,128)S(1)}, u32[]{:S(2)}, u32[]{:S(2)}) collective-permute-start(f32[72,256]{1,0:T(8,128)S(1)} %get-tuple-element.52), channel_id=1, source_target_pairs={{0,1},{1,0},{2,3},{3,2},{4,5},{5,4},{6,7},{7,6},{8,9},{9,8},{10,11... | collective-permute-start | bytes 221192 | tf_op jit(solution)/shard_map/ppermute | solution.py:369
  62.7 5.1 %collective-permute-start.11 = (f32[72,256]{1,0:T(8,128)S(1)}, f32[72,256]{1,0:T(8,128)S(1)}, u32[]{:S(2)}, u32[]{:S(2)}) collective-permute-start(f32[72,256]{1,0:T(8,128)S(1)} %get-tuple-element.51), channel_id=1, source_target_pairs={{0,4},{1,5},{2,6},{3,7},{4,0},{5,1},{6,2},{7,3},{8,12},{9,13},{10,... | collective-permute-start | bytes 221192 | tf_op jit(solution)/shard_map/ppermute | solution.py:369
  63.9 5.6 %collective-permute-start.12 = (f32[72,256]{1,0:T(8,128)S(1)}, f32[72,256]{1,0:T(8,128)S(1)}, u32[]{:S(2)}, u32[]{:S(2)}) collective-permute-start(f32[72,256]{1,0:T(8,128)S(1)} %get-tuple-element.50), channel_id=1, source_target_pairs={{0,5},{1,4},{2,7},{3,6},{4,1},{5,0},{6,3},{7,2},{8,13},{9,12},{10,... | collective-permute-start | bytes 221192 | tf_op jit(solution)/shard_map/ppermute | solution.py:369
  69.6 6.2 %collective-permute-start.13 = (f32[72,256]{1,0:T(8,128)S(1)}, f32[72,256]{1,0:T(8,128)S(1)}, u32[]{:S(2)}, u32[]{:S(2)}) collective-permute-start(f32[72,256]{1,0:T(8,128)S(1)} %fusion.1), channel_id=1, source_target_pairs={{0,8},{1,9},{2,10},{3,11},{4,12},{5,13},{6,14},{7,15},{8,0},{9,1},... | collective-permute-start | bytes 221192 | tf_op jit(solution)/shard_map/ppermute | solution.py:369
  72.4 8.2 %collective-permute-start.14 = (f32[72,256]{1,0:T(8,128)S(1)}, f32[72,256]{1,0:T(8,128)S(1)}, u32[]{:S(2)}, u32[]{:S(2)}) collective-permute-start(f32[72,256]{1,0:T(8,128)S(1)} %fusion.1), channel_id=1, source_target_pairs={{0,16},{1,17},{2,18},{3,19},{4,20},{5,21},{6,22},{7,23},{8,24},{9,... | collective-permute-start | bytes 221192 | tf_op jit(solution)/shard_map/ppermute | solution.py:369
  74.4 6.2 %collective-permute-start.15 = (f32[72,256]{1,0:T(8,128)S(1)}, f32[72,256]{1,0:T(8,128)S(1)}, u32[]{:S(2)}, u32[]{:S(2)}) collective-permute-start(f32[72,256]{1,0:T(8,128)S(1)} %fusion.1), channel_id=1, source_target_pairs={{0,24},{1,25},{2,26},{3,27},{4,28},{5,29},{6,30},{7,31},{8,16},{9,... | collective-permute-start | bytes 221192 | tf_op jit(solution)/shard_map/ppermute | solution.py:369
  80.6 4.4 %collective-permute-start.16 = (f32[72,256]{1,0:T(8,128)S(1)}, f32[72,256]{1,0:T(8,128)S(1)}, u32[]{:S(2)}, u32[]{:S(2)}) collective-permute-start(f32[72,256]{1,0:T(8,128)S(1)} %add_add_fusion), channel_id=1, source_target_pairs={{0,1},{1,0},{2,3},{3,2},{4,5},{5,4},{6,7},{7,6},{8,9},{9,8},{10,11... | collective-permute-start | bytes 221192 | tf_op jit(solution)/shard_map/ppermute | solution.py:369
  81.8 4.4 %collective-permute-start.17 = (f32[72,256]{1,0:T(8,128)S(1)}, f32[72,256]{1,0:T(8,128)S(1)}, u32[]{:S(2)}, u32[]{:S(2)}) collective-permute-start(f32[72,256]{1,0:T(8,128)S(1)} %add_add_fusion), channel_id=1, source_target_pairs={{0,4},{1,5},{2,6},{3,7},{4,0},{5,1},{6,2},{7,3},{8,12},{9,13},{10,... | collective-permute-start | bytes 221192 | tf_op jit(solution)/shard_map/ppermute | solution.py:369
  83.0 5.3 %collective-permute-start.18 = (f32[72,256]{1,0:T(8,128)S(1)}, f32[72,256]{1,0:T(8,128)S(1)}, u32[]{:S(2)}, u32[]{:S(2)}) collective-permute-start(f32[72,256]{1,0:T(8,128)S(1)} %add_add_fusion), channel_id=1, source_target_pairs={{0,5},{1,4},{2,7},{3,6},{4,1},{5,0},{6,3},{7,2},{8,13},{9,12},{10,... | collective-permute-start | bytes 221192 | tf_op jit(solution)/shard_map/ppermute | solution.py:369
  88.3 1.6 %collective-permute-start.19 = (f32[4,72,256]{2,1,0:T(8,128)S(1)}, f32[4,72,256]{2,1,0:T(8,128)S(1)}, u32[]{:S(2)}, u32[]{:S(2)}) collective-permute-start(f32[4,72,256]{2,1,0:T(8,128)S(1)} %pad_maximum_fusion.2.mine_ref), channel_id=1, source_target_pairs={{0,2},{1,3},{2,0},{3,1},{4,6},{5,7},{6,4},{7,5},{8,10},{9,11},{10,... | collective-permute-start | bytes 884744 | tf_op jit(solution)/shard_map/ppermute | solution.py:369
